TPU v7x, 32 devices: a whole 2x2x4 slice. The times are simulated.
32 devices in a mesh: ctx: 8 (over z, x), tp: 4 (over y, core).
Axes of the slice: x: 2, y: 2, z: 4, core: 2. Of those that a mesh axis runs over, the one named last changes fastest.
Arguments:
- attn_query: bfloat16 [2048, 4096], P('ctx', 'tp'), may hold values from -8 to 8
- attn_key: bfloat16 [2048, 4096], P('ctx', 'tp'), may hold values from -8 to 8
- attn_value: bfloat16 [2048, 4096], P('ctx', 'tp'), may hold values from -6 to 6
- out_weight: bfloat16 [4096, 8192], P('tp'), may hold values from -0.125 to 0.125
Outputs:
- attn_out: bfloat16 [2048, 8192], P('ctx', 'tp')
All inputs are finite; a program needn't handle non-finite values.
Results may differ from a plain program's by a relative error of at most 0.015.
Values may be sent and summed in bfloat16 or wider, within the bound.
No kernel may reach another device: no remote copies, remote signals or barrier semaphores. Data moves between devices by JAX's collectives and lax.ppermute only.
A program may use at most 128 MiB of HBM per device.

v0:
```python
import jax
import jax.numpy as jnp
from jax import lax
from jax.sharding import PartitionSpec as P

HD = 128


def attend(queries, keys, values, query_pos, key_position):
    rows = queries.shape[0]
    local_heads = queries.shape[1] // HD
    scale = HD ** (-0.5)
    shaped_q = queries.reshape(rows, local_heads, HD)
    latest = jnp.max(query_pos)
    initial = (
        jnp.full((local_heads, rows), -1e30, jnp.float32),
        jnp.zeros((local_heads, rows), jnp.float32),
        jnp.zeros((local_heads, rows, HD), jnp.float32),
    )
    piece_keys = lax.all_gather(keys, "ctx", axis=0, tiled=True)
    piece_values = lax.all_gather(values, "ctx", axis=0, tiled=True)
    count_rows = piece_keys.shape[0]
    span_rows = 512

    def one_block(block, state):
        offset = block * span_rows
        block_keys = lax.dynamic_slice_in_dim(piece_keys, offset, span_rows, 0).reshape(
            span_rows, local_heads, HD
        )
        block_values = lax.dynamic_slice_in_dim(piece_values, offset, span_rows, 0).reshape(
            span_rows, local_heads, HD
        )
        key_pos = key_position(offset + jnp.arange(span_rows, dtype=jnp.int32))

        def compute(inner):
            maxes, totals, accum = inner
            scores = (
                jnp.einsum("qhd,khd->hqk", shaped_q, block_keys, preferred_element_type=jnp.float32)
                * scale
            )
            allowed = key_pos[None, None, :] <= query_pos[None, :, None]
            new_max = jnp.maximum(maxes, jnp.max(jnp.where(allowed, scores, -1e30), axis=-1))
            factor = jnp.exp(maxes - new_max)
            weights = jnp.where(allowed, jnp.exp(scores - new_max[..., None]), 0.0)
            totals = totals * factor + jnp.sum(weights, axis=-1)
            accum = accum * factor[..., None] + jnp.einsum(
                "hqk,khd->hqd",
                weights.astype(jnp.bfloat16),
                block_values,
                preferred_element_type=jnp.float32,
            )
            return (new_max, totals, accum)

        def keep(inner):
            return inner

        return lax.cond(jnp.min(key_pos) <= latest, compute, keep, state)

    maxes, totals, accum = lax.fori_loop(0, count_rows // span_rows, one_block, initial)
    result = accum / totals[..., None]
    return jnp.transpose(result, (1, 0, 2)).reshape(rows, local_heads * HD).astype(jnp.bfloat16)


def per_device(attn_query, attn_key, attn_value, out_weight):
    index = lax.axis_index("ctx")
    rows = attn_query.shape[0]
    local_rows = jnp.arange(rows, dtype=jnp.int32)
    query_pos = index * rows + local_rows

    def key_position(global_rows):
        return global_rows

    heads = attend(attn_query, attn_key, attn_value, query_pos, key_position)
    partial_value = jnp.dot(heads, out_weight, preferred_element_type=jnp.float32).astype(
        jnp.bfloat16
    )
    partial_value = lax.optimization_barrier(partial_value).astype(jnp.float32)
    attn_out = lax.psum_scatter(
        partial_value.astype(jnp.bfloat16), "tp", scatter_dimension=1, tiled=True
    )
    return attn_out


def solution(mesh):
    return jax.shard_map(
        per_device,
        mesh=mesh,
        in_specs=(P("ctx", "tp"), P("ctx", "tp"), P("ctx", "tp"), P("tp", None)),
        out_specs=P("ctx", "tp"),
        check_vma=False,
    )
```

profile of v0, /device:TPU:0, one launch (start us, length us, event | category | flops | bytes accessed | tf_op | source)
XLA Modules:
  0.0 253.7 jit_solution(6015835707041163254)
XLA Ops:
  6.5 2.0 copy.9
  8.6 0.0 all-gather.5.cloned.1.call-start
  8.7 2.1 copy.11
  10.8 0.7 add_reduce_fusion
  11.5 1.2 copy.10
  12.7 0.3 copy.12
  13.0 74.1 %all-gather.3.cloned.1.call-done = bf16[2048,1024]{0,1:T(8,128)(2,1)} async-done(((bf16[256,1024]{0,1:T(8,128)(2,1)}), bf16[2048,1024]{0,1:T(8,128)(2,1)}) %all-gather.3.cloned.1.call-update) | async-done | bytes 4194320 | tf_op jit(solution)/shard_map/all_gather | solution.py:20
  87.1 75.3 %all-gather.5.cloned.1.call-done = bf16[2048,1024]{0,1:T(8,128)(2,1)} async-done(((bf16[256,1024]{0,1:T(8,128)(2,1)}), bf16[2048,1024]{0,1:T(8,128)(2,1)}) %all-gather.5.cloned.1.call-update) | async-done | bytes 4194320 | tf_op jit(solution)/shard_map/all_gather | solution.py:21
  162.4 0.1 broadcast_in_dim.44
  162.5 13.2 %while.18 = (s32[]{:T(128)}, f32[8,256]{1,0:T(8,128)S(1)}, f32[8,256]{1,0:T(8,128)S(1)}, f32[8,256,128]{2,1,0:T(8,128)S(1)}, s32[]{:T(128)}, /*index=5*/bf16[204...) while((s32[]{:T(128)}, f32[8,256]{1,0:T(8,128)S(1)}, ...), condition=%wide.region_7.8_spmd.clone, body=%wide.region_1.7_spmd.clone.sunk | while | flops 549065984 | bytes 22159680 | solution.py:59
  162.5 0.6 iota_add_fusion.2
  164.4 5.4 %conditional.3 = ((f32[8,256]{1,0:T(8,128)S(1)}, f32[8,256]{1,0:T(8,128)S(1)}, f32[8,256,128]{2,1,0:T(8,128)S(1)})) conditional(s32[]{:T(128)} %convert_element_type.39, (f32[8,256]{1,0:T(8,128)S(1)}, f32[8,256]{1,0:T(8,128)S(1)}, f32[8,256,128]{2,1,0:T(8,128)S(1)}) %tuple.58, (s32[512]{0:T(512)S(1)}, s32[]{:T(128)}, s32[]{:T(128)}, ...), branch_computations={%region_3.0_spmd, %region_4.6_spmd} | conditional | flops 549064960 | bytes 22156362 | solution.py:57
  164.5 0.1 broadcast_compare_fusion
  164.6 1.7 constant_dynamic-slice_fusion
  166.3 0.9 fusion.2
  167.3 0.9 fusion.6
  168.1 1.7 fusion.13
  169.9 0.6 iota_add_fusion.2
  171.8 0.6 iota_add_fusion.2
  173.8 0.6 iota_add_fusion.2
  175.7 0.3 copy.13
  176.0 0.1 divide_convert_fusion
  176.2 12.1 %convolution_convert_fusion = bf16[256,8192]{1,0:T(8,128)(2,1)} fusion(bf16[256,1024]{0,1:T(8,128)(2,1)S(1)} %bitcast.30, bf16[1024,8192]{1,0:T(8,128)(2,1)} %param.11), kind=kOutput, calls=%fused_computation.24 | convolution fusion | flops 4297064448 | bytes 21495808 | tf_op jit(solution)/shard_map/dot_general | solution.py:74
  188.2 58.9 %reduce-scatter.2.cloned.1.call-done = bf16[256,2048]{1,0:T(8,128)(2,1)} async-done(((bf16[256,8192]{1,0:T(8,128)(2,1)}), bf16[256,2048]{1,0:T(8,128)(2,1)}) %reduce-scatter.2.cloned.1.call-update) | async-done | bytes 1048592 | tf_op jit(solution)/shard_map/reduce_scatter | solution.py:78
  (18 shorter events, 0.2 us)
Async XLA Ops:
  6.5 80.6 %all-gather.3.cloned.1.call-start = ((), (), s32[]{:S(2)}) async-start(), calls=%async_computation.1 | async-start | bytes 4718592 | tf_op jit(solution)/shard_map/all_gather | solution.py:20
  8.6 153.8 %all-gather.5.cloned.1.call-start = ((), (), s32[]{:S(2)}) async-start(), calls=%async_computation.2 | async-start | bytes 4718592 | tf_op jit(solution)/shard_map/all_gather | solution.py:21
  10.8 236.4 %reduce-scatter.2.cloned.1.call-start = ((), (), s32[]{:S(2)}) async-start(), calls=%async_computation.3 | async-start | bytes 5242880 | tf_op jit(solution)/shard_map/reduce_scatter | solution.py:78
Sparse Core Ops, SparseCore 0:
  9.4 77.7 all-gather.2
  89.2 73.1 all-gather.4
  188.4 58.7 reduce-scatter.1
where the time goes:
time: 254 us
  waiting for transfers between devices  208 us (82%)
  matrix products  14.7 us (6%)
  between operations  13.1 us (5%)
  local copies, waits for them, and re-layouts  7.76 us (3%)
  loops' own time  5.29 us (2%)
  other arithmetic  4.35 us (2%)
    all_gather x1, waiting for transfers between devices, attend(): piece_values = lax.all_gather(values, 'ctx', axis=0, tiled=True)  75.3 us
    all_gather x1, waiting for transfers between devices, attend(): piece_keys = lax.all_gather(keys, 'ctx', axis=0, tiled=True)  74.1 us
    reduce_scatter x1, waiting for transfers between devices, per_device(): lax.psum_scatter(partial_value.astype(jnp.bfloat16), 'tp', scatter_dimens...  58.9 us
    dot_general x1, matrix products, per_device(): jnp.dot(heads, out_weight, preferred_element_type=jnp.float32)  12.1 us
    unnamed x4, local copies, waits for them, and re-layouts  5.65 us
    another operation x1, loops' own time, attend(): lax.fori_loop(0, count_rows // span_rows, one_block, initial)  5.17 us
  transfers between devices with their start and end apart: 3, of which 3 were waited for; matrix products, arithmetic and copies ran while one was open for 2% of the time, Pallas kernels for 0%

commit v1 on v0

--- a/solution.py
+++ b/solution.py
@@ -1,12 +1,22 @@
+import functools
+
 import jax
 import jax.numpy as jnp
 from jax import lax
+from jax.experimental import pallas as pl
+from jax.experimental.pallas import tpu as pltpu
 from jax.sharding import PartitionSpec as P
 
 HD = 128
-
-
-def attend(queries, keys, values, query_pos, key_position):
+MIB = 1 << 20
+VMEM = pl.BlockSpec(memory_space=pltpu.VMEM)
+
+
+def params(mib):
+    return pltpu.CompilerParams(vmem_limit_bytes=mib * MIB)
+
+
+def attend(queries, keys, values, query_pos):
     rows = queries.shape[0]
     local_heads = queries.shape[1] // HD
     scale = HD ** (-0.5)
@@ -20,7 +30,7 @@
     piece_keys = lax.all_gather(keys, "ctx", axis=0, tiled=True)
     piece_values = lax.all_gather(values, "ctx", axis=0, tiled=True)
     count_rows = piece_keys.shape[0]
-    span_rows = 512
+    span_rows = 2 * rows
 
     def one_block(block, state):
         offset = block * span_rows
@@ -30,7 +40,7 @@
         block_values = lax.dynamic_slice_in_dim(piece_values, offset, span_rows, 0).reshape(
             span_rows, local_heads, HD
         )
-        key_pos = key_position(offset + jnp.arange(span_rows, dtype=jnp.int32))
+        key_pos = offset + jnp.arange(span_rows, dtype=jnp.int32)
 
         def compute(inner):
             maxes, totals, accum = inner
@@ -51,37 +61,197 @@
             )
             return (new_max, totals, accum)
 
-        def keep(inner):
-            return inner
-
-        return lax.cond(jnp.min(key_pos) <= latest, compute, keep, state)
+        return lax.cond(jnp.min(key_pos) <= latest, compute, lambda inner: inner, state)
 
     maxes, totals, accum = lax.fori_loop(0, count_rows // span_rows, one_block, initial)
     result = accum / totals[..., None]
     return jnp.transpose(result, (1, 0, 2)).reshape(rows, local_heads * HD).astype(jnp.bfloat16)
 
 
-def per_device(attn_query, attn_key, attn_value, out_weight):
-    index = lax.axis_index("ctx")
+def gather_form(attn_query, attn_key, attn_value, out_weight):
     rows = attn_query.shape[0]
-    local_rows = jnp.arange(rows, dtype=jnp.int32)
-    query_pos = index * rows + local_rows
-
-    def key_position(global_rows):
-        return global_rows
-
-    heads = attend(attn_query, attn_key, attn_value, query_pos, key_position)
-    partial_value = jnp.dot(heads, out_weight, preferred_element_type=jnp.float32).astype(
-        jnp.bfloat16
-    )
-    partial_value = lax.optimization_barrier(partial_value).astype(jnp.float32)
-    attn_out = lax.psum_scatter(
+    query_pos = lax.axis_index("ctx") * rows + jnp.arange(rows, dtype=jnp.int32)
+    heads = attend(attn_query, attn_key, attn_value, query_pos)
+    partial_value = jnp.dot(heads, out_weight, preferred_element_type=jnp.float32)
+    return lax.psum_scatter(
         partial_value.astype(jnp.bfloat16), "tp", scatter_dimension=1, tiled=True
     )
-    return attn_out
+
+
+def pack_kernel(n, me_ref, q_ref, k_ref, v_ref, *outs):
+    rows = q_ref.shape[0]
+    for shift in range(n):
+        head = lax.rem(me_ref[0] + shift, n)
+        cols = pl.ds(pl.multiple_of(head * HD, HD), HD)
+        for part, ref in enumerate((q_ref, k_ref, v_ref)):
+            outs[shift][part * rows : (part + 1) * rows, :] = ref[:, cols]
+
+
+def attention_kernel(n, me_ref, *refs):
+    packed, outs = refs[:n], refs[n : 2 * n]
+    q_all, k_all, v_all, o_all = refs[2 * n :]
+    rows = packed[0].shape[0] // 3
+    me = me_ref[0]
+    for shift in range(n):
+        block = lax.rem(me - shift + n, n)
+        at = pl.ds(pl.multiple_of(block * rows, rows), rows)
+        q_all[at, :] = packed[shift][0:rows, :]
+        k_all[at, :] = packed[shift][rows : 2 * rows, :]
+        v_all[at, :] = packed[shift][2 * rows : 3 * rows, :]
+    factor = HD ** (-0.5) * 1.4426950408889634
+    diag = lax.broadcasted_iota(jnp.int32, (rows, rows), 1) <= lax.broadcasted_iota(
+        jnp.int32, (rows, rows), 0
+    )
+    for block in range(n):
+        lo, hi = block * rows, (block + 1) * rows
+        query = q_all[lo:hi, :]
+        dims = (((1,), (1,)), ((), ()))
+        last = lax.dot_general(query, k_all[lo:hi, :], dims, preferred_element_type=jnp.float32)
+        last = jnp.where(diag, last, -1e30)
+        top = jnp.max(last, axis=1, keepdims=True)
+        if block:
+            early = lax.dot_general(
+                query, k_all[0:lo, :], dims, preferred_element_type=jnp.float32
+            )
+            top = jnp.maximum(top, jnp.max(early, axis=1, keepdims=True))
+        w_last = jnp.where(diag, jnp.exp2((last - top) * factor), 0.0)
+        total = jnp.sum(w_last, axis=1, keepdims=True)
+        acc = jnp.dot(
+            w_last.astype(jnp.bfloat16), v_all[lo:hi, :], preferred_element_type=jnp.float32
+        )
+        if block:
+            w_early = jnp.exp2((early - top) * factor)
+            total += jnp.sum(w_early, axis=1, keepdims=True)
+            acc += jnp.dot(
+                w_early.astype(jnp.bfloat16), v_all[0:lo, :], preferred_element_type=jnp.float32
+            )
+        o_all[lo:hi, :] = (acc / total).astype(jnp.bfloat16)
+    for shift in range(n):
+        block = lax.rem(me + shift, n)
+        outs[shift][...] = o_all[pl.ds(pl.multiple_of(block * rows, rows), rows), :]
+
+
+def project_kernel(n, tiles, scalar_ref, *refs):
+    pieces, w_ref, outs, heads = refs[:n], refs[n], refs[n + 1 : n + 3], refs[n + 3]
+    step = pl.program_id(0)
+
+    @pl.when(step == 0)
+    def _():
+        for shift in range(n):
+            head = lax.rem(scalar_ref[0] - shift + n, n)
+            heads[:, pl.ds(pl.multiple_of(head * HD, HD), HD)] = pieces[shift][...]
+
+    product = jnp.dot(heads[...], w_ref[...], preferred_element_type=jnp.float32)
+    for which in range(2):
+
+        @pl.when(step // tiles == which)
+        def _():
+            outs[which][...] = product.astype(jnp.bfloat16)
+
+
+def project(scalars, pieces, weight, cols, tile):
+    n, rows = len(pieces), pieces[0].shape[0]
+    depth = weight.shape[0]
+    tiles = cols // tile
+    out = jax.ShapeDtypeStruct((rows, cols), jnp.bfloat16)
+    return pl.pallas_call(
+        functools.partial(project_kernel, n, tiles),
+        grid_spec=pltpu.PrefetchScalarGridSpec(
+            num_scalar_prefetch=1,
+            grid=(2 * tiles,),
+            in_specs=[pl.BlockSpec((rows, HD), lambda i, s: (0, 0)) for _ in range(n)]
+            + [
+                pl.BlockSpec(
+                    (depth, tile),
+                    lambda i, s: (0, jnp.where(i < tiles, s[1], s[2]) * tiles + lax.rem(i, tiles)),
+                )
+            ],
+            out_specs=[
+                pl.BlockSpec((rows, tile), lambda i, s: (0, jnp.minimum(i, tiles - 1))),
+                pl.BlockSpec((rows, tile), lambda i, s: (0, jnp.maximum(i - tiles, 0))),
+            ],
+            scratch_shapes=[pltpu.VMEM((rows, depth), jnp.bfloat16)],
+        ),
+        out_shape=[out, out],
+        compiler_params=params(40),
+        cost_estimate=pl.CostEstimate(
+            flops=4 * rows * depth * cols, bytes_accessed=4 * depth * cols, transcendentals=0
+        ),
+    )(scalars, *pieces, weight)
+
+
+def heads_form(attn_query, attn_key, attn_value, out_weight):
+    n = lax.axis_size("ctx")
+    tp = lax.axis_size("tp")
+    rows = attn_query.shape[0]
+    me = lax.axis_index("ctx")
+    mine = lax.axis_index("tp")
+    me_arr = me.astype(jnp.int32).reshape(1)
+    smem = pl.BlockSpec(memory_space=pltpu.SMEM)
+    order = sorted(range(1, n), key=lambda s: -min(s, n - s))
+
+    def around(arrays):
+        got = [arrays[0]] + [None] * (n - 1)
+        for shift in order:
+            got[shift] = lax.ppermute(
+                arrays[shift], "ctx", [(i, (i + shift) % n) for i in range(n)]
+            )
+        return got
+
+    packed = pl.pallas_call(
+        functools.partial(pack_kernel, n),
+        in_specs=[smem] + [VMEM] * 3,
+        out_specs=[VMEM] * n,
+        out_shape=[jax.ShapeDtypeStruct((3 * rows, HD), jnp.bfloat16)] * n,
+        compiler_params=params(16),
+    )(me_arr, attn_query, attn_key, attn_value)
+    packed = around(packed)
+    pairs = n * (n + 1) // 2
+    outs = pl.pallas_call(
+        functools.partial(attention_kernel, n),
+        in_specs=[smem] + [VMEM] * n,
+        out_specs=[VMEM] * n,
+        out_shape=[jax.ShapeDtypeStruct((rows, HD), jnp.bfloat16)] * n,
+        scratch_shapes=[pltpu.VMEM((n * rows, HD), jnp.bfloat16)] * 4,
+        compiler_params=params(40),
+        cost_estimate=pl.CostEstimate(
+            flops=4 * pairs * rows * rows * HD,
+            bytes_accessed=8 * n * rows * HD,
+            transcendentals=pairs * rows * rows,
+        ),
+    )(me_arr, *packed)
+    pieces = around(outs)
+
+    cols = out_weight.shape[1] // tp
+    half = tp // 2
+    y, core = mine // 2, lax.rem(mine, 2)
+    swap = [(i, i ^ 1) for i in range(tp)]
+
+    def wanted(plane):
+        return jnp.stack([me, 2 * plane + 1 - core, 2 * plane + core]).astype(jnp.int32)
+
+    f32 = jnp.float32
+    crossing = []
+    for shift in range(1, half):
+        plane = lax.rem(y + shift, half)
+        give, keep = project(wanted(plane), pieces, out_weight, cols, 512)
+        both = (keep.astype(f32) + lax.ppermute(give, "tp", swap).astype(f32)).astype(jnp.bfloat16)
+        crossing.append(
+            lax.ppermute(both, "tp", [(i, (i + 2 * shift) % tp) for i in range(tp)])
+        )
+    give, keep = project(wanted(y), pieces, out_weight, cols, 512)
+    total = keep.astype(f32) + lax.ppermute(give, "tp", swap).astype(f32)
+    for one in crossing:
+        total += one.astype(f32)
+    return total.astype(jnp.bfloat16)
 
 
 def solution(mesh):
+    def per_device(attn_query, attn_key, attn_value, out_weight):
+        heads = attn_query.shape[1] // HD
+        form = heads_form if heads == mesh.shape["ctx"] else gather_form
+        return form(attn_query, attn_key, attn_value, out_weight)
+
     return jax.shard_map(
         per_device,
         mesh=mesh,

time: 254 us -> 107 us (0.42)
  waiting for transfers between devices: 208 us -> 40 us
  starting transfers between devices: 0.09 us -> 39.4 us
  Pallas kernels: 0 us -> 21.9 us
  matrix products: 14.7 us -> 0 us
  between operations: 13.1 us -> 0.07 us
  loops' own time: 5.29 us -> 0 us
  local copies, waits for them, and re-layouts: 7.76 us -> 3.12 us
    all_gather x2 -> x0, waiting for transfers between devices: 149 us -> none  [the longest x1 75.3 us: attend(): piece_values = lax.all_gather(values, 'ctx', axis=0, tiled=True)]
    reduce_scatter x1 -> x0, waiting for transfers between devices: 58.9 us -> none  [per_device(): lax.psum_scatter(partial_value.astype(jnp.bfloat16), 'tp', scatter_dimens...]
    ppermute x0 -> x17, waiting for transfers between devices: none -> 40 us  [the longest x1 23.3 us: heads_form(): lax.ppermute(both, 'tp', [(i, (i + 2 * shift) % tp) for i in range(tp)])]
    ppermute x0 -> x17, starting transfers between devices: none -> 39.4 us  [the longest x14 37.2 us: around(): lax.ppermute(arrays[shift], 'ctx', [(i, (i + shift) % n) for i in range(n)])]
    pallas_call x0 -> x4, Pallas kernels: none -> 21.9 us  [the longest x2 16.9 us: project(): pl.pallas_call(functools.partial(project_kernel, n, tiles), grid_spec=plt...]
    dot_general x3 -> x0, matrix products: 14.7 us -> none  [the longest x1 12.1 us: per_device(): jnp.dot(heads, out_weight, preferred_element_type=jnp.float32)]
    another operation x5 -> x0, loops' own time: 5.29 us -> none  [the longest x1 5.17 us: attend(): lax.fori_loop(0, count_rows // span_rows, one_block, initial)]
    add x6 -> x0, other arithmetic: 2.59 us -> none  [the longest x4 2.57 us: one_block(): key_pos = key_position(offset + jnp.arange(span_rows, dtype=jnp.int32))]
  transfers between devices with their start and end apart: 3 -> 17, of which waited for: 3 -> 10; matrix products, arithmetic and copies ran while one was open for 2% -> 0% of each run, Pallas kernels for 0% -> 8%
where the time goes in v1:
time: 107 us
  waiting for transfers between devices  40 us (37%)
  starting transfers between devices  39.4 us (37%)
  Pallas kernels  21.9 us (20%)
  local copies, waits for them, and re-layouts  3.12 us (3%)
  other arithmetic  1.97 us (2%)
    ppermute x14, starting transfers between devices, around(): lax.ppermute(arrays[shift], 'ctx', [(i, (i + shift) % n) for i in range(n)])  37.2 us
    ppermute x1, waiting for transfers between devices, heads_form(): lax.ppermute(both, 'tp', [(i, (i + 2 * shift) % tp) for i in range(tp)])  23.3 us
    pallas_call x2, Pallas kernels, project(): pl.pallas_call(functools.partial(project_kernel, n, tiles), grid_spec=plt...  16.9 us
    ppermute x14, waiting for transfers between devices, around(): lax.ppermute(arrays[shift], 'ctx', [(i, (i + shift) % n) for i in range(n)])  16.5 us
    pallas_call x1, Pallas kernels, heads_form(): pl.pallas_call(functools.partial(attention_kernel, n), in_specs=[smem] +...  4.65 us
    unnamed x6, local copies, waits for them, and re-layouts  3.12 us
  transfers between devices with their start and end apart: 17, of which 10 were waited for; matrix products, arithmetic and copies ran while one was open for 0% of the time, Pallas kernels for 8%

profile of v1, /device:TPU:0, one launch (start us, length us, event | category | flops | bytes accessed | tf_op | source)
XLA Modules:
  0.0 106.5 jit_solution(9534984901011932861)
XLA Ops:
  0.0 1.0 copy-done
  1.0 1.0 copy-done.1
  2.1 1.0 copy-done.2
  3.5 3.0 %collective-permute-start = (bf16[768,128]{1,0:T(8,128)(2,1)S(1)}, bf16[768,128]{1,0:T(8,128)(2,1)S(1)}, u32[]{:S(2)}, u32[]{:S(2)}) collective-permute-start(bf16[768,128]{1,0:T(8,128)(2,1)S(1)} %get-tuple-element.26), channel_id=1, source_target_pairs={{0,4},{4,8},{8,12},{12,16},{16,20},{20,24},{24,28},{28,0},{1,5},{5... | collective-permute-start | bytes 589832 | tf_op jit(solution)/shard_map/ppermute | solution.py:196
  6.5 1.6 %collective-permute-start.1 = (bf16[768,128]{1,0:T(8,128)(2,1)S(1)}, bf16[768,128]{1,0:T(8,128)(2,1)S(1)}, u32[]{:S(2)}, u32[]{:S(2)}) collective-permute-start(bf16[768,128]{1,0:T(8,128)(2,1)S(1)} %get-tuple-element.27), channel_id=1, source_target_pairs={{0,8},{4,12},{8,16},{12,20},{16,24},{20,28},{24,0},{28,4},{1,9},{5... | collective-permute-start | bytes 589832 | tf_op jit(solution)/shard_map/ppermute | solution.py:196
  8.1 2.6 %collective-permute-start.2 = (bf16[768,128]{1,0:T(8,128)(2,1)S(1)}, bf16[768,128]{1,0:T(8,128)(2,1)S(1)}, u32[]{:S(2)}, u32[]{:S(2)}) collective-permute-start(bf16[768,128]{1,0:T(8,128)(2,1)S(1)} %get-tuple-element.28), channel_id=1, source_target_pairs={{0,12},{4,16},{8,20},{12,24},{16,28},{20,0},{24,4},{28,8},{1,13},{... | collective-permute-start | bytes 589832 | tf_op jit(solution)/shard_map/ppermute | solution.py:196
  10.7 1.2 %collective-permute-start.3 = (bf16[768,128]{1,0:T(8,128)(2,1)S(1)}, bf16[768,128]{1,0:T(8,128)(2,1)S(1)}, u32[]{:S(2)}, u32[]{:S(2)}) collective-permute-start(bf16[768,128]{1,0:T(8,128)(2,1)S(1)} %get-tuple-element.29), channel_id=1, source_target_pairs={{0,16},{4,20},{8,24},{12,28},{16,0},{20,4},{24,8},{28,12},{1,17},{... | collective-permute-start | bytes 589832 | tf_op jit(solution)/shard_map/ppermute | solution.py:196
  11.9 2.6 %collective-permute-start.4 = (bf16[768,128]{1,0:T(8,128)(2,1)S(1)}, bf16[768,128]{1,0:T(8,128)(2,1)S(1)}, u32[]{:S(2)}, u32[]{:S(2)}) collective-permute-start(bf16[768,128]{1,0:T(8,128)(2,1)S(1)} %get-tuple-element.30), channel_id=1, source_target_pairs={{0,20},{4,24},{8,28},{12,0},{16,4},{20,8},{24,12},{28,16},{1,21},{... | collective-permute-start | bytes 589832 | tf_op jit(solution)/shard_map/ppermute | solution.py:196
  15.5 1.8 %collective-permute-start.5 = (bf16[768,128]{1,0:T(8,128)(2,1)S(1)}, bf16[768,128]{1,0:T(8,128)(2,1)S(1)}, u32[]{:S(2)}, u32[]{:S(2)}) collective-permute-start(bf16[768,128]{1,0:T(8,128)(2,1)S(1)} %get-tuple-element.31), channel_id=1, source_target_pairs={{0,24},{4,28},{8,0},{12,4},{16,8},{20,12},{24,16},{28,20},{1,25},{... | collective-permute-start | bytes 589832 | tf_op jit(solution)/shard_map/ppermute | solution.py:196
  17.3 3.4 %collective-permute-start.6 = (bf16[768,128]{1,0:T(8,128)(2,1)S(1)}, bf16[768,128]{1,0:T(8,128)(2,1)S(1)}, u32[]{:S(2)}, u32[]{:S(2)}) collective-permute-start(bf16[768,128]{1,0:T(8,128)(2,1)S(1)} %get-tuple-element.32), channel_id=1, source_target_pairs={{0,28},{4,0},{8,4},{12,8},{16,12},{20,16},{24,20},{28,24},{1,29},{... | collective-permute-start | bytes 589832 | tf_op jit(solution)/shard_map/ppermute | solution.py:196
  20.8 10.7 %collective-permute-done.2.refs_3_ = bf16[768,128]{1,0:T(8,128)(2,1)S(1)} collective-permute-done((bf16[768,128]{1,0:T(8,128)(2,1)S(1)}, bf16[768,128]{1,0:T(8,128)(2,1)S(1)}, u32[]{:S(2)}, u32[]{:S(2)}) %collective-permute-start.2) | collective-permute-done | bytes 196640 | tf_op jit(solution)/shard_map/ppermute | solution.py:196
  31.7 1.4 %collective-permute-done.6.refs_7_ = bf16[768,128]{1,0:T(8,128)(2,1)S(1)} collective-permute-done((bf16[768,128]{1,0:T(8,128)(2,1)S(1)}, bf16[768,128]{1,0:T(8,128)(2,1)S(1)}, u32[]{:S(2)}, u32[]{:S(2)}) %collective-permute-start.6) | collective-permute-done | bytes 196640 | tf_op jit(solution)/shard_map/ppermute | solution.py:196
  33.1 4.6 %shard_map.47 = (bf16[256,128]{1,0:T(8,128)(2,1)S(1)}, bf16[256,128]{1,0:T(8,128)(2,1)S(1)}, bf16[256,128]{1,0:T(8,128)(2,1)S(1)}, bf16[256,128]{1,0:T(8,128)(2,...) custom-call(s32[1]{0:T(128)} %bitcast.me_ref, ...), custom_call_target="tpu_custom_call" | custom-call | flops 1207959552 | bytes 2097152 | tf_op jit(solution)/shard_map/pallas_call | solution.py:210
  37.8 4.3 %collective-permute-start.7 = (bf16[256,128]{1,0:T(8,128)(2,1)S(1)}, bf16[256,128]{1,0:T(8,128)(2,1)S(1)}, u32[]{:S(2)}, u32[]{:S(2)}) collective-permute-start(bf16[256,128]{1,0:T(8,128)(2,1)S(1)} %get-tuple-element.34), channel_id=1, source_target_pairs={{0,4},{4,8},{8,12},{12,16},{16,20},{20,24},{24,28},{28,0},{1,5},{5... | collective-permute-start | bytes 196616 | tf_op jit(solution)/shard_map/ppermute | solution.py:196
  42.1 8.9 %collective-permute-start.8 = (bf16[256,128]{1,0:T(8,128)(2,1)S(1)}, bf16[256,128]{1,0:T(8,128)(2,1)S(1)}, u32[]{:S(2)}, u32[]{:S(2)}) collective-permute-start(bf16[256,128]{1,0:T(8,128)(2,1)S(1)} %get-tuple-element.35), channel_id=1, source_target_pairs={{0,8},{4,12},{8,16},{12,20},{16,24},{20,28},{24,0},{28,4},{1,9},{5... | collective-permute-start | bytes 196616 | tf_op jit(solution)/shard_map/ppermute | solution.py:196
  51.0 2.1 %collective-permute-start.10 = (bf16[256,128]{1,0:T(8,128)(2,1)S(1)}, bf16[256,128]{1,0:T(8,128)(2,1)S(1)}, u32[]{:S(2)}, u32[]{:S(2)}) collective-permute-start(bf16[256,128]{1,0:T(8,128)(2,1)S(1)} %get-tuple-element.37), channel_id=1, source_target_pairs={{0,16},{4,20},{8,24},{12,28},{16,0},{20,4},{24,8},{28,12},{1,17},{... | collective-permute-start | bytes 196616 | tf_op jit(solution)/shard_map/ppermute | solution.py:196
  53.1 3.4 %collective-permute-start.11 = (bf16[256,128]{1,0:T(8,128)(2,1)S(1)}, bf16[256,128]{1,0:T(8,128)(2,1)S(1)}, u32[]{:S(2)}, u32[]{:S(2)}) collective-permute-start(bf16[256,128]{1,0:T(8,128)(2,1)S(1)} %get-tuple-element.38), channel_id=1, source_target_pairs={{0,20},{4,24},{8,28},{12,0},{16,4},{20,8},{24,12},{28,16},{1,21},{... | collective-permute-start | bytes 196616 | tf_op jit(solution)/shard_map/ppermute | solution.py:196
  57.2 1.5 %collective-permute-start.13 = (bf16[256,128]{1,0:T(8,128)(2,1)S(1)}, bf16[256,128]{1,0:T(8,128)(2,1)S(1)}, u32[]{:S(2)}, u32[]{:S(2)}) collective-permute-start(bf16[256,128]{1,0:T(8,128)(2,1)S(1)} %get-tuple-element.40), channel_id=1, source_target_pairs={{0,28},{4,0},{8,4},{12,8},{16,12},{20,16},{24,20},{28,24},{1,29},{... | collective-permute-start | bytes 196616 | tf_op jit(solution)/shard_map/ppermute | solution.py:196
  59.1 1.2 %collective-permute-done.10.refs_4_ = bf16[256,128]{1,0:T(8,128)(2,1)S(1)} collective-permute-done((bf16[256,128]{1,0:T(8,128)(2,1)S(1)}, bf16[256,128]{1,0:T(8,128)(2,1)S(1)}, u32[]{:S(2)}, u32[]{:S(2)}) %collective-permute-start.10) | collective-permute-done | bytes 65568 | tf_op jit(solution)/shard_map/ppermute | solution.py:196
  62.0 8.4 %shard_map.49 = (bf16[256,2048]{1,0:T(8,128)(2,1)S(1)}, bf16[256,2048]{1,0:T(8,128)(2,1)S(1)}) custom-call(s32[3]{0:T(128)S(1)} %get-tuple-element.46.scalar_ref, bf16[256,128]{1,0:T(8,128)(2,1)S(1)} %get-tuple-element.33.refs_0_, bf16[256,128]{1,0:T(8,128)(2,1)S(1)} %collective-permute-done.7.refs_1_, bf16[256,128]{1,0:T(8,128)(2,1)S(1)} %collective-permute-done.8.refs_2_, ...), custom_call_target="tpu_custom_call" | custom-call | flops 2147483648 | bytes 8388608 | tf_op jit(solution)/shard_map/pallas_call | solution.py:157
  70.5 8.4 %shard_map.48 = (bf16[256,2048]{1,0:T(8,128)(2,1)S(1)}, bf16[256,2048]{1,0:T(8,128)(2,1)S(1)}) custom-call(s32[3]{0:T(128)S(1)} %get-tuple-element.45.scalar_ref, bf16[256,128]{1,0:T(8,128)(2,1)S(1)} %get-tuple-element.33.refs_0_, bf16[256,128]{1,0:T(8,128)(2,1)S(1)} %collective-permute-done.7.refs_1_, bf16[256,128]{1,0:T(8,128)(2,1)S(1)} %collective-permute-done.8.refs_2_, ...), custom_call_target="tpu_custom_call" | custom-call | flops 2147483648 | bytes 8388608 | tf_op jit(solution)/shard_map/pallas_call | solution.py:157
  79.9 1.6 %collective-permute-start.16 = (bf16[256,2048]{1,0:T(8,128)(2,1)S(1)}, bf16[256,2048]{1,0:T(8,128)(2,1)S(1)}, u32[]{:S(2)}, u32[]{:S(2)}) collective-permute-start(bf16[256,2048]{1,0:T(8,128)(2,1)S(1)} %add_convert_fusion.1), channel_id=1, source_target_pairs={{0,2},{1,3},{2,0},{3,1},{4,6},{5,7},{6,4},{7,5},{8,10},{9,11},{10,... | collective-permute-start | bytes 3145736 | tf_op jit(solution)/shard_map/ppermute | solution.py:240
  81.8 23.3 %collective-permute-done.16 = bf16[256,2048]{1,0:T(8,128)(2,1)S(1)} collective-permute-done((bf16[256,2048]{1,0:T(8,128)(2,1)S(1)}, bf16[256,2048]{1,0:T(8,128)(2,1)S(1)}, u32[]{:S(2)}, u32[]{:S(2)}) %collective-permute-start.16) | collective-permute-done | bytes 1048608 | tf_op jit(solution)/shard_map/ppermute | solution.py:240
  105.0 1.5 %add_convert_fusion = bf16[256,2048]{1,0:T(8,128)(2,1)} fusion(bf16[256,2048]{1,0:T(8,128)(2,1)S(1)} %collective-permute-done.16, bf16[256,2048]{1,0:T(8,128)(2,1)S(1)} %collective-permute-done.14, bf16[256,2048]{1,0:T(8,128)(2,1)S(1)} %get-tuple-element.41), kind=kLoop, calls=%fused_computation | loop fusion | flops 3145728 | bytes 4194304 | tf_op jit(solution)/shard_map/convert_element_type | solution.py:246
  (23 shorter events, 5.8 us)
Async XLA Ops:
  0.0 1.0 copy-start
  1.0 1.0 copy-start.1
  2.1 1.0 copy-start.2
  3.5 12.0 %collective-permute-start = (bf16[768,128]{1,0:T(8,128)(2,1)S(1)}, bf16[768,128]{1,0:T(8,128)(2,1)S(1)}, u32[]{:S(2)}, u32[]{:S(2)}) collective-permute-start(bf16[768,128]{1,0:T(8,128)(2,1)S(1)} %get-tuple-element.26), channel_id=1, source_target_pairs={{0,4},{4,8},{8,12},{12,16},{16,20},{20,24},{24,28},{28,0},{1,5},{5... | collective-permute-start | bytes 589832 | tf_op jit(solution)/shard_map/ppermute | solution.py:196
  6.5 10.8 %collective-permute-start.1 = (bf16[768,128]{1,0:T(8,128)(2,1)S(1)}, bf16[768,128]{1,0:T(8,128)(2,1)S(1)}, u32[]{:S(2)}, u32[]{:S(2)}) collective-permute-start(bf16[768,128]{1,0:T(8,128)(2,1)S(1)} %get-tuple-element.27), channel_id=1, source_target_pairs={{0,8},{4,12},{8,16},{12,20},{16,24},{20,28},{24,0},{28,4},{1,9},{5... | collective-permute-start | bytes 589832 | tf_op jit(solution)/shard_map/ppermute | solution.py:196
  8.1 23.4 %collective-permute-start.2 = (bf16[768,128]{1,0:T(8,128)(2,1)S(1)}, bf16[768,128]{1,0:T(8,128)(2,1)S(1)}, u32[]{:S(2)}, u32[]{:S(2)}) collective-permute-start(bf16[768,128]{1,0:T(8,128)(2,1)S(1)} %get-tuple-element.28), channel_id=1, source_target_pairs={{0,12},{4,16},{8,20},{12,24},{16,28},{20,0},{24,4},{28,8},{1,13},{... | collective-permute-start | bytes 589832 | tf_op jit(solution)/shard_map/ppermute | solution.py:196
  10.7 21.0 %collective-permute-start.3 = (bf16[768,128]{1,0:T(8,128)(2,1)S(1)}, bf16[768,128]{1,0:T(8,128)(2,1)S(1)}, u32[]{:S(2)}, u32[]{:S(2)}) collective-permute-start(bf16[768,128]{1,0:T(8,128)(2,1)S(1)} %get-tuple-element.29), channel_id=1, source_target_pairs={{0,16},{4,20},{8,24},{12,28},{16,0},{20,4},{24,8},{28,12},{1,17},{... | collective-permute-start | bytes 589832 | tf_op jit(solution)/shard_map/ppermute | solution.py:196
  11.9 19.8 %collective-permute-start.4 = (bf16[768,128]{1,0:T(8,128)(2,1)S(1)}, bf16[768,128]{1,0:T(8,128)(2,1)S(1)}, u32[]{:S(2)}, u32[]{:S(2)}) collective-permute-start(bf16[768,128]{1,0:T(8,128)(2,1)S(1)} %get-tuple-element.30), channel_id=1, source_target_pairs={{0,20},{4,24},{8,28},{12,0},{16,4},{20,8},{24,12},{28,16},{1,21},{... | collective-permute-start | bytes 589832 | tf_op jit(solution)/shard_map/ppermute | solution.py:196
  15.5 16.2 %collective-permute-start.5 = (bf16[768,128]{1,0:T(8,128)(2,1)S(1)}, bf16[768,128]{1,0:T(8,128)(2,1)S(1)}, u32[]{:S(2)}, u32[]{:S(2)}) collective-permute-start(bf16[768,128]{1,0:T(8,128)(2,1)S(1)} %get-tuple-element.31), channel_id=1, source_target_pairs={{0,24},{4,28},{8,0},{12,4},{16,8},{20,12},{24,16},{28,20},{1,25},{... | collective-permute-start | bytes 589832 | tf_op jit(solution)/shard_map/ppermute | solution.py:196
  17.3 15.8 %collective-permute-start.6 = (bf16[768,128]{1,0:T(8,128)(2,1)S(1)}, bf16[768,128]{1,0:T(8,128)(2,1)S(1)}, u32[]{:S(2)}, u32[]{:S(2)}) collective-permute-start(bf16[768,128]{1,0:T(8,128)(2,1)S(1)} %get-tuple-element.32), channel_id=1, source_target_pairs={{0,28},{4,0},{8,4},{12,8},{16,12},{20,16},{24,20},{28,24},{1,29},{... | collective-permute-start | bytes 589832 | tf_op jit(solution)/shard_map/ppermute | solution.py:196
  37.8 18.7 %collective-permute-start.7 = (bf16[256,128]{1,0:T(8,128)(2,1)S(1)}, bf16[256,128]{1,0:T(8,128)(2,1)S(1)}, u32[]{:S(2)}, u32[]{:S(2)}) collective-permute-start(bf16[256,128]{1,0:T(8,128)(2,1)S(1)} %get-tuple-element.34), channel_id=1, source_target_pairs={{0,4},{4,8},{8,12},{12,16},{16,20},{20,24},{24,28},{28,0},{1,5},{5... | collective-permute-start | bytes 196616 | tf_op jit(solution)/shard_map/ppermute | solution.py:196
  42.1 15.1 %collective-permute-start.8 = (bf16[256,128]{1,0:T(8,128)(2,1)S(1)}, bf16[256,128]{1,0:T(8,128)(2,1)S(1)}, u32[]{:S(2)}, u32[]{:S(2)}) collective-permute-start(bf16[256,128]{1,0:T(8,128)(2,1)S(1)} %get-tuple-element.35), channel_id=1, source_target_pairs={{0,8},{4,12},{8,16},{12,20},{16,24},{20,28},{24,0},{28,4},{1,9},{5... | collective-permute-start | bytes 196616 | tf_op jit(solution)/shard_map/ppermute | solution.py:196
  51.0 8.1 %collective-permute-start.9 = (bf16[256,128]{1,0:T(8,128)(2,1)S(1)}, bf16[256,128]{1,0:T(8,128)(2,1)S(1)}, u32[]{:S(2)}, u32[]{:S(2)}) collective-permute-start(bf16[256,128]{1,0:T(8,128)(2,1)S(1)} %get-tuple-element.36), channel_id=1, source_target_pairs={{0,12},{4,16},{8,20},{12,24},{16,28},{20,0},{24,4},{28,8},{1,13},{... | collective-permute-start | bytes 196616 | tf_op jit(solution)/shard_map/ppermute | solution.py:196
  51.0 9.3 %collective-permute-start.10 = (bf16[256,128]{1,0:T(8,128)(2,1)S(1)}, bf16[256,128]{1,0:T(8,128)(2,1)S(1)}, u32[]{:S(2)}, u32[]{:S(2)}) collective-permute-start(bf16[256,128]{1,0:T(8,128)(2,1)S(1)} %get-tuple-element.37), channel_id=1, source_target_pairs={{0,16},{4,20},{8,24},{12,28},{16,0},{20,4},{24,8},{28,12},{1,17},{... | collective-permute-start | bytes 196616 | tf_op jit(solution)/shard_map/ppermute | solution.py:196
  53.1 7.9 %collective-permute-start.11 = (bf16[256,128]{1,0:T(8,128)(2,1)S(1)}, bf16[256,128]{1,0:T(8,128)(2,1)S(1)}, u32[]{:S(2)}, u32[]{:S(2)}) collective-permute-start(bf16[256,128]{1,0:T(8,128)(2,1)S(1)} %get-tuple-element.38), channel_id=1, source_target_pairs={{0,20},{4,24},{8,28},{12,0},{16,4},{20,8},{24,12},{28,16},{1,21},{... | collective-permute-start | bytes 196616 | tf_op jit(solution)/shard_map/ppermute | solution.py:196
  56.4 5.5 %collective-permute-start.12 = (bf16[256,128]{1,0:T(8,128)(2,1)S(1)}, bf16[256,128]{1,0:T(8,128)(2,1)S(1)}, u32[]{:S(2)}, u32[]{:S(2)}) collective-permute-start(bf16[256,128]{1,0:T(8,128)(2,1)S(1)} %get-tuple-element.39), channel_id=1, source_target_pairs={{0,24},{4,28},{8,0},{12,4},{16,8},{20,12},{24,16},{28,20},{1,25},{... | collective-permute-start | bytes 196616 | tf_op jit(solution)/shard_map/ppermute | solution.py:196
  57.2 4.8 %collective-permute-start.13 = (bf16[256,128]{1,0:T(8,128)(2,1)S(1)}, bf16[256,128]{1,0:T(8,128)(2,1)S(1)}, u32[]{:S(2)}, u32[]{:S(2)}) collective-permute-start(bf16[256,128]{1,0:T(8,128)(2,1)S(1)} %get-tuple-element.40), channel_id=1, source_target_pairs={{0,28},{4,0},{8,4},{12,8},{16,12},{20,16},{24,20},{28,24},{1,29},{... | collective-permute-start | bytes 196616 | tf_op jit(solution)/shard_map/ppermute | solution.py:196
  70.4 9.1 %collective-permute-start.15 = (bf16[256,2048]{1,0:T(8,128)(2,1)S(1)}, bf16[256,2048]{1,0:T(8,128)(2,1)S(1)}, u32[]{:S(2)}, u32[]{:S(2)}) collective-permute-start(bf16[256,2048]{1,0:T(8,128)(2,1)S(1)} %get-tuple-element.44), channel_id=1, source_target_pairs={{0,1},{1,0},{2,3},{3,2},{4,5},{5,4},{6,7},{7,6},{8,9},{9,8},{10,11... | collective-permute-start | bytes 3145736 | tf_op jit(solution)/shard_map/ppermute | solution.py:238
  78.9 2.8 %collective-permute-start.14 = (bf16[256,2048]{1,0:T(8,128)(2,1)S(1)}, bf16[256,2048]{1,0:T(8,128)(2,1)S(1)}, u32[]{:S(2)}, u32[]{:S(2)}) collective-permute-start(bf16[256,2048]{1,0:T(8,128)(2,1)S(1)} %get-tuple-element.42), channel_id=1, source_target_pairs={{0,1},{1,0},{2,3},{3,2},{4,5},{5,4},{6,7},{7,6},{8,9},{9,8},{10,11... | collective-permute-start | bytes 3145736 | tf_op jit(solution)/shard_map/ppermute | solution.py:243
  79.9 25.1 %collective-permute-start.16 = (bf16[256,2048]{1,0:T(8,128)(2,1)S(1)}, bf16[256,2048]{1,0:T(8,128)(2,1)S(1)}, u32[]{:S(2)}, u32[]{:S(2)}) collective-permute-start(bf16[256,2048]{1,0:T(8,128)(2,1)S(1)} %add_convert_fusion.1), channel_id=1, source_target_pairs={{0,2},{1,3},{2,0},{3,1},{4,6},{5,7},{6,4},{7,5},{8,10},{9,11},{10,... | collective-permute-start | bytes 3145736 | tf_op jit(solution)/shard_map/ppermute | solution.py:240

commit v2 on v1

--- a/solution.py
+++ b/solution.py
@@ -9,6 +9,9 @@
 
 HD = 128
 MIB = 1 << 20
+OWN_PARTS = 2
+FETCH_MIB = 40
+COST = pl.CostEstimate(flops=1, bytes_accessed=1, transcendentals=1)
 VMEM = pl.BlockSpec(memory_space=pltpu.VMEM)
 
 
@@ -78,13 +81,21 @@
     )
 
 
-def pack_kernel(n, me_ref, q_ref, k_ref, v_ref, *outs):
+def pack_kernel(n, me_ref, q_ref, k_ref, v_ref, *refs):
+    outs, (held, sem) = refs[:n], refs[n:]
     rows = q_ref.shape[0]
-    for shift in range(n):
-        head = lax.rem(me_ref[0] + shift, n)
-        cols = pl.ds(pl.multiple_of(head * HD, HD), HD)
-        for part, ref in enumerate((q_ref, k_ref, v_ref)):
-            outs[shift][part * rows : (part + 1) * rows, :] = ref[:, cols]
+    copies = [
+        pltpu.make_async_copy(ref, held.at[part], sem.at[part])
+        for part, ref in enumerate((q_ref, k_ref, v_ref))
+    ]
+    for one in copies:
+        one.start()
+    for part, one in enumerate(copies):
+        one.wait()
+        for shift in range(n):
+            head = lax.rem(me_ref[0] + shift, n)
+            cols = pl.ds(pl.multiple_of(head * HD, HD), HD)
+            outs[shift][part * rows : (part + 1) * rows, :] = held[part, :, cols]
 
 
 def attention_kernel(n, me_ref, *refs):
@@ -114,7 +125,7 @@
                 query, k_all[0:lo, :], dims, preferred_element_type=jnp.float32
             )
             top = jnp.maximum(top, jnp.max(early, axis=1, keepdims=True))
-        w_last = jnp.where(diag, jnp.exp2((last - top) * factor), 0.0)
+        w_last = jnp.exp2((last - top) * factor)
         total = jnp.sum(w_last, axis=1, keepdims=True)
         acc = jnp.dot(
             w_last.astype(jnp.bfloat16), v_all[lo:hi, :], preferred_element_type=jnp.float32
@@ -131,53 +142,60 @@
         outs[shift][...] = o_all[pl.ds(pl.multiple_of(block * rows, rows), rows), :]
 
 
-def project_kernel(n, tiles, scalar_ref, *refs):
-    pieces, w_ref, outs, heads = refs[:n], refs[n], refs[n + 1 : n + 3], refs[n + 3]
-    step = pl.program_id(0)
-
-    @pl.when(step == 0)
-    def _():
-        for shift in range(n):
-            head = lax.rem(scalar_ref[0] - shift + n, n)
-            heads[:, pl.ds(pl.multiple_of(head * HD, HD), HD)] = pieces[shift][...]
-
-    product = jnp.dot(heads[...], w_ref[...], preferred_element_type=jnp.float32)
-    for which in range(2):
-
-        @pl.when(step // tiles == which)
-        def _():
-            outs[which][...] = product.astype(jnp.bfloat16)
-
-
-def project(scalars, pieces, weight, cols, tile):
+def fetch_kernel(place_ref, w_ref, *refs):
+    outs, sem = refs[:-1], refs[-1]
+    cols = outs[0].shape[1]
+    copies = []
+    for which, out in enumerate(outs):
+        at = pl.ds(pl.multiple_of(place_ref[1 + which], cols), cols)
+        copies.append(pltpu.make_async_copy(w_ref.at[:, at], out, sem.at[which]))
+    for one in copies:
+        one.start()
+    for one in copies:
+        one.wait()
+
+
+def fetch(place, weight, cols):
+    depth, groups = weight.shape[0], place.shape[0] - 1
+    return pl.pallas_call(
+        fetch_kernel,
+        in_specs=[pl.BlockSpec(memory_space=pltpu.SMEM), pl.BlockSpec(memory_space=pl.ANY)],
+        out_specs=[VMEM] * groups,
+        out_shape=[jax.ShapeDtypeStruct((depth, cols), weight.dtype)] * groups,
+        scratch_shapes=[pltpu.SemaphoreType.DMA((groups,))],
+        compiler_params=params(FETCH_MIB),
+        cost_estimate=pl.CostEstimate(
+            flops=1, bytes_accessed=4 * depth * cols * groups, transcendentals=1
+        ),
+    )(place, weight)
+
+
+def project_kernel(n, tile, place_ref, *refs):
+    pieces, (heads,) = refs[:n], refs[-1:]
+    groups = (len(refs) - 1 - n) // 2
+    weights, outs = refs[n : n + groups], refs[n + groups : -1]
+    for shift in range(n):
+        head = lax.rem(place_ref[0] - shift + n, n)
+        heads[:, pl.ds(pl.multiple_of(head * HD, HD), HD)] = pieces[shift][...]
+    for weight, out in zip(weights, outs):
+        for at in range(0, out.shape[1], tile):
+            out[:, at : at + tile] = jnp.dot(
+                heads[...], weight[:, at : at + tile], preferred_element_type=jnp.float32
+            ).astype(jnp.bfloat16)
+
+
+def project(place, pieces, weights):
     n, rows = len(pieces), pieces[0].shape[0]
-    depth = weight.shape[0]
-    tiles = cols // tile
-    out = jax.ShapeDtypeStruct((rows, cols), jnp.bfloat16)
+    depth, cols = weights[0].shape
     return pl.pallas_call(
-        functools.partial(project_kernel, n, tiles),
-        grid_spec=pltpu.PrefetchScalarGridSpec(
-            num_scalar_prefetch=1,
-            grid=(2 * tiles,),
-            in_specs=[pl.BlockSpec((rows, HD), lambda i, s: (0, 0)) for _ in range(n)]
-            + [
-                pl.BlockSpec(
-                    (depth, tile),
-                    lambda i, s: (0, jnp.where(i < tiles, s[1], s[2]) * tiles + lax.rem(i, tiles)),
-                )
-            ],
-            out_specs=[
-                pl.BlockSpec((rows, tile), lambda i, s: (0, jnp.minimum(i, tiles - 1))),
-                pl.BlockSpec((rows, tile), lambda i, s: (0, jnp.maximum(i - tiles, 0))),
-            ],
-            scratch_shapes=[pltpu.VMEM((rows, depth), jnp.bfloat16)],
-        ),
-        out_shape=[out, out],
-        compiler_params=params(40),
-        cost_estimate=pl.CostEstimate(
-            flops=4 * rows * depth * cols, bytes_accessed=4 * depth * cols, transcendentals=0
-        ),
-    )(scalars, *pieces, weight)
+        functools.partial(project_kernel, n, 512),
+        in_specs=[pl.BlockSpec(memory_space=pltpu.SMEM)] + [VMEM] * (n + len(weights)),
+        out_specs=[VMEM] * len(weights),
+        out_shape=[jax.ShapeDtypeStruct((rows, cols), jnp.bfloat16)] * len(weights),
+        scratch_shapes=[pltpu.VMEM((rows, depth), jnp.bfloat16)],
+        compiler_params=params(16),
+        cost_estimate=COST,
+    )(place, *pieces, *weights)
 
 
 def heads_form(attn_query, attn_key, attn_value, out_weight):
@@ -198,13 +216,31 @@
             )
         return got
 
-    packed = pl.pallas_call(
+    packed = list(pl.pallas_call(
         functools.partial(pack_kernel, n),
-        in_specs=[smem] + [VMEM] * 3,
+        in_specs=[smem] + [pl.BlockSpec(memory_space=pl.ANY)] * 3,
         out_specs=[VMEM] * n,
         out_shape=[jax.ShapeDtypeStruct((3 * rows, HD), jnp.bfloat16)] * n,
-        compiler_params=params(16),
-    )(me_arr, attn_query, attn_key, attn_value)
+        scratch_shapes=[
+            pltpu.VMEM((3, rows, n * HD), jnp.bfloat16),
+            pltpu.SemaphoreType.DMA((3,)),
+        ],
+        compiler_params=params(56),
+        cost_estimate=COST,
+    )(me_arr, attn_query, attn_key, attn_value))
+    cols = out_weight.shape[1] // tp
+    half = tp // 2
+    y, core = mine // 2, lax.rem(mine, 2)
+    swap = [(i, i ^ 1) for i in range(tp)]
+    f32, bf16 = jnp.float32, jnp.bfloat16
+
+    def wanted(plane):
+        groups = [2 * plane + 1 - core, 2 * plane + core]
+        return jnp.stack([me] + [group * cols for group in groups]).astype(jnp.int32)
+
+    near = [fetch(wanted(lax.rem(y + shift, half)), out_weight, cols) for shift in range(1, half)]
+    last = order[-1]
+    packed[last], near = lax.optimization_barrier((packed[last], near))
     packed = around(packed)
     pairs = n * (n + 1) // 2
     outs = pl.pallas_call(
@@ -213,7 +249,7 @@
         out_specs=[VMEM] * n,
         out_shape=[jax.ShapeDtypeStruct((rows, HD), jnp.bfloat16)] * n,
         scratch_shapes=[pltpu.VMEM((n * rows, HD), jnp.bfloat16)] * 4,
-        compiler_params=params(40),
+        compiler_params=params(24),
         cost_estimate=pl.CostEstimate(
             flops=4 * pairs * rows * rows * HD,
             bytes_accessed=8 * n * rows * HD,
@@ -222,28 +258,24 @@
     )(me_arr, *packed)
     pieces = around(outs)
 
-    cols = out_weight.shape[1] // tp
-    half = tp // 2
-    y, core = mine // 2, lax.rem(mine, 2)
-    swap = [(i, i ^ 1) for i in range(tp)]
-
-    def wanted(plane):
-        return jnp.stack([me, 2 * plane + 1 - core, 2 * plane + core]).astype(jnp.int32)
-
-    f32 = jnp.float32
     crossing = []
-    for shift in range(1, half):
+    for shift, weights in enumerate(near, 1):
         plane = lax.rem(y + shift, half)
-        give, keep = project(wanted(plane), pieces, out_weight, cols, 512)
-        both = (keep.astype(f32) + lax.ppermute(give, "tp", swap).astype(f32)).astype(jnp.bfloat16)
-        crossing.append(
-            lax.ppermute(both, "tp", [(i, (i + 2 * shift) % tp) for i in range(tp)])
-        )
-    give, keep = project(wanted(y), pieces, out_weight, cols, 512)
-    total = keep.astype(f32) + lax.ppermute(give, "tp", swap).astype(f32)
+        perm = [(i, (i + 2 * shift) % tp) for i in range(tp)]
+        give, keep = project(wanted(plane), pieces, weights)
+        both = (keep.astype(f32) + lax.ppermute(give, "tp", swap).astype(f32)).astype(bf16)
+        crossing.append(lax.ppermute(both, "tp", perm))
+        both, *pieces = lax.optimization_barrier((both, *pieces))
+    out_weight, *pieces = lax.optimization_barrier((out_weight, *pieces))
+    give, keep = project(wanted(y), pieces, fetch(wanted(y), out_weight, cols))
+    piece = cols // OWN_PARTS
+    swapped = [
+        lax.ppermute(give[:, at : at + piece], "tp", swap) for at in range(0, cols, piece)
+    ]
+    total = keep.astype(f32) + jnp.concatenate(swapped, axis=1).astype(f32)
     for one in crossing:
         total += one.astype(f32)
-    return total.astype(jnp.bfloat16)
+    return total.astype(bf16)
 
 
 def solution(mesh):

time: 107 us -> 94.5 us (0.88)
  waiting for transfers between devices: 40 us -> 33.5 us
  local copies, waits for them, and re-layouts: 3.12 us -> 0.09 us
  starting transfers between devices: 39.4 us -> 37 us
    ppermute x2 -> x3, waiting for transfers between devices: 23.6 us -> 15.8 us  [the longest x1 13.7 us: heads_form(): crossing.append(lax.ppermute(both, 'tp', perm))]
    unnamed x6, local copies, waits for them, and re-layouts: 3.12 us -> 0.01 us
    ppermute x1, waiting for transfers between devices: 0.01 us -> 2.65 us  [heads_form(): lax.ppermute(give, 'tp', swap).astype(f32)]
    ppermute x14, starting transfers between devices: 37.2 us -> 34.8 us  [around(): lax.ppermute(arrays[shift], 'ctx', [(i, (i + shift) % n) for i in range(n)])]
    ppermute x14, waiting for transfers between devices: 16.5 us -> 15 us  [around(): lax.ppermute(arrays[shift], 'ctx', [(i, (i + shift) % n) for i in range(n)])]
    pallas_call x3 -> x5, Pallas kernels: 17.3 us -> 16.9 us  [the longest x2 8.07 us: fetch(): pl.pallas_call(fetch_kernel, in_specs=[pl.BlockSpec(memory_space=pltpu.SM...]
    ppermute x2 -> x3, starting transfers between devices: 2.14 us -> 2.17 us  [the longest x1 1.6 us: heads_form(): crossing.append(lax.ppermute(both, 'tp', perm))]
  transfers between devices with their start and end apart: 17 -> 18, of which waited for: 10 -> 11; matrix products, arithmetic and copies ran while one was open for 0% -> 0% of each run, Pallas kernels for 8% -> 12%
where the time goes in v2:
time: 94.5 us; the launch traced here: 94.4 us
  starting transfers between devices  37 us (39%)
  waiting for transfers between devices  33.5 us (35%)
  Pallas kernels  21.6 us (23%)
  other arithmetic  2.1 us (2%)
    ppermute x14, starting transfers between devices, around(): lax.ppermute(arrays[shift], 'ctx', [(i, (i + shift) % n) for i in range(n)])  34.8 us
    ppermute x14, waiting for transfers between devices, around(): lax.ppermute(arrays[shift], 'ctx', [(i, (i + shift) % n) for i in range(n)])  15 us
    ppermute x1, waiting for transfers between devices, heads_form(): crossing.append(lax.ppermute(both, 'tp', perm))  13.7 us
    pallas_call x2, Pallas kernels, fetch(): pl.pallas_call(fetch_kernel, in_specs=[pl.BlockSpec(memory_space=pltpu.SM...  8.07 us
    pallas_call x2, Pallas kernels, project(): pl.pallas_call(functools.partial(project_kernel, n, 512), in_specs=[pl.Bl...  6.15 us
    pallas_call x1, Pallas kernels, heads_form(): pl.pallas_call(functools.partial(attention_kernel, n), in_specs=[smem] +...  4.66 us
    pallas_call x1, Pallas kernels, heads_form(): pl.pallas_call(functools.partial(pack_kernel, n), in_specs=[smem] + [pl.B...  2.7 us
    ppermute x1, waiting for transfers between devices, heads_form(): lax.ppermute(give, 'tp', swap).astype(f32)  2.65 us
  transfers between devices with their start and end apart: 18, of which 11 were waited for; matrix products, arithmetic and copies ran while one was open for 0% of the time, Pallas kernels for 12%

profile of v2, /device:TPU:0, one launch (start us, length us, event | category | flops | bytes accessed | tf_op | source)
XLA Modules:
  0.0 94.4 jit_solution(3483356091392755334)
XLA Ops:
  0.0 2.7 %shard_map.46 = (bf16[768,128]{1,0:T(8,128)(2,1)}, bf16[768,128]{1,0:T(8,128)(2,1)}, bf16[768,128]{1,0:T(8,128)(2,1)}, bf16[768,128]{1,0:T(8,128)(2,1)}, bf16[76...) custom-call(s32[1]{0:T(128)} %bitcast.me_ref, ...), custom_call_target="tpu_custom_call" | custom-call | flops 1 | bytes 1 | tf_op jit(solution)/shard_map/pallas_call | solution.py:219
  2.7 3.0 %collective-permute-start = (bf16[768,128]{1,0:T(8,128)(2,1)}, bf16[768,128]{1,0:T(8,128)(2,1)S(1)}, u32[]{:S(2)}, u32[]{:S(2)}) collective-permute-start(bf16[768,128]{1,0:T(8,128)(2,1)} %get-tuple-element.50), channel_id=1, source_target_pairs={{0,4},{4,8},{8,12},{12,16},{16,20},{20,24},{24,28},{28,0},{1,5},{5... | collective-permute-start | bytes 589832 | tf_op jit(solution)/shard_map/ppermute | solution.py:214
  5.7 1.6 %collective-permute-start.1 = (bf16[768,128]{1,0:T(8,128)(2,1)}, bf16[768,128]{1,0:T(8,128)(2,1)S(1)}, u32[]{:S(2)}, u32[]{:S(2)}) collective-permute-start(bf16[768,128]{1,0:T(8,128)(2,1)} %get-tuple-element.51), channel_id=1, source_target_pairs={{0,8},{4,12},{8,16},{12,20},{16,24},{20,28},{24,0},{28,4},{1,9},{5... | collective-permute-start | bytes 589832 | tf_op jit(solution)/shard_map/ppermute | solution.py:214
  7.3 2.6 %collective-permute-start.2 = (bf16[768,128]{1,0:T(8,128)(2,1)}, bf16[768,128]{1,0:T(8,128)(2,1)S(1)}, u32[]{:S(2)}, u32[]{:S(2)}) collective-permute-start(bf16[768,128]{1,0:T(8,128)(2,1)} %get-tuple-element.52), channel_id=1, source_target_pairs={{0,12},{4,16},{8,20},{12,24},{16,28},{20,0},{24,4},{28,8},{1,13},{... | collective-permute-start | bytes 589832 | tf_op jit(solution)/shard_map/ppermute | solution.py:214
  11.1 2.6 %collective-permute-start.4 = (bf16[768,128]{1,0:T(8,128)(2,1)}, bf16[768,128]{1,0:T(8,128)(2,1)S(1)}, u32[]{:S(2)}, u32[]{:S(2)}) collective-permute-start(bf16[768,128]{1,0:T(8,128)(2,1)} %get-tuple-element.54), channel_id=1, source_target_pairs={{0,20},{4,24},{8,28},{12,0},{16,4},{20,8},{24,12},{28,16},{1,21},{... | collective-permute-start | bytes 589832 | tf_op jit(solution)/shard_map/ppermute | solution.py:214
  13.8 4.0 %shard_map.47 = (bf16[1024,2048]{1,0:T(8,128)(2,1)S(1)}, bf16[1024,2048]{1,0:T(8,128)(2,1)S(1)}) custom-call(s32[3]{0:T(128)S(1)} %pad_add_fusion.1.place_ref, bf16[1024,8192]{1,0:T(8,128)(2,1)} %w_ref.2), custom_call_target="tpu_custom_call" | custom-call | flops 1 | bytes 16777216 | tf_op jit(solution)/shard_map/pallas_call | solution.py:160
  17.8 1.4 %collective-permute-start.5 = (bf16[768,128]{1,0:T(8,128)(2,1)S(1)}, bf16[768,128]{1,0:T(8,128)(2,1)S(1)}, u32[]{:S(2)}, u32[]{:S(2)}) collective-permute-start(bf16[768,128]{1,0:T(8,128)(2,1)S(1)} %copy-done.2), channel_id=1, source_target_pairs={{0,24},{4,28},{8,0},{12,4},{16,8},{20,12},{24,16},{28,20},{1,25},{... | collective-permute-start | bytes 589832 | tf_op jit(solution)/shard_map/ppermute | solution.py:214
  19.2 1.4 %collective-permute-start.6 = (bf16[768,128]{1,0:T(8,128)(2,1)S(1)}, bf16[768,128]{1,0:T(8,128)(2,1)S(1)}, u32[]{:S(2)}, u32[]{:S(2)}) collective-permute-start(bf16[768,128]{1,0:T(8,128)(2,1)S(1)} %copy-done.1), channel_id=1, source_target_pairs={{0,28},{4,0},{8,4},{12,8},{16,12},{20,16},{24,20},{28,24},{1,29},{... | collective-permute-start | bytes 589832 | tf_op jit(solution)/shard_map/ppermute | solution.py:214
  20.7 10.2 %collective-permute-done.2.refs_3_ = bf16[768,128]{1,0:T(8,128)(2,1)S(1)} collective-permute-done((bf16[768,128]{1,0:T(8,128)(2,1)}, bf16[768,128]{1,0:T(8,128)(2,1)S(1)}, u32[]{:S(2)}, u32[]{:S(2)}) %collective-permute-start.2) | collective-permute-done | bytes 196640 | tf_op jit(solution)/shard_map/ppermute | solution.py:214
  31.2 1.3 %collective-permute-done.6.refs_7_ = bf16[768,128]{1,0:T(8,128)(2,1)S(1)} collective-permute-done((bf16[768,128]{1,0:T(8,128)(2,1)S(1)}, bf16[768,128]{1,0:T(8,128)(2,1)S(1)}, u32[]{:S(2)}, u32[]{:S(2)}) %collective-permute-start.6) | collective-permute-done | bytes 196640 | tf_op jit(solution)/shard_map/ppermute | solution.py:214
  32.5 4.7 %shard_map.48 = (bf16[256,128]{1,0:T(8,128)(2,1)S(1)}, bf16[256,128]{1,0:T(8,128)(2,1)S(1)}, bf16[256,128]{1,0:T(8,128)(2,1)S(1)}, bf16[256,128]{1,0:T(8,128)(2,...) custom-call(s32[1]{0:T(128)} %bitcast.me_ref, ...), custom_call_target="tpu_custom_call" | custom-call | flops 1207959552 | bytes 2097152 | tf_op jit(solution)/shard_map/pallas_call | solution.py:246
  37.1 5.2 %collective-permute-start.7 = (bf16[256,128]{1,0:T(8,128)(2,1)S(1)}, bf16[256,128]{1,0:T(8,128)(2,1)S(1)}, u32[]{:S(2)}, u32[]{:S(2)}) collective-permute-start(bf16[256,128]{1,0:T(8,128)(2,1)S(1)} %get-tuple-element.61), channel_id=1, source_target_pairs={{0,4},{4,8},{8,12},{12,16},{16,20},{20,24},{24,28},{28,0},{1,5},{5... | collective-permute-start | bytes 196616 | tf_op jit(solution)/shard_map/ppermute | solution.py:214
  42.3 8.1 %collective-permute-start.8 = (bf16[256,128]{1,0:T(8,128)(2,1)S(1)}, bf16[256,128]{1,0:T(8,128)(2,1)S(1)}, u32[]{:S(2)}, u32[]{:S(2)}) collective-permute-start(bf16[256,128]{1,0:T(8,128)(2,1)S(1)} %get-tuple-element.62), channel_id=1, source_target_pairs={{0,8},{4,12},{8,16},{12,20},{16,24},{20,28},{24,0},{28,4},{1,9},{5... | collective-permute-start | bytes 196616 | tf_op jit(solution)/shard_map/ppermute | solution.py:214
  50.4 2.1 %collective-permute-start.10 = (bf16[256,128]{1,0:T(8,128)(2,1)S(1)}, bf16[256,128]{1,0:T(8,128)(2,1)S(1)}, u32[]{:S(2)}, u32[]{:S(2)}) collective-permute-start(bf16[256,128]{1,0:T(8,128)(2,1)S(1)} %get-tuple-element.64), channel_id=1, source_target_pairs={{0,16},{4,20},{8,24},{12,28},{16,0},{20,4},{24,8},{28,12},{1,17},{... | collective-permute-start | bytes 196616 | tf_op jit(solution)/shard_map/ppermute | solution.py:214
  52.5 3.3 %collective-permute-start.11 = (bf16[256,128]{1,0:T(8,128)(2,1)S(1)}, bf16[256,128]{1,0:T(8,128)(2,1)S(1)}, u32[]{:S(2)}, u32[]{:S(2)}) collective-permute-start(bf16[256,128]{1,0:T(8,128)(2,1)S(1)} %get-tuple-element.65), channel_id=1, source_target_pairs={{0,20},{4,24},{8,28},{12,0},{16,4},{20,8},{24,12},{28,16},{1,21},{... | collective-permute-start | bytes 196616 | tf_op jit(solution)/shard_map/ppermute | solution.py:214
  56.6 1.5 %collective-permute-start.13 = (bf16[256,128]{1,0:T(8,128)(2,1)S(1)}, bf16[256,128]{1,0:T(8,128)(2,1)S(1)}, u32[]{:S(2)}, u32[]{:S(2)}) collective-permute-start(bf16[256,128]{1,0:T(8,128)(2,1)S(1)} %get-tuple-element.67), channel_id=1, source_target_pairs={{0,28},{4,0},{8,4},{12,8},{16,12},{20,16},{24,20},{28,24},{1,29},{... | collective-permute-start | bytes 196616 | tf_op jit(solution)/shard_map/ppermute | solution.py:214
  61.3 3.1 %shard_map.49 = (bf16[256,2048]{1,0:T(8,128)(2,1)S(1)}, bf16[256,2048]{1,0:T(8,128)(2,1)S(1)}) custom-call(s32[3]{0:T(128)S(1)} %pad_add_fusion.1.place_ref, bf16[256,128]{1,0:T(8,128)(2,1)S(1)} %get-tuple-element.80.refs_0_, bf16[256,128]{1,0:T(8,128)(2,1)S(1)} %collective-permute-done.7.refs_1_, bf16[256,128]{1,0:T(8,128)(2,1)S(1)} %collective-permute-done.8.refs_2_, ...), custom_call_target="tpu_custom_call" | custom-call | flops 1 | bytes 1 | tf_op jit(solution)/shard_map/pallas_call | solution.py:190
  64.5 2.6 %collective-permute-done.14 = bf16[256,2048]{1,0:T(8,128)(2,1)S(1)} collective-permute-done((bf16[256,2048]{1,0:T(8,128)(2,1)S(1)}, bf16[256,2048]{1,0:T(8,128)(2,1)S(1)}, u32[]{:S(2)}, u32[]{:S(2)}) %collective-permute-start.14) | collective-permute-done | bytes 1048608 | tf_op jit(solution)/shard_map/ppermute | solution.py:266
  67.6 1.6 %collective-permute-start.17 = (bf16[256,2048]{1,0:T(8,128)(2,1)S(1)}, bf16[256,2048]{1,0:T(8,128)(2,1)S(1)}, u32[]{:S(2)}, u32[]{:S(2)}) collective-permute-start(bf16[256,2048]{1,0:T(8,128)(2,1)S(1)} %add_convert_fusion.1), channel_id=1, source_target_pairs={{0,2},{1,3},{2,0},{3,1},{4,6},{5,7},{6,4},{7,5},{8,10},{9,11},{10,... | collective-permute-start | bytes 3145736 | tf_op jit(solution)/shard_map/ppermute | solution.py:267
  69.3 4.0 %shard_map.50 = (bf16[1024,2048]{1,0:T(8,128)(2,1)S(1)}, bf16[1024,2048]{1,0:T(8,128)(2,1)S(1)}) custom-call(s32[3]{0:T(128)S(1)} %pad_add_fusion.place_ref, bf16[1024,8192]{1,0:T(8,128)(2,1)} %w_ref.2), custom_call_target="tpu_custom_call" | custom-call | flops 1 | bytes 16777216 | tf_op jit(solution)/shard_map/pallas_call | solution.py:160
  73.3 3.1 %shard_map.51 = (bf16[256,2048]{1,0:T(8,128)(2,1)S(1)}, bf16[256,2048]{1,0:T(8,128)(2,1)S(1)}) custom-call(s32[3]{0:T(128)S(1)} %pad_add_fusion.place_ref, bf16[256,128]{1,0:T(8,128)(2,1)S(1)} %get-tuple-element.80.refs_0_, bf16[256,128]{1,0:T(8,128)(2,1)S(1)} %collective-permute-done.7.refs_1_, bf16[256,128]{1,0:T(8,128)(2,1)S(1)} %collective-permute-done.8.refs_2_, ...), custom_call_target="tpu_custom_call" | custom-call | flops 1 | bytes 1 | tf_op jit(solution)/shard_map/pallas_call | solution.py:190
  77.1 1.4 %collective-permute-done.15 = bf16[256,1024]{1,0:T(8,128)(2,1)S(1)} collective-permute-done((bf16[256,1024]{1,0:T(8,128)(2,1)S(1)}, bf16[256,1024]{1,0:T(8,128)(2,1)S(1)}, u32[]{:S(2)}, u32[]{:S(2)}) %collective-permute-start.15) | collective-permute-done | bytes 524320 | tf_op jit(solution)/shard_map/ppermute | solution.py:273
  79.2 13.7 %collective-permute-done.17 = bf16[256,2048]{1,0:T(8,128)(2,1)S(1)} collective-permute-done((bf16[256,2048]{1,0:T(8,128)(2,1)S(1)}, bf16[256,2048]{1,0:T(8,128)(2,1)S(1)}, u32[]{:S(2)}, u32[]{:S(2)}) %collective-permute-start.17) | collective-permute-done | bytes 1048608 | tf_op jit(solution)/shard_map/ppermute | solution.py:267
  92.9 1.5 %add_convert_fusion = bf16[256,2048]{1,0:T(8,128)(2,1)} fusion(bf16[256,2048]{1,0:T(8,128)(2,1)S(1)} %collective-permute-done.17, bf16[256,2048]{1,0:T(8,128)(2,1)S(1)} %get-tuple-element.91, bf16[256,1024]{1,0:T(8,128)(2,1)S(1)} %collective-permute-done.16, bf16[256,1024]{1,0:T(8,128)(2,1)S(1)} %collective-permute-done.15), kind=kLoop, calls=%fused_computation | loop fusion | flops 4718592 | bytes 4194304 | tf_op jit(solution)/shard_map/convert_element_type | solution.py:278
  (29 shorter events, 7.6 us)
Async XLA Ops:
  2.7 15.1 %collective-permute-start = (bf16[768,128]{1,0:T(8,128)(2,1)}, bf16[768,128]{1,0:T(8,128)(2,1)S(1)}, u32[]{:S(2)}, u32[]{:S(2)}) collective-permute-start(bf16[768,128]{1,0:T(8,128)(2,1)} %get-tuple-element.50), channel_id=1, source_target_pairs={{0,4},{4,8},{8,12},{12,16},{16,20},{20,24},{24,28},{28,0},{1,5},{5... | collective-permute-start | bytes 589832 | tf_op jit(solution)/shard_map/ppermute | solution.py:214
  5.7 13.5 %collective-permute-start.1 = (bf16[768,128]{1,0:T(8,128)(2,1)}, bf16[768,128]{1,0:T(8,128)(2,1)S(1)}, u32[]{:S(2)}, u32[]{:S(2)}) collective-permute-start(bf16[768,128]{1,0:T(8,128)(2,1)} %get-tuple-element.51), channel_id=1, source_target_pairs={{0,8},{4,12},{8,16},{12,20},{16,24},{20,28},{24,0},{28,4},{1,9},{5... | collective-permute-start | bytes 589832 | tf_op jit(solution)/shard_map/ppermute | solution.py:214
  7.3 23.6 %collective-permute-start.2 = (bf16[768,128]{1,0:T(8,128)(2,1)}, bf16[768,128]{1,0:T(8,128)(2,1)S(1)}, u32[]{:S(2)}, u32[]{:S(2)}) collective-permute-start(bf16[768,128]{1,0:T(8,128)(2,1)} %get-tuple-element.52), channel_id=1, source_target_pairs={{0,12},{4,16},{8,20},{12,24},{16,28},{20,0},{24,4},{28,8},{1,13},{... | collective-permute-start | bytes 589832 | tf_op jit(solution)/shard_map/ppermute | solution.py:214
  9.8 21.3 %collective-permute-start.3 = (bf16[768,128]{1,0:T(8,128)(2,1)}, bf16[768,128]{1,0:T(8,128)(2,1)S(1)}, u32[]{:S(2)}, u32[]{:S(2)}) collective-permute-start(bf16[768,128]{1,0:T(8,128)(2,1)} %get-tuple-element.53), channel_id=1, source_target_pairs={{0,16},{4,20},{8,24},{12,28},{16,0},{20,4},{24,8},{28,12},{1,17},{... | collective-permute-start | bytes 589832 | tf_op jit(solution)/shard_map/ppermute | solution.py:214
  11.1 20.1 %collective-permute-start.4 = (bf16[768,128]{1,0:T(8,128)(2,1)}, bf16[768,128]{1,0:T(8,128)(2,1)S(1)}, u32[]{:S(2)}, u32[]{:S(2)}) collective-permute-start(bf16[768,128]{1,0:T(8,128)(2,1)} %get-tuple-element.54), channel_id=1, source_target_pairs={{0,20},{4,24},{8,28},{12,0},{16,4},{20,8},{24,12},{28,16},{1,21},{... | collective-permute-start | bytes 589832 | tf_op jit(solution)/shard_map/ppermute | solution.py:214
  13.8 4.1 %copy-start.2 = (bf16[768,128]{1,0:T(8,128)(2,1)S(1)}, bf16[768,128]{1,0:T(8,128)(2,1)}, u32[]{:S(2)}) copy-start(bf16[768,128]{1,0:T(8,128)(2,1)} %get-tuple-element.55) | copy-start | bytes 589828
  13.8 5.5 %copy-start.1 = (bf16[768,128]{1,0:T(8,128)(2,1)S(1)}, bf16[768,128]{1,0:T(8,128)(2,1)}, u32[]{:S(2)}) copy-start(bf16[768,128]{1,0:T(8,128)(2,1)} %get-tuple-element.59) | copy-start | bytes 589828
  13.8 18.7 %copy-start = (bf16[768,128]{1,0:T(8,128)(2,1)S(1)}, bf16[768,128]{1,0:T(8,128)(2,1)}, u32[]{:S(2)}) copy-start(bf16[768,128]{1,0:T(8,128)(2,1)} %get-tuple-element.49.refs_0_) | copy-start | bytes 589828
  17.8 13.3 %collective-permute-start.5 = (bf16[768,128]{1,0:T(8,128)(2,1)S(1)}, bf16[768,128]{1,0:T(8,128)(2,1)S(1)}, u32[]{:S(2)}, u32[]{:S(2)}) collective-permute-start(bf16[768,128]{1,0:T(8,128)(2,1)S(1)} %copy-done.2), channel_id=1, source_target_pairs={{0,24},{4,28},{8,0},{12,4},{16,8},{20,12},{24,16},{28,20},{1,25},{... | collective-permute-start | bytes 589832 | tf_op jit(solution)/shard_map/ppermute | solution.py:214
  19.2 13.2 %collective-permute-start.6 = (bf16[768,128]{1,0:T(8,128)(2,1)S(1)}, bf16[768,128]{1,0:T(8,128)(2,1)S(1)}, u32[]{:S(2)}, u32[]{:S(2)}) collective-permute-start(bf16[768,128]{1,0:T(8,128)(2,1)S(1)} %copy-done.1), channel_id=1, source_target_pairs={{0,28},{4,0},{8,4},{12,8},{16,12},{20,16},{24,20},{28,24},{1,29},{... | collective-permute-start | bytes 589832 | tf_op jit(solution)/shard_map/ppermute | solution.py:214
  37.1 18.7 %collective-permute-start.7 = (bf16[256,128]{1,0:T(8,128)(2,1)S(1)}, bf16[256,128]{1,0:T(8,128)(2,1)S(1)}, u32[]{:S(2)}, u32[]{:S(2)}) collective-permute-start(bf16[256,128]{1,0:T(8,128)(2,1)S(1)} %get-tuple-element.61), channel_id=1, source_target_pairs={{0,4},{4,8},{8,12},{12,16},{16,20},{20,24},{24,28},{28,0},{1,5},{5... | collective-permute-start | bytes 196616 | tf_op jit(solution)/shard_map/ppermute | solution.py:214
  42.3 14.3 %collective-permute-start.8 = (bf16[256,128]{1,0:T(8,128)(2,1)S(1)}, bf16[256,128]{1,0:T(8,128)(2,1)S(1)}, u32[]{:S(2)}, u32[]{:S(2)}) collective-permute-start(bf16[256,128]{1,0:T(8,128)(2,1)S(1)} %get-tuple-element.62), channel_id=1, source_target_pairs={{0,8},{4,12},{8,16},{12,20},{16,24},{20,28},{24,0},{28,4},{1,9},{5... | collective-permute-start | bytes 196616 | tf_op jit(solution)/shard_map/ppermute | solution.py:214
  50.4 8.1 %collective-permute-start.9 = (bf16[256,128]{1,0:T(8,128)(2,1)S(1)}, bf16[256,128]{1,0:T(8,128)(2,1)S(1)}, u32[]{:S(2)}, u32[]{:S(2)}) collective-permute-start(bf16[256,128]{1,0:T(8,128)(2,1)S(1)} %get-tuple-element.63), channel_id=1, source_target_pairs={{0,12},{4,16},{8,20},{12,24},{16,28},{20,0},{24,4},{28,8},{1,13},{... | collective-permute-start | bytes 196616 | tf_op jit(solution)/shard_map/ppermute | solution.py:214
  50.4 9.3 %collective-permute-start.10 = (bf16[256,128]{1,0:T(8,128)(2,1)S(1)}, bf16[256,128]{1,0:T(8,128)(2,1)S(1)}, u32[]{:S(2)}, u32[]{:S(2)}) collective-permute-start(bf16[256,128]{1,0:T(8,128)(2,1)S(1)} %get-tuple-element.64), channel_id=1, source_target_pairs={{0,16},{4,20},{8,24},{12,28},{16,0},{20,4},{24,8},{28,12},{1,17},{... | collective-permute-start | bytes 196616 | tf_op jit(solution)/shard_map/ppermute | solution.py:214
  52.5 7.9 %collective-permute-start.11 = (bf16[256,128]{1,0:T(8,128)(2,1)S(1)}, bf16[256,128]{1,0:T(8,128)(2,1)S(1)}, u32[]{:S(2)}, u32[]{:S(2)}) collective-permute-start(bf16[256,128]{1,0:T(8,128)(2,1)S(1)} %get-tuple-element.65), channel_id=1, source_target_pairs={{0,20},{4,24},{8,28},{12,0},{16,4},{20,8},{24,12},{28,16},{1,21},{... | collective-permute-start | bytes 196616 | tf_op jit(solution)/shard_map/ppermute | solution.py:214
  55.8 5.5 %collective-permute-start.12 = (bf16[256,128]{1,0:T(8,128)(2,1)S(1)}, bf16[256,128]{1,0:T(8,128)(2,1)S(1)}, u32[]{:S(2)}, u32[]{:S(2)}) collective-permute-start(bf16[256,128]{1,0:T(8,128)(2,1)S(1)} %get-tuple-element.66), channel_id=1, source_target_pairs={{0,24},{4,28},{8,0},{12,4},{16,8},{20,12},{24,16},{28,20},{1,25},{... | collective-permute-start | bytes 196616 | tf_op jit(solution)/shard_map/ppermute | solution.py:214
  56.6 4.7 %collective-permute-start.13 = (bf16[256,128]{1,0:T(8,128)(2,1)S(1)}, bf16[256,128]{1,0:T(8,128)(2,1)S(1)}, u32[]{:S(2)}, u32[]{:S(2)}) collective-permute-start(bf16[256,128]{1,0:T(8,128)(2,1)S(1)} %get-tuple-element.67), channel_id=1, source_target_pairs={{0,28},{4,0},{8,4},{12,8},{16,12},{20,16},{24,20},{28,24},{1,29},{... | collective-permute-start | bytes 196616 | tf_op jit(solution)/shard_map/ppermute | solution.py:214
  64.4 2.7 %collective-permute-start.14 = (bf16[256,2048]{1,0:T(8,128)(2,1)S(1)}, bf16[256,2048]{1,0:T(8,128)(2,1)S(1)}, u32[]{:S(2)}, u32[]{:S(2)}) collective-permute-start(bf16[256,2048]{1,0:T(8,128)(2,1)S(1)} %get-tuple-element.71), channel_id=1, source_target_pairs={{0,1},{1,0},{2,3},{3,2},{4,5},{5,4},{6,7},{7,6},{8,9},{9,8},{10,11... | collective-permute-start | bytes 3145736 | tf_op jit(solution)/shard_map/ppermute | solution.py:266
  67.6 25.3 %collective-permute-start.17 = (bf16[256,2048]{1,0:T(8,128)(2,1)S(1)}, bf16[256,2048]{1,0:T(8,128)(2,1)S(1)}, u32[]{:S(2)}, u32[]{:S(2)}) collective-permute-start(bf16[256,2048]{1,0:T(8,128)(2,1)S(1)} %add_convert_fusion.1), channel_id=1, source_target_pairs={{0,2},{1,3},{2,0},{3,1},{4,6},{5,7},{6,4},{7,5},{8,10},{9,11},{10,... | collective-permute-start | bytes 3145736 | tf_op jit(solution)/shard_map/ppermute | solution.py:267
  76.5 2.0 %collective-permute-start.15 = (bf16[256,1024]{1,0:T(8,128)(2,1)S(1)}, bf16[256,1024]{1,0:T(8,128)(2,1)S(1)}, u32[]{:S(2)}, u32[]{:S(2)}) collective-permute-start(bf16[256,1024]{1,0:T(8,128)(2,1)S(1)} %get-tuple-element.93), channel_id=1, source_target_pairs={{0,1},{1,0},{2,3},{3,2},{4,5},{5,4},{6,7},{7,6},{8,9},{9,8},{10,11... | collective-permute-start | bytes 1572872 | tf_op jit(solution)/shard_map/ppermute | solution.py:273
  76.6 2.6 %collective-permute-start.16 = (bf16[256,1024]{1,0:T(8,128)(2,1)S(1)}, bf16[256,1024]{1,0:T(8,128)(2,1)S(1)}, u32[]{:S(2)}, u32[]{:S(2)}) collective-permute-start(bf16[256,1024]{1,0:T(8,128)(2,1)S(1)} %get-tuple-element.94), channel_id=1, source_target_pairs={{0,1},{1,0},{2,3},{3,2},{4,5},{5,4},{6,7},{7,6},{8,9},{9,8},{10,11... | collective-permute-start | bytes 1572872 | tf_op jit(solution)/shard_map/ppermute | solution.py:273

commit v3 on v0

v3 whole, which is shorter than its diff:
```python
import functools

import jax
import jax.numpy as jnp
from jax import lax
from jax.experimental import pallas as pl
from jax.experimental.pallas import tpu as pltpu
from jax.sharding import PartitionSpec as P

HD = 128
MIB = 1 << 20
OWN_PARTS = 2
STAT_ROWS = 16
LOG2E = 1.4426950408889634
FETCH_MIB = 40
COST = pl.CostEstimate(flops=1, bytes_accessed=1, transcendentals=1)
VMEM = pl.BlockSpec(memory_space=pltpu.VMEM)


def params(mib):
    return pltpu.CompilerParams(vmem_limit_bytes=mib * MIB)


def attend(queries, keys, values, query_pos):
    rows = queries.shape[0]
    local_heads = queries.shape[1] // HD
    scale = HD ** (-0.5)
    shaped_q = queries.reshape(rows, local_heads, HD)
    latest = jnp.max(query_pos)
    initial = (
        jnp.full((local_heads, rows), -1e30, jnp.float32),
        jnp.zeros((local_heads, rows), jnp.float32),
        jnp.zeros((local_heads, rows, HD), jnp.float32),
    )
    piece_keys = lax.all_gather(keys, "ctx", axis=0, tiled=True)
    piece_values = lax.all_gather(values, "ctx", axis=0, tiled=True)
    count_rows = piece_keys.shape[0]
    span_rows = 2 * rows

    def one_block(block, state):
        offset = block * span_rows
        block_keys = lax.dynamic_slice_in_dim(piece_keys, offset, span_rows, 0).reshape(
            span_rows, local_heads, HD
        )
        block_values = lax.dynamic_slice_in_dim(piece_values, offset, span_rows, 0).reshape(
            span_rows, local_heads, HD
        )
        key_pos = offset + jnp.arange(span_rows, dtype=jnp.int32)

        def compute(inner):
            maxes, totals, accum = inner
            scores = (
                jnp.einsum("qhd,khd->hqk", shaped_q, block_keys, preferred_element_type=jnp.float32)
                * scale
            )
            allowed = key_pos[None, None, :] <= query_pos[None, :, None]
            new_max = jnp.maximum(maxes, jnp.max(jnp.where(allowed, scores, -1e30), axis=-1))
            factor = jnp.exp(maxes - new_max)
            weights = jnp.where(allowed, jnp.exp(scores - new_max[..., None]), 0.0)
            totals = totals * factor + jnp.sum(weights, axis=-1)
            accum = accum * factor[..., None] + jnp.einsum(
                "hqk,khd->hqd",
                weights.astype(jnp.bfloat16),
                block_values,
                preferred_element_type=jnp.float32,
            )
            return (new_max, totals, accum)

        return lax.cond(jnp.min(key_pos) <= latest, compute, lambda inner: inner, state)

    maxes, totals, accum = lax.fori_loop(0, count_rows // span_rows, one_block, initial)
    result = accum / totals[..., None]
    return jnp.transpose(result, (1, 0, 2)).reshape(rows, local_heads * HD).astype(jnp.bfloat16)


def gather_form(attn_query, attn_key, attn_value, out_weight):
    rows = attn_query.shape[0]
    query_pos = lax.axis_index("ctx") * rows + jnp.arange(rows, dtype=jnp.int32)
    heads = attend(attn_query, attn_key, attn_value, query_pos)
    partial_value = jnp.dot(heads, out_weight, preferred_element_type=jnp.float32)
    return lax.psum_scatter(
        partial_value.astype(jnp.bfloat16), "tp", scatter_dimension=1, tiled=True
    )


def pack_kernel(half, me_ref, q_ref, k_ref, v_ref, *refs):
    inner, cross, (held, sem) = refs[:half], refs[half : 2 * half], refs[2 * half :]
    upper, place = me_ref[0] // half, lax.rem(me_ref[0], half)
    copies = [
        pltpu.make_async_copy(ref, held.at[part], sem.at[part])
        for part, ref in enumerate((q_ref, k_ref, v_ref))
    ]
    for one in copies:
        one.start()
    for part, one in enumerate(copies):
        one.wait()
        for shift in range(half):
            goal = place ^ shift
            cols = pl.ds(pl.multiple_of(goal * 2 * HD, 2 * HD), 2 * HD)
            inner[shift][part] = held[part, :, cols]
    for shift in range(half):
        goal = place ^ shift
        even = pl.ds(pl.multiple_of(goal * 2 * HD, HD), HD)
        odd = pl.ds(pl.multiple_of(goal * 2 * HD + HD, HD), HD)

        @pl.when(upper == 0)
        def _():
            cross[shift][0] = held[1, :, odd]
            cross[shift][1] = held[2, :, odd]

        @pl.when(upper == 1)
        def _():
            cross[shift][0] = held[0, :, even]
            cross[shift][1] = held[0, :, even]


def split3(value):
    high = value.astype(jnp.bfloat16)
    value = value - high.astype(jnp.float32)
    middle = value.astype(jnp.bfloat16)
    return high, middle, (value - middle.astype(jnp.float32)).astype(jnp.bfloat16)


def gather(half, place, rows, pieces, part, out, cols=slice(None)):
    for shift in range(half):
        source = place ^ shift
        at = pl.ds(pl.multiple_of(source * rows, rows), rows)
        out[at, :] = pieces[shift][part, :, cols]


def scores(query, keys):
    dims = (((1,), (1,)), ((), ()))
    return lax.dot_general(query, keys, dims, preferred_element_type=jnp.float32)


def weigh(raw, top, values):
    weights = jnp.exp2((raw - top) * (HD ** (-0.5) * LOG2E))
    total = jnp.sum(weights, axis=1, keepdims=True)
    acc = jnp.dot(weights.astype(jnp.bfloat16), values, preferred_element_type=jnp.float32)
    return total, acc


def log_sum(top, total):
    return top * (HD ** (-0.5) * LOG2E) + jnp.log2(total)


def inner_kernel(half, me_ref, *refs):
    inner, (o_ref, table_ref), (q_all, k_all, v_all) = refs[:half], refs[half:-3], refs[-3:]
    rows = inner[0].shape[1]
    place = lax.rem(me_ref[0], half)
    for part, out in enumerate((q_all, k_all, v_all)):
        gather(half, place, rows, inner, part, out)
    diag = lax.broadcasted_iota(jnp.int32, (rows, rows), 1) <= lax.broadcasted_iota(
        jnp.int32, (rows, rows), 0
    )
    lane = lax.broadcasted_iota(jnp.int32, (rows, HD), 1)
    table = jnp.zeros((rows, HD), jnp.float32)
    for block in reversed(range(half)):
        lo, hi = block * rows, (block + 1) * rows
        for head in range(2):
            at = slice(head * HD, (head + 1) * HD)
            query = q_all[lo:hi, at]
            last = jnp.where(diag, scores(query, k_all[lo:hi, at]), -1e30)
            top = jnp.max(last, axis=1, keepdims=True)
            if block:
                early = scores(query, k_all[0:lo, at])
                top = jnp.maximum(top, jnp.max(early, axis=1, keepdims=True))
            total, acc = weigh(last, top, v_all[lo:hi, at])
            if block:
                total_early, acc_early = weigh(early, top, v_all[0:lo, at])
                total, acc = total + total_early, acc + acc_early
            o_ref[lo:hi, at] = acc / total
            table = jnp.where(lane == head * half + block, log_sum(top, total), table)
    table_ref[...] = table


def cross_kernel(half, me_ref, *refs):
    inner, cross, (o_ref, table_ref) = refs[:half], refs[half : 2 * half], refs[2 * half : 2 * half + 2]
    back, over = refs[2 * half + 2 : 3 * half + 2], refs[3 * half + 2 : 4 * half + 2]
    q_x, k_x, v_x, o_all, o_x, stats = refs[4 * half + 2 :]
    rows = inner[0].shape[1]
    upper, place = me_ref[0] // half, lax.rem(me_ref[0], half)

    @pl.when(upper == 0)
    def _():
        gather(half, place, rows, cross, 0, q_x)
        gather(half, place, rows, inner, 1, k_x, slice(0, HD))
        gather(half, place, rows, inner, 2, v_x, slice(0, HD))

    @pl.when(upper == 1)
    def _():
        gather(half, place, rows, inner, 0, q_x, slice(HD, 2 * HD))
        gather(half, place, rows, cross, 0, k_x)
        gather(half, place, rows, cross, 1, v_x)

    lane = lax.broadcasted_iota(jnp.int32, (rows, HD), 1)
    logs = table_ref[...]
    table = logs
    for block in range(half):
        lo, hi = block * rows, (block + 1) * rows
        raw = scores(q_x[lo:hi, :], k_x[...])
        top = jnp.max(raw, axis=1, keepdims=True)
        total, acc = weigh(raw, top, v_x[...])
        result = acc / total
        o_x[lo:hi, :] = result.astype(jnp.bfloat16)
        log_x = log_sum(top, total)
        table = jnp.where(lane == half + block, log_x, table)
        gap = jnp.where(upper == 1, log_x - logs[:, half + block : half + block + 1], -1e30)
        near, far = 1.0 / (1.0 + jnp.exp2(gap)), 1.0 / (1.0 + jnp.exp2(-gap))
        o_all[lo:hi, :HD] = o_ref[lo:hi, :HD].astype(jnp.bfloat16)
        o_all[lo:hi, HD:] = (near * o_ref[lo:hi, HD:] + far * result).astype(jnp.bfloat16)
    turned = jnp.transpose(table)
    for i, part in enumerate(split3(turned[0 : 2 * half, :])):
        stats[i] = part.astype(jnp.float32)
    empty = jnp.zeros((STAT_ROWS - 3, rows), jnp.float32)
    for shift in range(half):
        goal = place ^ shift
        at = pl.ds(pl.multiple_of(goal * rows, rows), rows)
        for out, source, first in ((back[shift], o_all, 0), (over[shift], o_x, half)):
            out[0:rows, :] = source[at, :]
            lines = [stats[i, pl.ds(first + goal, 1), :] for i in range(3)]
            block = jnp.concatenate(lines + [empty], axis=0).astype(jnp.bfloat16)
            wide = out.shape[1]
            for step in range(rows // wide):
                here = slice(rows + step * STAT_ROWS, rows + (step + 1) * STAT_ROWS)
                out[here, :] = block[:, step * wide : (step + 1) * wide]


def assemble(half, me_ref, back, over, heads):
    rows = heads.shape[0]
    upper, place = me_ref[0] // half, lax.rem(me_ref[0], half)

    def read_log(piece):
        wide = piece.shape[1]
        blocks = [
            piece[rows + i * STAT_ROWS : rows + (i + 1) * STAT_ROWS, :] for i in range(rows // wide)
        ]
        block = jnp.concatenate([one.astype(jnp.float32) for one in blocks], axis=1)
        return block[0:1, :] + block[1:2, :] + block[2:3, :]

    gaps = []
    for shift in range(half):
        gap = read_log(over[shift]) - read_log(back[shift])
        gaps.append(jnp.where(upper == 1, gap, -1e30))
    table = jnp.concatenate(gaps + [jnp.zeros((HD - half, rows), jnp.float32)], axis=0)
    table = jnp.transpose(table)
    for shift in range(half):
        source = place ^ shift
        even = pl.ds(pl.multiple_of(source * 2 * HD, HD), HD)
        odd = pl.ds(pl.multiple_of(source * 2 * HD + HD, HD), HD)
        gap = table[:, shift : shift + 1]
        near = 1.0 / (1.0 + jnp.exp2(gap))
        far = 1.0 / (1.0 + jnp.exp2(-gap))
        merged = near * back[shift][0:rows, 0:HD].astype(jnp.float32)
        merged += far * over[shift][0:rows, :].astype(jnp.float32)
        heads[:, even] = merged.astype(jnp.bfloat16)
        heads[:, odd] = back[shift][0:rows, HD:]


def multiply(heads, weight, out, tile):
    for at in range(0, out.shape[1], tile):
        out[:, at : at + tile] = jnp.dot(
            heads[...], weight[:, at : at + tile], preferred_element_type=jnp.float32
        ).astype(jnp.bfloat16)


def first_kernel(half, tile, me_ref, *refs):
    back, over, (weight, heads, out) = refs[:half], refs[half : 2 * half], refs[2 * half :]
    assemble(half, me_ref, back, over, heads)
    multiply(heads, weight, out, tile)


def later_kernel(tile, heads, *refs):
    count = len(refs) // 2
    for weight, out in zip(refs[:count], refs[count:]):
        multiply(heads, weight, out, tile)


def project(heads, weights):
    out = jax.ShapeDtypeStruct((heads.shape[0], weights[0].shape[1]), jnp.bfloat16)
    return pl.pallas_call(
        functools.partial(later_kernel, 512),
        in_specs=[VMEM] * (1 + len(weights)),
        out_specs=[VMEM] * len(weights),
        out_shape=[out] * len(weights),
        compiler_params=params(16),
        cost_estimate=COST,
    )(heads, *weights)


def fetch_kernel(place_ref, w_ref, *refs):
    outs, sem = refs[:-1], refs[-1]
    cols = outs[0].shape[1]
    copies = []
    for which, out in enumerate(outs):
        at = pl.ds(pl.multiple_of(place_ref[1 + which], cols), cols)
        copies.append(pltpu.make_async_copy(w_ref.at[:, at], out, sem.at[which]))
    for one in copies:
        one.start()
    for one in copies:
        one.wait()


def fetch(place, weight, cols):
    depth, groups = weight.shape[0], place.shape[0] - 1
    return pl.pallas_call(
        fetch_kernel,
        in_specs=[pl.BlockSpec(memory_space=pltpu.SMEM), pl.BlockSpec(memory_space=pl.ANY)],
        out_specs=[VMEM] * groups,
        out_shape=[jax.ShapeDtypeStruct((depth, cols), weight.dtype)] * groups,
        scratch_shapes=[pltpu.SemaphoreType.DMA((groups,))],
        compiler_params=params(FETCH_MIB),
        cost_estimate=pl.CostEstimate(
            flops=1, bytes_accessed=4 * depth * cols * groups, transcendentals=1
        ),
    )(place, weight)


def heads_form(attn_query, attn_key, attn_value, out_weight):
    n, tp = lax.axis_size("ctx"), lax.axis_size("tp")
    half = n // 2
    rows = attn_query.shape[0]
    bf16, f32 = jnp.bfloat16, jnp.float32
    me, mine = lax.axis_index("ctx"), lax.axis_index("tp")
    place = me.astype(jnp.int32).reshape(1)
    smem = pl.BlockSpec(memory_space=pltpu.SMEM)

    def within(shift):
        return [(i, i ^ shift) for i in range(n)]

    def between(shift, lower, upper):
        up = [(i, half + (i ^ shift)) for i in range(half)]
        down = [(half + i, i ^ shift) for i in range(half)]
        return up * lower + down * upper

    inner_shape = jax.ShapeDtypeStruct((3, rows, 2 * HD), bf16)
    cross_shape = jax.ShapeDtypeStruct((2, rows, HD), bf16)
    packed = pl.pallas_call(
        functools.partial(pack_kernel, half),
        in_specs=[smem] + [pl.BlockSpec(memory_space=pl.ANY)] * 3,
        out_specs=[VMEM] * n,
        out_shape=[inner_shape] * half + [cross_shape] * half,
        scratch_shapes=[
            pltpu.VMEM((3, rows, n * HD), bf16),
            pltpu.SemaphoreType.DMA((3,)),
        ],
        compiler_params=params(56),
        cost_estimate=COST,
    )(place, attn_query, attn_key, attn_value)
    inner, cross = list(packed[:half]), list(packed[half:])

    cols = out_weight.shape[1] // tp
    planes = tp // 2
    y, core = mine // 2, lax.rem(mine, 2)
    swap = [(i, i ^ 1) for i in range(tp)]

    def wanted(plane):
        groups = [2 * plane + 1 - core, 2 * plane + core]
        return jnp.stack([me] + [group * cols for group in groups]).astype(jnp.int32)

    near = [
        fetch(wanted(lax.rem(y + shift, planes)), out_weight, cols) for shift in range(1, planes)
    ]
    for shift in range(1, half):
        inner[shift] = lax.ppermute(inner[shift], "ctx", within(shift))
    cross = [
        lax.ppermute(piece, "ctx", between(shift, 1, 1)) for shift, piece in enumerate(cross)
    ]

    inner[1], *rest = lax.optimization_barrier((inner[1], *inner[2:], near))
    inner[2:], near = rest[:-1], rest[-1]
    back_shape = jax.ShapeDtypeStruct((rows + STAT_ROWS * (rows // (2 * HD)), 2 * HD), bf16)
    over_shape = jax.ShapeDtypeStruct((rows + STAT_ROWS * (rows // HD), HD), bf16)
    big, small = pltpu.VMEM((half * rows, 2 * HD), bf16), pltpu.VMEM((half * rows, HD), bf16)
    results = pl.pallas_call(
        functools.partial(inner_kernel, half),
        in_specs=[smem] + [VMEM] * half,
        out_specs=[VMEM] * 2,
        out_shape=[
            jax.ShapeDtypeStruct((half * rows, 2 * HD), f32),
            jax.ShapeDtypeStruct((rows, HD), f32),
        ],
        scratch_shapes=[big] * 3,
        compiler_params=params(24),
        cost_estimate=COST,
    )(place, *inner)
    outs = pl.pallas_call(
        functools.partial(cross_kernel, half),
        in_specs=[smem] + [VMEM] * (n + 2),
        out_specs=[VMEM] * n,
        out_shape=[back_shape] * half + [over_shape] * half,
        scratch_shapes=[small] * 3 + [big, small, pltpu.VMEM((3, n, rows), f32)],
        compiler_params=params(24),
        cost_estimate=COST,
    )(place, *inner, *cross, *results)
    back, over = list(outs[:half]), list(outs[half:])
    over = [lax.ppermute(piece, "ctx", between(shift, 1, 0)) for shift, piece in enumerate(over)]
    for shift in range(1, half):
        back[shift] = lax.ppermute(back[shift], "ctx", within(shift))

    tied = (back[1], *over, *back[2:])
    back[1], *tied = lax.optimization_barrier(tied)
    over, back[2:] = tied[:half], tied[half:]
    heads, crossing = None, []
    for shift, (w_give, w_keep) in enumerate(near, 1):
        perm = [(i, (i + 2 * shift) % tp) for i in range(tp)]
        if heads is None:
            heads, give = pl.pallas_call(
                functools.partial(first_kernel, half, 512),
                in_specs=[smem] + [VMEM] * (n + 1),
                out_specs=[VMEM] * 2,
                out_shape=[
                    jax.ShapeDtypeStruct((rows, n * HD), bf16),
                    jax.ShapeDtypeStruct((rows, cols), bf16),
                ],
                compiler_params=params(16),
                cost_estimate=COST,
            )(place, *back, *over, w_give)
        else:
            (give,) = project(heads, [w_give])
        (keep,) = project(heads, [w_keep])
        both = (keep.astype(f32) + lax.ppermute(give, "tp", swap).astype(f32)).astype(bf16)
        crossing.append(lax.ppermute(both, "tp", perm))
        both, heads = lax.optimization_barrier((both, heads))
    out_weight, heads = lax.optimization_barrier((out_weight, heads))
    give, keep = project(heads, fetch(wanted(y), out_weight, cols))
    piece = cols // OWN_PARTS
    swapped = [
        lax.ppermute(give[:, at : at + piece], "tp", swap) for at in range(0, cols, piece)
    ]
    total = keep.astype(f32) + jnp.concatenate(swapped, axis=1).astype(f32)
    for one in crossing:
        total += one.astype(f32)
    return total.astype(bf16)


def solution(mesh):
    def per_device(attn_query, attn_key, attn_value, out_weight):
        heads, n, tp = attn_query.shape[1] // HD, mesh.shape["ctx"], mesh.shape["tp"]
        paired = heads == n and n > 2 and n & (n - 1) == 0 and n <= HD and tp % 2 == 0 and tp > 2
        form = heads_form if paired and attn_query.shape[0] % (2 * HD) == 0 else gather_form
        return form(attn_query, attn_key, attn_value, out_weight)

    return jax.shard_map(
        per_device,
        mesh=mesh,
        in_specs=(P("ctx", "tp"), P("ctx", "tp"), P("ctx", "tp"), P("tp", None)),
        out_specs=P("ctx", "tp"),
        check_vma=False,
    )
```

time: 254 us -> 89.5 us (0.35)
  waiting for transfers between devices: 208 us -> 32.2 us
  starting transfers between devices: 0.09 us -> 32.4 us
  Pallas kernels: 0 us -> 21.9 us
  matrix products: 14.7 us -> 0 us
  between operations: 13.1 us -> 0.18 us
  local copies, waits for them, and re-layouts: 7.76 us -> 0.08 us
  loops' own time: 5.29 us -> 0 us
    all_gather x2 -> x0, waiting for transfers between devices: 149 us -> none  [the longest x1 75.3 us: attend(): piece_values = lax.all_gather(values, 'ctx', axis=0, tiled=True)]
    reduce_scatter x1 -> x0, waiting for transfers between devices: 58.9 us -> none  [per_device(): lax.psum_scatter(partial_value.astype(jnp.bfloat16), 'tp', scatter_dimens...]
    ppermute x0 -> x18, starting transfers between devices: none -> 32.4 us  [the longest x4 11.5 us: heads_form(): lax.ppermute(piece, 'ctx', between(shift, 1, 1))]
    ppermute x0 -> x18, waiting for transfers between devices: none -> 32.2 us  [the longest x1 14.4 us: heads_form(): crossing.append(lax.ppermute(both, 'tp', perm))]
    pallas_call x0 -> x8, Pallas kernels: none -> 21.9 us  [the longest x2 8.07 us: fetch(): pl.pallas_call(fetch_kernel, in_specs=[pl.BlockSpec(memory_space=pltpu.SM...]
    dot_general x3 -> x0, matrix products: 14.7 us -> none  [the longest x1 12.1 us: per_device(): jnp.dot(heads, out_weight, preferred_element_type=jnp.float32)]
    unnamed x4 -> x2, local copies, waits for them, and re-layouts: 5.65 us -> 0.01 us
    another operation x5 -> x0, loops' own time: 5.29 us -> none  [the longest x1 5.17 us: attend(): lax.fori_loop(0, count_rows // span_rows, one_block, initial)]
  transfers between devices with their start and end apart: 3 -> 18, of which waited for: 3 -> 10; matrix products, arithmetic and copies ran while one was open for 2% -> 0% of each run, Pallas kernels for 0% -> 16%
where the time goes in v3:
time: 89.5 us; the launch traced here: 88.8 us
  starting transfers between devices  32.4 us (36%)
  waiting for transfers between devices  32.2 us (36%)
  Pallas kernels  21.9 us (24%)
  other arithmetic  2.05 us (2%)
    ppermute x1, waiting for transfers between devices, heads_form(): crossing.append(lax.ppermute(both, 'tp', perm))  14.4 us
    ppermute x4, starting transfers between devices, heads_form(): lax.ppermute(piece, 'ctx', between(shift, 1, 1))  11.5 us
    ppermute x4, starting transfers between devices, heads_form(): lax.ppermute(piece, 'ctx', between(shift, 1, 0))  10.5 us
    ppermute x3, waiting for transfers between devices, heads_form(): inner[shift] = lax.ppermute(inner[shift], 'ctx', within(shift))  8.24 us
    pallas_call x2, Pallas kernels, fetch(): pl.pallas_call(fetch_kernel, in_specs=[pl.BlockSpec(memory_space=pltpu.SM...  8.07 us
    ppermute x3, starting transfers between devices, heads_form(): inner[shift] = lax.ppermute(inner[shift], 'ctx', within(shift))  4.58 us
    ppermute x4, waiting for transfers between devices, heads_form(): lax.ppermute(piece, 'ctx', between(shift, 1, 1))  4.07 us
    pallas_call x2, Pallas kernels, project(): pl.pallas_call(functools.partial(later_kernel, 512), in_specs=[VMEM] * (1...  3.66 us
  transfers between devices with their start and end apart: 18, of which 10 were waited for; matrix products, arithmetic and copies ran while one was open for 0% of the time, Pallas kernels for 16%

profile of v3, /device:TPU:0, one launch (start us, length us, event | category | flops | bytes accessed | tf_op | source)
XLA Modules:
  0.0 88.8 jit_solution(1121905472265407083)
XLA Ops:
  0.0 2.9 %shard_map.46 = (bf16[3,256,256]{2,1,0:T(8,128)(2,1)}, bf16[3,256,256]{2,1,0:T(8,128)(2,1)}, bf16[3,256,256]{2,1,0:T(8,128)(2,1)}, bf16[3,256,256]{2,1,0:T(8,128...) custom-call(s32[1]{0:T(128)} %bitcast.me_ref, ...), custom_call_target="tpu_custom_call" | custom-call | flops 1 | bytes 1 | tf_op jit(solution)/shard_map/pallas_call | solution.py:338
  3.0 3.0 %collective-permute-start = (bf16[3,256,256]{2,1,0:T(8,128)(2,1)}, bf16[3,256,256]{2,1,0:T(8,128)(2,1)S(1)}, u32[]{:S(2)}, u32[]{:S(2)}) collective-permute-start(bf16[3,256,256]{2,1,0:T(8,128)(2,1)} %get-tuple-element.47), channel_id=1, source_target_pairs={{0,4},{4,0},{8,12},{12,8},{16,20},{20,16},{24,28},{28,24},{1,5},{5... | collective-permute-start | bytes 1179656 | tf_op jit(solution)/shard_map/ppermute | solution.py:365
  6.0 1.6 %collective-permute-start.1 = (bf16[3,256,256]{2,1,0:T(8,128)(2,1)}, bf16[3,256,256]{2,1,0:T(8,128)(2,1)S(1)}, u32[]{:S(2)}, u32[]{:S(2)}) collective-permute-start(bf16[3,256,256]{2,1,0:T(8,128)(2,1)} %get-tuple-element.48), channel_id=1, source_target_pairs={{0,8},{4,12},{8,0},{12,4},{16,24},{20,28},{24,16},{28,20},{1,9},{5... | collective-permute-start | bytes 1179656 | tf_op jit(solution)/shard_map/ppermute | solution.py:365
  7.5 2.9 %collective-permute-start.3 = (bf16[2,256,128]{2,1,0:T(8,128)(2,1)}, bf16[2,256,128]{2,1,0:T(8,128)(2,1)S(1)}, u32[]{:S(2)}, u32[]{:S(2)}) collective-permute-start(bf16[2,256,128]{2,1,0:T(8,128)(2,1)} %get-tuple-element.55), channel_id=1, source_target_pairs={{0,16},{4,20},{8,24},{12,28},{16,0},{20,4},{24,8},{28,12},{1,17},{... | collective-permute-start | bytes 393224 | tf_op jit(solution)/shard_map/ppermute | solution.py:367
  11.8 6.3 %collective-permute-done.refs_1_ = bf16[3,256,256]{2,1,0:T(8,128)(2,1)S(1)} collective-permute-done((bf16[3,256,256]{2,1,0:T(8,128)(2,1)}, bf16[3,256,256]{2,1,0:T(8,128)(2,1)S(1)}, u32[]{:S(2)}, u32[]{:S(2)}) %collective-permute-start) | collective-permute-done | bytes 393248 | tf_op jit(solution)/shard_map/ppermute | solution.py:365
  18.1 3.8 %collective-permute-start.5 = (bf16[2,256,128]{2,1,0:T(8,128)(2,1)}, bf16[2,256,128]{2,1,0:T(8,128)(2,1)S(1)}, u32[]{:S(2)}, u32[]{:S(2)}) collective-permute-start(bf16[2,256,128]{2,1,0:T(8,128)(2,1)} %get-tuple-element.57), channel_id=1, source_target_pairs={{0,24},{4,28},{8,16},{12,20},{16,8},{20,12},{24,0},{28,4},{1,25},{... | collective-permute-start | bytes 393224 | tf_op jit(solution)/shard_map/ppermute | solution.py:367
  21.9 2.0 %collective-permute-done.1.refs_2_ = bf16[3,256,256]{2,1,0:T(8,128)(2,1)S(1)} collective-permute-done((bf16[3,256,256]{2,1,0:T(8,128)(2,1)}, bf16[3,256,256]{2,1,0:T(8,128)(2,1)S(1)}, u32[]{:S(2)}, u32[]{:S(2)}) %collective-permute-start.1) | collective-permute-done | bytes 393248 | tf_op jit(solution)/shard_map/ppermute | solution.py:365
  23.8 3.5 %collective-permute-start.6 = (bf16[2,256,128]{2,1,0:T(8,128)(2,1)}, bf16[2,256,128]{2,1,0:T(8,128)(2,1)S(1)}, u32[]{:S(2)}, u32[]{:S(2)}) collective-permute-start(bf16[2,256,128]{2,1,0:T(8,128)(2,1)} %get-tuple-element.58), channel_id=1, source_target_pairs={{0,28},{4,24},{8,20},{12,16},{16,12},{20,8},{24,4},{28,0},{1,29},{... | collective-permute-start | bytes 393224 | tf_op jit(solution)/shard_map/ppermute | solution.py:367
  27.4 4.0 %shard_map.47 = (bf16[1024,2048]{1,0:T(8,128)(2,1)S(1)}, bf16[1024,2048]{1,0:T(8,128)(2,1)S(1)}) custom-call(s32[3]{0:T(128)S(1)} %pad_add_fusion.place_ref, bf16[1024,8192]{1,0:T(8,128)(2,1)} %w_ref.2), custom_call_target="tpu_custom_call" | custom-call | flops 1 | bytes 16777216 | tf_op jit(solution)/shard_map/pallas_call | solution.py:306
  31.5 2.9 %shard_map.48 = (f32[1024,256]{1,0:T(8,128)S(1)}, f32[256,128]{1,0:T(8,128)S(1)}) custom-call(s32[1]{0:T(128)} %bitcast.me_ref, bf16[3,256,256]{2,1,0:T(8,128)(2,1)S(1)} %copy-done, bf16[3,256,256]{2,1,0:T(8,128)(2,1)S(1)} %collective-permute-done.refs_1_, bf16[3,256,256]{2,1,0:T(8,128)(2,1)S(1)} %collective-permute-done.1.refs_2_, ...), custom_call_target="tpu_custom_call" | custom-call | flops 1 | bytes 1 | tf_op jit(solution)/shard_map/pallas_call | solution.py:375
  34.4 2.7 %collective-permute-done.5.refs_6_ = bf16[2,256,128]{2,1,0:T(8,128)(2,1)S(1)} collective-permute-done((bf16[2,256,128]{2,1,0:T(8,128)(2,1)}, bf16[2,256,128]{2,1,0:T(8,128)(2,1)S(1)}, u32[]{:S(2)}, u32[]{:S(2)}) %collective-permute-start.5) | collective-permute-done | bytes 131104 | tf_op jit(solution)/shard_map/ppermute | solution.py:367
  38.4 2.6 %shard_map.49 = (bf16[272,256]{1,0:T(8,128)(2,1)S(1)}, bf16[272,256]{1,0:T(8,128)(2,1)S(1)}, bf16[272,256]{1,0:T(8,128)(2,1)S(1)}, bf16[272,256]{1,0:T(8,128)(2,...) custom-call(s32[1]{0:T(128)} %bitcast.me_ref, ...), custom_call_target="tpu_custom_call" | custom-call | flops 1 | bytes 1 | tf_op jit(solution)/shard_map/pallas_call | solution.py:387
  41.0 3.8 %collective-permute-start.8 = (bf16[288,128]{1,0:T(8,128)(2,1)S(1)}, bf16[288,128]{1,0:T(8,128)(2,1)S(1)}, u32[]{:S(2)}, u32[]{:S(2)}) collective-permute-start(bf16[288,128]{1,0:T(8,128)(2,1)S(1)} %get-tuple-element.63), channel_id=1, source_target_pairs={{0,16},{4,20},{8,24},{12,28},{1,17},{5,21},{9,25},{13,29},{2,18},{... | collective-permute-start | bytes 221192 | tf_op jit(solution)/shard_map/ppermute | solution.py:397
  44.8 2.1 %collective-permute-start.9 = (bf16[288,128]{1,0:T(8,128)(2,1)S(1)}, bf16[288,128]{1,0:T(8,128)(2,1)S(1)}, u32[]{:S(2)}, u32[]{:S(2)}) collective-permute-start(bf16[288,128]{1,0:T(8,128)(2,1)S(1)} %get-tuple-element.64), channel_id=1, source_target_pairs={{0,20},{4,16},{8,28},{12,24},{1,21},{5,17},{9,29},{13,25},{2,22},{... | collective-permute-start | bytes 221192 | tf_op jit(solution)/shard_map/ppermute | solution.py:397
  47.8 2.7 %collective-permute-start.13 = (bf16[272,256]{1,0:T(8,128)(2,1)S(1)}, bf16[272,256]{1,0:T(8,128)(2,1)S(1)}, u32[]{:S(2)}, u32[]{:S(2)}) collective-permute-start(bf16[272,256]{1,0:T(8,128)(2,1)S(1)} %get-tuple-element.68), channel_id=1, source_target_pairs={{0,12},{4,8},{8,4},{12,0},{16,28},{20,24},{24,20},{28,16},{1,13},{... | collective-permute-start | bytes 417800 | tf_op jit(solution)/shard_map/ppermute | solution.py:399
  50.5 1.5 %collective-permute-start.10 = (bf16[288,128]{1,0:T(8,128)(2,1)S(1)}, bf16[288,128]{1,0:T(8,128)(2,1)S(1)}, u32[]{:S(2)}, u32[]{:S(2)}) collective-permute-start(bf16[288,128]{1,0:T(8,128)(2,1)S(1)} %get-tuple-element.65), channel_id=1, source_target_pairs={{0,24},{4,28},{8,16},{12,20},{1,25},{5,29},{9,17},{13,21},{2,26},{... | collective-permute-start | bytes 221192 | tf_op jit(solution)/shard_map/ppermute | solution.py:397
  52.0 3.0 %collective-permute-start.11 = (bf16[288,128]{1,0:T(8,128)(2,1)S(1)}, bf16[288,128]{1,0:T(8,128)(2,1)S(1)}, u32[]{:S(2)}, u32[]{:S(2)}) collective-permute-start(bf16[288,128]{1,0:T(8,128)(2,1)S(1)} %get-tuple-element.66), channel_id=1, source_target_pairs={{0,28},{4,24},{8,20},{12,16},{1,29},{5,25},{9,21},{13,17},{2,30},{... | collective-permute-start | bytes 221192 | tf_op jit(solution)/shard_map/ppermute | solution.py:397
  55.6 1.4 %collective-permute-done.11.refs_7_ = bf16[288,128]{1,0:T(8,128)(2,1)S(1)} collective-permute-done((bf16[288,128]{1,0:T(8,128)(2,1)S(1)}, bf16[288,128]{1,0:T(8,128)(2,1)S(1)}, u32[]{:S(2)}, u32[]{:S(2)}) %collective-permute-start.11) | collective-permute-done | bytes 73760 | tf_op jit(solution)/shard_map/ppermute | solution.py:397
  57.1 1.8 %shard_map.50 = (bf16[256,1024]{1,0:T(8,128)(2,1)S(1)}, bf16[256,2048]{1,0:T(8,128)(2,1)S(1)}) custom-call(s32[1]{0:T(128)} %bitcast.me_ref, bf16[272,256]{1,0:T(8,128)(2,1)S(1)} %get-tuple-element.61.refs_0_, bf16[272,256]{1,0:T(8,128)(2,1)S(1)} %collective-permute-done.7.refs_1_, bf16[272,256]{1,0:T(8,128)(2,1)S(1)} %collective-permute-done.12.refs_2_, ...), custom_call_target="tpu_custom_call" | custom-call | flops 1 | bytes 1 | tf_op jit(solution)/shard_map/pallas_call | solution.py:408
  62.0 1.6 %collective-permute-start.17 = (bf16[256,2048]{1,0:T(8,128)(2,1)S(1)}, bf16[256,2048]{1,0:T(8,128)(2,1)S(1)}, u32[]{:S(2)}, u32[]{:S(2)}) collective-permute-start(bf16[256,2048]{1,0:T(8,128)(2,1)S(1)} %add_convert_fusion.1), channel_id=1, source_target_pairs={{0,2},{1,3},{2,0},{3,1},{4,6},{5,7},{6,4},{7,5},{8,10},{9,11},{10,... | collective-permute-start | bytes 3145736 | tf_op jit(solution)/shard_map/ppermute | solution.py:423
  63.7 4.0 %shard_map.52 = (bf16[1024,2048]{1,0:T(8,128)(2,1)S(1)}, bf16[1024,2048]{1,0:T(8,128)(2,1)S(1)}) custom-call(s32[3]{0:T(128)S(1)} %pad_add_fusion.1.place_ref, bf16[1024,8192]{1,0:T(8,128)(2,1)} %w_ref.2), custom_call_target="tpu_custom_call" | custom-call | flops 1 | bytes 16777216 | tf_op jit(solution)/shard_map/pallas_call | solution.py:306
  67.7 2.4 %shard_map.53 = (bf16[256,2048]{1,0:T(8,128)(2,1)S(1)}, bf16[256,2048]{1,0:T(8,128)(2,1)S(1)}) custom-call(bf16[256,1024]{1,0:T(8,128)(2,1)S(1)} %get-tuple-element.81.heads, bf16[1024,2048]{1,0:T(8,128)(2,1)S(1)} %get-tuple-element.83.refs_0_, bf16[1024,2048]{1,0:T(8,128)(2,1)S(1)} %get-tuple-element.84.refs_1_), custom_call_target="tpu_custom_call" | custom-call | flops 1 | bytes 1 | tf_op jit(solution)/shard_map/pallas_call | solution.py:281
  72.9 14.4 %collective-permute-done.17 = bf16[256,2048]{1,0:T(8,128)(2,1)S(1)} collective-permute-done((bf16[256,2048]{1,0:T(8,128)(2,1)S(1)}, bf16[256,2048]{1,0:T(8,128)(2,1)S(1)}, u32[]{:S(2)}, u32[]{:S(2)}) %collective-permute-start.17) | collective-permute-done | bytes 1048608 | tf_op jit(solution)/shard_map/ppermute | solution.py:423
  87.3 1.5 %add_convert_fusion = bf16[256,2048]{1,0:T(8,128)(2,1)} fusion(bf16[256,2048]{1,0:T(8,128)(2,1)S(1)} %collective-permute-done.17, bf16[256,2048]{1,0:T(8,128)(2,1)S(1)} %get-tuple-element.85, bf16[256,1024]{1,0:T(8,128)(2,1)S(1)} %collective-permute-done.16, bf16[256,1024]{1,0:T(8,128)(2,1)S(1)} %collective-permute-done.15), kind=kLoop, calls=%fused_computation | loop fusion | flops 4718592 | bytes 4194304 | tf_op jit(solution)/shard_map/convert_element_type | solution.py:434
  (27 shorter events, 10.2 us)
Async XLA Ops:
  3.0 15.1 %collective-permute-start = (bf16[3,256,256]{2,1,0:T(8,128)(2,1)}, bf16[3,256,256]{2,1,0:T(8,128)(2,1)S(1)}, u32[]{:S(2)}, u32[]{:S(2)}) collective-permute-start(bf16[3,256,256]{2,1,0:T(8,128)(2,1)} %get-tuple-element.47), channel_id=1, source_target_pairs={{0,4},{4,0},{8,12},{12,8},{16,20},{20,16},{24,28},{28,24},{1,5},{5... | collective-permute-start | bytes 1179656 | tf_op jit(solution)/shard_map/ppermute | solution.py:365
  6.0 17.9 %collective-permute-start.1 = (bf16[3,256,256]{2,1,0:T(8,128)(2,1)}, bf16[3,256,256]{2,1,0:T(8,128)(2,1)S(1)}, u32[]{:S(2)}, u32[]{:S(2)}) collective-permute-start(bf16[3,256,256]{2,1,0:T(8,128)(2,1)} %get-tuple-element.48), channel_id=1, source_target_pairs={{0,8},{4,12},{8,0},{12,4},{16,24},{20,28},{24,16},{28,20},{1,9},{5... | collective-permute-start | bytes 1179656 | tf_op jit(solution)/shard_map/ppermute | solution.py:365
  7.5 23.9 %collective-permute-start.2 = (bf16[3,256,256]{2,1,0:T(8,128)(2,1)}, bf16[3,256,256]{2,1,0:T(8,128)(2,1)S(1)}, u32[]{:S(2)}, u32[]{:S(2)}) collective-permute-start(bf16[3,256,256]{2,1,0:T(8,128)(2,1)} %get-tuple-element.49), channel_id=1, source_target_pairs={{0,12},{4,8},{8,4},{12,0},{16,28},{20,24},{24,20},{28,16},{1,13},{... | collective-permute-start | bytes 1179656 | tf_op jit(solution)/shard_map/ppermute | solution.py:365
  7.5 26.8 %collective-permute-start.3 = (bf16[2,256,128]{2,1,0:T(8,128)(2,1)}, bf16[2,256,128]{2,1,0:T(8,128)(2,1)S(1)}, u32[]{:S(2)}, u32[]{:S(2)}) collective-permute-start(bf16[2,256,128]{2,1,0:T(8,128)(2,1)} %get-tuple-element.55), channel_id=1, source_target_pairs={{0,16},{4,20},{8,24},{12,28},{16,0},{20,4},{24,8},{28,12},{1,17},{... | collective-permute-start | bytes 393224 | tf_op jit(solution)/shard_map/ppermute | solution.py:367
  10.5 23.9 %collective-permute-start.4 = (bf16[2,256,128]{2,1,0:T(8,128)(2,1)}, bf16[2,256,128]{2,1,0:T(8,128)(2,1)S(1)}, u32[]{:S(2)}, u32[]{:S(2)}) collective-permute-start(bf16[2,256,128]{2,1,0:T(8,128)(2,1)} %get-tuple-element.56), channel_id=1, source_target_pairs={{0,20},{4,16},{8,28},{12,24},{16,4},{20,0},{24,12},{28,8},{1,21},{... | collective-permute-start | bytes 393224 | tf_op jit(solution)/shard_map/ppermute | solution.py:367
  18.1 19.0 %collective-permute-start.5 = (bf16[2,256,128]{2,1,0:T(8,128)(2,1)}, bf16[2,256,128]{2,1,0:T(8,128)(2,1)S(1)}, u32[]{:S(2)}, u32[]{:S(2)}) collective-permute-start(bf16[2,256,128]{2,1,0:T(8,128)(2,1)} %get-tuple-element.57), channel_id=1, source_target_pairs={{0,24},{4,28},{8,16},{12,20},{16,8},{20,12},{24,0},{28,4},{1,25},{... | collective-permute-start | bytes 393224 | tf_op jit(solution)/shard_map/ppermute | solution.py:367
  23.8 14.6 %collective-permute-start.6 = (bf16[2,256,128]{2,1,0:T(8,128)(2,1)}, bf16[2,256,128]{2,1,0:T(8,128)(2,1)S(1)}, u32[]{:S(2)}, u32[]{:S(2)}) collective-permute-start(bf16[2,256,128]{2,1,0:T(8,128)(2,1)} %get-tuple-element.58), channel_id=1, source_target_pairs={{0,28},{4,24},{8,20},{12,16},{16,12},{20,8},{24,4},{28,0},{1,29},{... | collective-permute-start | bytes 393224 | tf_op jit(solution)/shard_map/ppermute | solution.py:367
  27.4 4.1 %copy-start = (bf16[3,256,256]{2,1,0:T(8,128)(2,1)S(1)}, bf16[3,256,256]{2,1,0:T(8,128)(2,1)}, u32[]{:S(2)}) copy-start(bf16[3,256,256]{2,1,0:T(8,128)(2,1)} %get-tuple-element.46.refs_0_) | copy-start | bytes 1179652
  41.0 9.5 %collective-permute-start.8 = (bf16[288,128]{1,0:T(8,128)(2,1)S(1)}, bf16[288,128]{1,0:T(8,128)(2,1)S(1)}, u32[]{:S(2)}, u32[]{:S(2)}) collective-permute-start(bf16[288,128]{1,0:T(8,128)(2,1)S(1)} %get-tuple-element.63), channel_id=1, source_target_pairs={{0,16},{4,20},{8,24},{12,28},{1,17},{5,21},{9,25},{13,29},{2,18},{... | collective-permute-start | bytes 221192 | tf_op jit(solution)/shard_map/ppermute | solution.py:397
  44.8 7.2 %collective-permute-start.9 = (bf16[288,128]{1,0:T(8,128)(2,1)S(1)}, bf16[288,128]{1,0:T(8,128)(2,1)S(1)}, u32[]{:S(2)}, u32[]{:S(2)}) collective-permute-start(bf16[288,128]{1,0:T(8,128)(2,1)S(1)} %get-tuple-element.64), channel_id=1, source_target_pairs={{0,20},{4,16},{8,28},{12,24},{1,21},{5,17},{9,29},{13,25},{2,22},{... | collective-permute-start | bytes 221192 | tf_op jit(solution)/shard_map/ppermute | solution.py:397
  46.9 10.1 %collective-permute-start.7 = (bf16[272,256]{1,0:T(8,128)(2,1)S(1)}, bf16[272,256]{1,0:T(8,128)(2,1)S(1)}, u32[]{:S(2)}, u32[]{:S(2)}) collective-permute-start(bf16[272,256]{1,0:T(8,128)(2,1)S(1)} %get-tuple-element.62), channel_id=1, source_target_pairs={{0,4},{4,0},{8,12},{12,8},{16,20},{20,16},{24,28},{28,24},{1,5},{5... | collective-permute-start | bytes 417800 | tf_op jit(solution)/shard_map/ppermute | solution.py:399
  47.6 9.4 %collective-permute-start.12 = (bf16[272,256]{1,0:T(8,128)(2,1)S(1)}, bf16[272,256]{1,0:T(8,128)(2,1)S(1)}, u32[]{:S(2)}, u32[]{:S(2)}) collective-permute-start(bf16[272,256]{1,0:T(8,128)(2,1)S(1)} %get-tuple-element.67), channel_id=1, source_target_pairs={{0,8},{4,12},{8,0},{12,4},{16,24},{20,28},{24,16},{28,20},{1,9},{5... | collective-permute-start | bytes 417800 | tf_op jit(solution)/shard_map/ppermute | solution.py:399
  47.8 9.2 %collective-permute-start.13 = (bf16[272,256]{1,0:T(8,128)(2,1)S(1)}, bf16[272,256]{1,0:T(8,128)(2,1)S(1)}, u32[]{:S(2)}, u32[]{:S(2)}) collective-permute-start(bf16[272,256]{1,0:T(8,128)(2,1)S(1)} %get-tuple-element.68), channel_id=1, source_target_pairs={{0,12},{4,8},{8,4},{12,0},{16,28},{20,24},{24,20},{28,16},{1,13},{... | collective-permute-start | bytes 417800 | tf_op jit(solution)/shard_map/ppermute | solution.py:399
  50.5 5.1 %collective-permute-start.10 = (bf16[288,128]{1,0:T(8,128)(2,1)S(1)}, bf16[288,128]{1,0:T(8,128)(2,1)S(1)}, u32[]{:S(2)}, u32[]{:S(2)}) collective-permute-start(bf16[288,128]{1,0:T(8,128)(2,1)S(1)} %get-tuple-element.65), channel_id=1, source_target_pairs={{0,24},{4,28},{8,16},{12,20},{1,25},{5,29},{9,17},{13,21},{2,26},{... | collective-permute-start | bytes 221192 | tf_op jit(solution)/shard_map/ppermute | solution.py:397
  52.0 5.0 %collective-permute-start.11 = (bf16[288,128]{1,0:T(8,128)(2,1)S(1)}, bf16[288,128]{1,0:T(8,128)(2,1)S(1)}, u32[]{:S(2)}, u32[]{:S(2)}) collective-permute-start(bf16[288,128]{1,0:T(8,128)(2,1)S(1)} %get-tuple-element.66), channel_id=1, source_target_pairs={{0,28},{4,24},{8,20},{12,16},{1,29},{5,25},{9,21},{13,17},{2,30},{... | collective-permute-start | bytes 221192 | tf_op jit(solution)/shard_map/ppermute | solution.py:397
  58.9 2.7 %collective-permute-start.14 = (bf16[256,2048]{1,0:T(8,128)(2,1)S(1)}, bf16[256,2048]{1,0:T(8,128)(2,1)S(1)}, u32[]{:S(2)}, u32[]{:S(2)}) collective-permute-start(bf16[256,2048]{1,0:T(8,128)(2,1)S(1)} %get-tuple-element.79), channel_id=1, source_target_pairs={{0,1},{1,0},{2,3},{3,2},{4,5},{5,4},{6,7},{7,6},{8,9},{9,8},{10,11... | collective-permute-start | bytes 3145736 | tf_op jit(solution)/shard_map/ppermute | solution.py:422
  62.0 25.3 %collective-permute-start.17 = (bf16[256,2048]{1,0:T(8,128)(2,1)S(1)}, bf16[256,2048]{1,0:T(8,128)(2,1)S(1)}, u32[]{:S(2)}, u32[]{:S(2)}) collective-permute-start(bf16[256,2048]{1,0:T(8,128)(2,1)S(1)} %add_convert_fusion.1), channel_id=1, source_target_pairs={{0,2},{1,3},{2,0},{3,1},{4,6},{5,7},{6,4},{7,5},{8,10},{9,11},{10,... | collective-permute-start | bytes 3145736 | tf_op jit(solution)/shard_map/ppermute | solution.py:423
  70.2 2.0 %collective-permute-start.15 = (bf16[256,1024]{1,0:T(8,128)(2,1)S(1)}, bf16[256,1024]{1,0:T(8,128)(2,1)S(1)}, u32[]{:S(2)}, u32[]{:S(2)}) collective-permute-start(bf16[256,1024]{1,0:T(8,128)(2,1)S(1)} %get-tuple-element.87), channel_id=1, source_target_pairs={{0,1},{1,0},{2,3},{3,2},{4,5},{5,4},{6,7},{7,6},{8,9},{9,8},{10,11... | collective-permute-start | bytes 1572872 | tf_op jit(solution)/shard_map/ppermute | solution.py:429
  70.3 2.6 %collective-permute-start.16 = (bf16[256,1024]{1,0:T(8,128)(2,1)S(1)}, bf16[256,1024]{1,0:T(8,128)(2,1)S(1)}, u32[]{:S(2)}, u32[]{:S(2)}) collective-permute-start(bf16[256,1024]{1,0:T(8,128)(2,1)S(1)} %get-tuple-element.88), channel_id=1, source_target_pairs={{0,1},{1,0},{2,3},{3,2},{4,5},{5,4},{6,7},{7,6},{8,9},{9,8},{10,11... | collective-permute-start | bytes 1572872 | tf_op jit(solution)/shard_map/ppermute | solution.py:429

commit v4 on v3

--- a/solution.py
+++ b/solution.py
@@ -11,6 +11,7 @@
 MIB = 1 << 20
 OWN_PARTS = 2
 STAT_ROWS = 16
+T2TIE = (2, 3)
 LOG2E = 1.4426950408889634
 FETCH_MIB = 40
 COST = pl.CostEstimate(flops=1, bytes_accessed=1, transcendentals=1)
@@ -212,18 +213,16 @@
     turned = jnp.transpose(table)
     for i, part in enumerate(split3(turned[0 : 2 * half, :])):
         stats[i] = part.astype(jnp.float32)
-    empty = jnp.zeros((STAT_ROWS - 3, rows), jnp.float32)
     for shift in range(half):
         goal = place ^ shift
         at = pl.ds(pl.multiple_of(goal * rows, rows), rows)
         for out, source, first in ((back[shift], o_all, 0), (over[shift], o_x, half)):
             out[0:rows, :] = source[at, :]
+            wide = out.shape[1]
             lines = [stats[i, pl.ds(first + goal, 1), :] for i in range(3)]
-            block = jnp.concatenate(lines + [empty], axis=0).astype(jnp.bfloat16)
-            wide = out.shape[1]
-            for step in range(rows // wide):
-                here = slice(rows + step * STAT_ROWS, rows + (step + 1) * STAT_ROWS)
-                out[here, :] = block[:, step * wide : (step + 1) * wide]
+            lines = [line[:, at : at + wide] for line in lines for at in range(0, rows, wide)]
+            empty = jnp.zeros((STAT_ROWS - len(lines), wide), jnp.float32)
+            out[rows:, :] = jnp.concatenate(lines + [empty], axis=0).astype(jnp.bfloat16)
 
 
 def assemble(half, me_ref, back, over, heads):
@@ -231,12 +230,14 @@
     upper, place = me_ref[0] // half, lax.rem(me_ref[0], half)
 
     def read_log(piece):
-        wide = piece.shape[1]
-        blocks = [
-            piece[rows + i * STAT_ROWS : rows + (i + 1) * STAT_ROWS, :] for i in range(rows // wide)
+        steps = rows // piece.shape[1]
+        block = piece[rows:, :].astype(jnp.float32)
+        sums = [
+            block[i : i + 1, :] + block[steps + i : steps + i + 1, :]
+            + block[2 * steps + i : 2 * steps + i + 1, :]
+            for i in range(steps)
         ]
-        block = jnp.concatenate([one.astype(jnp.float32) for one in blocks], axis=1)
-        return block[0:1, :] + block[1:2, :] + block[2:3, :]
+        return jnp.concatenate(sums, axis=1)
 
     gaps = []
     for shift in range(half):
@@ -369,8 +370,8 @@
 
     inner[1], *rest = lax.optimization_barrier((inner[1], *inner[2:], near))
     inner[2:], near = rest[:-1], rest[-1]
-    back_shape = jax.ShapeDtypeStruct((rows + STAT_ROWS * (rows // (2 * HD)), 2 * HD), bf16)
-    over_shape = jax.ShapeDtypeStruct((rows + STAT_ROWS * (rows // HD), HD), bf16)
+    back_shape = jax.ShapeDtypeStruct((rows + STAT_ROWS, 2 * HD), bf16)
+    over_shape = jax.ShapeDtypeStruct((rows + STAT_ROWS, HD), bf16)
     big, small = pltpu.VMEM((half * rows, 2 * HD), bf16), pltpu.VMEM((half * rows, HD), bf16)
     results = pl.pallas_call(
         functools.partial(inner_kernel, half),
@@ -394,9 +395,12 @@
         cost_estimate=COST,
     )(place, *inner, *cross, *results)
     back, over = list(outs[:half]), list(outs[half:])
-    over = [lax.ppermute(piece, "ctx", between(shift, 1, 0)) for shift, piece in enumerate(over)]
     for shift in range(1, half):
         back[shift] = lax.ppermute(back[shift], "ctx", within(shift))
+    for shift in range(half):
+        if shift in T2TIE:
+            over[shift], back[1] = lax.optimization_barrier((over[shift], back[1]))
+        over[shift] = lax.ppermute(over[shift], "ctx", between(shift, 1, 0))
 
     tied = (back[1], *over, *back[2:])
     back[1], *tied = lax.optimization_barrier(tied)
@@ -438,7 +442,7 @@
     def per_device(attn_query, attn_key, attn_value, out_weight):
         heads, n, tp = attn_query.shape[1] // HD, mesh.shape["ctx"], mesh.shape["tp"]
         paired = heads == n and n > 2 and n & (n - 1) == 0 and n <= HD and tp % 2 == 0 and tp > 2
-        form = heads_form if paired and attn_query.shape[0] % (2 * HD) == 0 else gather_form
+        form = heads_form if paired and attn_query.shape[0] == 2 * HD else gather_form
         return form(attn_query, attn_key, attn_value, out_weight)
 
     return jax.shard_map(

time: 89.5 us -> 87.9 us (0.982)
  starting transfers between devices: 32.4 us -> 30.6 us
    ppermute x4, starting transfers between devices: 10.5 us -> 8.52 us  [heads_form(): over[shift] = lax.ppermute(over[shift], 'ctx', between(shift, 1, 0))]
  transfers between devices with their start and end apart: 18 -> 18, of which waited for: 10 -> 11; matrix products, arithmetic and copies ran while one was open for 0% -> 0% of each run, Pallas kernels for 16% -> 17%
where the time goes in v4:
time: 87.9 us; the launch traced here: 87.5 us
  waiting for transfers between devices  32.7 us (37%)
  starting transfers between devices  30.6 us (35%)
  Pallas kernels  21.9 us (25%)
  other arithmetic  2.05 us (2%)
    ppermute x1, waiting for transfers between devices, heads_form(): crossing.append(lax.ppermute(both, 'tp', perm))  14.4 us
    ppermute x4, starting transfers between devices, heads_form(): lax.ppermute(piece, 'ctx', between(shift, 1, 1))  11.5 us
    ppermute x4, starting transfers between devices, heads_form(): over[shift] = lax.ppermute(over[shift], 'ctx', between(shift, 1, 0))  8.52 us
    ppermute x3, waiting for transfers between devices, heads_form(): inner[shift] = lax.ppermute(inner[shift], 'ctx', within(shift))  8.24 us
    pallas_call x2, Pallas kernels, fetch(): pl.pallas_call(fetch_kernel, in_specs=[pl.BlockSpec(memory_space=pltpu.SM...  8.07 us
    ppermute x3, starting transfers between devices, heads_form(): inner[shift] = lax.ppermute(inner[shift], 'ctx', within(shift))  4.58 us
    ppermute x4, waiting for transfers between devices, heads_form(): lax.ppermute(piece, 'ctx', between(shift, 1, 1))  4.07 us
    ppermute x3, starting transfers between devices, heads_form(): back[shift] = lax.ppermute(back[shift], 'ctx', within(shift))  3.68 us
  transfers between devices with their start and end apart: 18, of which 11 were waited for; matrix products, arithmetic and copies ran while one was open for 0% of the time, Pallas kernels for 17%

profile of v4, /device:TPU:0, one launch (start us, length us, event | category | flops | bytes accessed | tf_op | source)
XLA Modules:
  0.0 87.5 jit_solution(17142794161855149371)
XLA Ops:
  0.0 2.9 %shard_map.46 = (bf16[3,256,256]{2,1,0:T(8,128)(2,1)}, bf16[3,256,256]{2,1,0:T(8,128)(2,1)}, bf16[3,256,256]{2,1,0:T(8,128)(2,1)}, bf16[3,256,256]{2,1,0:T(8,128...) custom-call(s32[1]{0:T(128)} %bitcast.me_ref, ...), custom_call_target="tpu_custom_call" | custom-call | flops 1 | bytes 1 | tf_op jit(solution)/shard_map/pallas_call | solution.py:339
  3.0 3.0 %collective-permute-start = (bf16[3,256,256]{2,1,0:T(8,128)(2,1)}, bf16[3,256,256]{2,1,0:T(8,128)(2,1)S(1)}, u32[]{:S(2)}, u32[]{:S(2)}) collective-permute-start(bf16[3,256,256]{2,1,0:T(8,128)(2,1)} %get-tuple-element.51), channel_id=1, source_target_pairs={{0,4},{4,0},{8,12},{12,8},{16,20},{20,16},{24,28},{28,24},{1,5},{5... | collective-permute-start | bytes 1179656 | tf_op jit(solution)/shard_map/ppermute | solution.py:366
  6.0 1.6 %collective-permute-start.1 = (bf16[3,256,256]{2,1,0:T(8,128)(2,1)}, bf16[3,256,256]{2,1,0:T(8,128)(2,1)S(1)}, u32[]{:S(2)}, u32[]{:S(2)}) collective-permute-start(bf16[3,256,256]{2,1,0:T(8,128)(2,1)} %get-tuple-element.52), channel_id=1, source_target_pairs={{0,8},{4,12},{8,0},{12,4},{16,24},{20,28},{24,16},{28,20},{1,9},{5... | collective-permute-start | bytes 1179656 | tf_op jit(solution)/shard_map/ppermute | solution.py:366
  7.5 2.9 %collective-permute-start.3 = (bf16[2,256,128]{2,1,0:T(8,128)(2,1)}, bf16[2,256,128]{2,1,0:T(8,128)(2,1)S(1)}, u32[]{:S(2)}, u32[]{:S(2)}) collective-permute-start(bf16[2,256,128]{2,1,0:T(8,128)(2,1)} %get-tuple-element.59), channel_id=1, source_target_pairs={{0,16},{4,20},{8,24},{12,28},{16,0},{20,4},{24,8},{28,12},{1,17},{... | collective-permute-start | bytes 393224 | tf_op jit(solution)/shard_map/ppermute | solution.py:368
  11.8 6.3 %collective-permute-done.refs_1_ = bf16[3,256,256]{2,1,0:T(8,128)(2,1)S(1)} collective-permute-done((bf16[3,256,256]{2,1,0:T(8,128)(2,1)}, bf16[3,256,256]{2,1,0:T(8,128)(2,1)S(1)}, u32[]{:S(2)}, u32[]{:S(2)}) %collective-permute-start) | collective-permute-done | bytes 393248 | tf_op jit(solution)/shard_map/ppermute | solution.py:366
  18.1 3.8 %collective-permute-start.5 = (bf16[2,256,128]{2,1,0:T(8,128)(2,1)}, bf16[2,256,128]{2,1,0:T(8,128)(2,1)S(1)}, u32[]{:S(2)}, u32[]{:S(2)}) collective-permute-start(bf16[2,256,128]{2,1,0:T(8,128)(2,1)} %get-tuple-element.61), channel_id=1, source_target_pairs={{0,24},{4,28},{8,16},{12,20},{16,8},{20,12},{24,0},{28,4},{1,25},{... | collective-permute-start | bytes 393224 | tf_op jit(solution)/shard_map/ppermute | solution.py:368
  21.9 2.0 %collective-permute-done.1.refs_2_ = bf16[3,256,256]{2,1,0:T(8,128)(2,1)S(1)} collective-permute-done((bf16[3,256,256]{2,1,0:T(8,128)(2,1)}, bf16[3,256,256]{2,1,0:T(8,128)(2,1)S(1)}, u32[]{:S(2)}, u32[]{:S(2)}) %collective-permute-start.1) | collective-permute-done | bytes 393248 | tf_op jit(solution)/shard_map/ppermute | solution.py:366
  23.8 3.5 %collective-permute-start.6 = (bf16[2,256,128]{2,1,0:T(8,128)(2,1)}, bf16[2,256,128]{2,1,0:T(8,128)(2,1)S(1)}, u32[]{:S(2)}, u32[]{:S(2)}) collective-permute-start(bf16[2,256,128]{2,1,0:T(8,128)(2,1)} %get-tuple-element.62), channel_id=1, source_target_pairs={{0,28},{4,24},{8,20},{12,16},{16,12},{20,8},{24,4},{28,0},{1,29},{... | collective-permute-start | bytes 393224 | tf_op jit(solution)/shard_map/ppermute | solution.py:368
  27.4 4.0 %shard_map.47 = (bf16[1024,2048]{1,0:T(8,128)(2,1)S(1)}, bf16[1024,2048]{1,0:T(8,128)(2,1)S(1)}) custom-call(s32[3]{0:T(128)S(1)} %pad_add_fusion.place_ref, bf16[1024,8192]{1,0:T(8,128)(2,1)} %w_ref.2), custom_call_target="tpu_custom_call" | custom-call | flops 1 | bytes 16777216 | tf_op jit(solution)/shard_map/pallas_call | solution.py:307
  31.5 2.9 %shard_map.48 = (f32[1024,256]{1,0:T(8,128)S(1)}, f32[256,128]{1,0:T(8,128)S(1)}) custom-call(s32[1]{0:T(128)} %bitcast.me_ref, bf16[3,256,256]{2,1,0:T(8,128)(2,1)S(1)} %copy-done, bf16[3,256,256]{2,1,0:T(8,128)(2,1)S(1)} %collective-permute-done.refs_1_, bf16[3,256,256]{2,1,0:T(8,128)(2,1)S(1)} %collective-permute-done.1.refs_2_, ...), custom_call_target="tpu_custom_call" | custom-call | flops 1 | bytes 1 | tf_op jit(solution)/shard_map/pallas_call | solution.py:376
  34.4 2.7 %collective-permute-done.5.refs_6_ = bf16[2,256,128]{2,1,0:T(8,128)(2,1)S(1)} collective-permute-done((bf16[2,256,128]{2,1,0:T(8,128)(2,1)}, bf16[2,256,128]{2,1,0:T(8,128)(2,1)S(1)}, u32[]{:S(2)}, u32[]{:S(2)}) %collective-permute-start.5) | collective-permute-done | bytes 131104 | tf_op jit(solution)/shard_map/ppermute | solution.py:368
  37.0 1.4 %collective-permute-done.6.refs_7_ = bf16[2,256,128]{2,1,0:T(8,128)(2,1)S(1)} collective-permute-done((bf16[2,256,128]{2,1,0:T(8,128)(2,1)}, bf16[2,256,128]{2,1,0:T(8,128)(2,1)S(1)}, u32[]{:S(2)}, u32[]{:S(2)}) %collective-permute-start.6) | collective-permute-done | bytes 131104 | tf_op jit(solution)/shard_map/ppermute | solution.py:368
  38.4 2.6 %shard_map.49 = (bf16[272,256]{1,0:T(8,128)(2,1)S(1)}, bf16[272,256]{1,0:T(8,128)(2,1)S(1)}, bf16[272,256]{1,0:T(8,128)(2,1)S(1)}, bf16[272,256]{1,0:T(8,128)(2,...) custom-call(s32[1]{0:T(128)} %bitcast.me_ref, ...), custom_call_target="tpu_custom_call" | custom-call | flops 1 | bytes 1 | tf_op jit(solution)/shard_map/pallas_call | solution.py:388
  41.0 1.6 %collective-permute-start.7 = (bf16[272,256]{1,0:T(8,128)(2,1)S(1)}, bf16[272,256]{1,0:T(8,128)(2,1)S(1)}, u32[]{:S(2)}, u32[]{:S(2)}) collective-permute-start(bf16[272,256]{1,0:T(8,128)(2,1)S(1)} %get-tuple-element.68), channel_id=1, source_target_pairs={{0,4},{4,0},{8,12},{12,8},{16,20},{20,16},{24,28},{28,24},{1,5},{5... | collective-permute-start | bytes 417800 | tf_op jit(solution)/shard_map/ppermute | solution.py:399
  42.6 3.8 %collective-permute-start.8 = (bf16[272,128]{1,0:T(8,128)(2,1)S(1)}, bf16[272,128]{1,0:T(8,128)(2,1)S(1)}, u32[]{:S(2)}, u32[]{:S(2)}) collective-permute-start(bf16[272,128]{1,0:T(8,128)(2,1)S(1)} %get-tuple-element.71), channel_id=1, source_target_pairs={{0,16},{4,20},{8,24},{12,28},{1,17},{5,21},{9,25},{13,29},{2,18},{... | collective-permute-start | bytes 208904 | tf_op jit(solution)/shard_map/ppermute | solution.py:403
  46.6 1.9 %collective-permute-start.13 = (bf16[272,256]{1,0:T(8,128)(2,1)S(1)}, bf16[272,256]{1,0:T(8,128)(2,1)S(1)}, u32[]{:S(2)}, u32[]{:S(2)}) collective-permute-start(bf16[272,256]{1,0:T(8,128)(2,1)S(1)} %get-tuple-element.76), channel_id=1, source_target_pairs={{0,12},{4,8},{8,4},{12,0},{16,28},{20,24},{24,20},{28,16},{1,13},{... | collective-permute-start | bytes 417800 | tf_op jit(solution)/shard_map/ppermute | solution.py:399
  48.5 2.1 %collective-permute-start.9 = (bf16[272,128]{1,0:T(8,128)(2,1)S(1)}, bf16[272,128]{1,0:T(8,128)(2,1)S(1)}, u32[]{:S(2)}, u32[]{:S(2)}) collective-permute-start(bf16[272,128]{1,0:T(8,128)(2,1)S(1)} %get-tuple-element.72), channel_id=1, source_target_pairs={{0,20},{4,16},{8,28},{12,24},{1,21},{5,17},{9,29},{13,25},{2,22},{... | collective-permute-start | bytes 208904 | tf_op jit(solution)/shard_map/ppermute | solution.py:403
  55.8 1.8 %shard_map.50 = (bf16[256,1024]{1,0:T(8,128)(2,1)S(1)}, bf16[256,2048]{1,0:T(8,128)(2,1)S(1)}) custom-call(s32[1]{0:T(128)} %bitcast.me_ref, bf16[272,256]{1,0:T(8,128)(2,1)S(1)} %get-tuple-element.65.refs_0_, bf16[272,256]{1,0:T(8,128)(2,1)S(1)} %collective-permute-done.7.refs_1_, bf16[272,256]{1,0:T(8,128)(2,1)S(1)} %collective-permute-done.12.refs_2_, ...), custom_call_target="tpu_custom_call" | custom-call | flops 1 | bytes 1 | tf_op jit(solution)/shard_map/pallas_call | solution.py:412
  60.7 1.6 %collective-permute-start.17 = (bf16[256,2048]{1,0:T(8,128)(2,1)S(1)}, bf16[256,2048]{1,0:T(8,128)(2,1)S(1)}, u32[]{:S(2)}, u32[]{:S(2)}) collective-permute-start(bf16[256,2048]{1,0:T(8,128)(2,1)S(1)} %add_convert_fusion.1), channel_id=1, source_target_pairs={{0,2},{1,3},{2,0},{3,1},{4,6},{5,7},{6,4},{7,5},{8,10},{9,11},{10,... | collective-permute-start | bytes 3145736 | tf_op jit(solution)/shard_map/ppermute | solution.py:427
  62.4 4.0 %shard_map.52 = (bf16[1024,2048]{1,0:T(8,128)(2,1)S(1)}, bf16[1024,2048]{1,0:T(8,128)(2,1)S(1)}) custom-call(s32[3]{0:T(128)S(1)} %pad_add_fusion.1.place_ref, bf16[1024,8192]{1,0:T(8,128)(2,1)} %w_ref.2), custom_call_target="tpu_custom_call" | custom-call | flops 1 | bytes 16777216 | tf_op jit(solution)/shard_map/pallas_call | solution.py:307
  66.4 2.4 %shard_map.53 = (bf16[256,2048]{1,0:T(8,128)(2,1)S(1)}, bf16[256,2048]{1,0:T(8,128)(2,1)S(1)}) custom-call(bf16[256,1024]{1,0:T(8,128)(2,1)S(1)} %get-tuple-element.89.heads, bf16[1024,2048]{1,0:T(8,128)(2,1)S(1)} %get-tuple-element.91.refs_0_, bf16[1024,2048]{1,0:T(8,128)(2,1)S(1)} %get-tuple-element.92.refs_1_), custom_call_target="tpu_custom_call" | custom-call | flops 1 | bytes 1 | tf_op jit(solution)/shard_map/pallas_call | solution.py:282
  69.5 1.4 %collective-permute-done.15 = bf16[256,1024]{1,0:T(8,128)(2,1)S(1)} collective-permute-done((bf16[256,1024]{1,0:T(8,128)(2,1)S(1)}, bf16[256,1024]{1,0:T(8,128)(2,1)S(1)}, u32[]{:S(2)}, u32[]{:S(2)}) %collective-permute-start.15) | collective-permute-done | bytes 524320 | tf_op jit(solution)/shard_map/ppermute | solution.py:433
  71.6 14.4 %collective-permute-done.17 = bf16[256,2048]{1,0:T(8,128)(2,1)S(1)} collective-permute-done((bf16[256,2048]{1,0:T(8,128)(2,1)S(1)}, bf16[256,2048]{1,0:T(8,128)(2,1)S(1)}, u32[]{:S(2)}, u32[]{:S(2)}) %collective-permute-start.17) | collective-permute-done | bytes 1048608 | tf_op jit(solution)/shard_map/ppermute | solution.py:427
  86.0 1.5 %add_convert_fusion = bf16[256,2048]{1,0:T(8,128)(2,1)} fusion(bf16[256,2048]{1,0:T(8,128)(2,1)S(1)} %collective-permute-done.17, bf16[256,2048]{1,0:T(8,128)(2,1)S(1)} %get-tuple-element.93, bf16[256,1024]{1,0:T(8,128)(2,1)S(1)} %collective-permute-done.16, bf16[256,1024]{1,0:T(8,128)(2,1)S(1)} %collective-permute-done.15), kind=kLoop, calls=%fused_computation | loop fusion | flops 4718592 | bytes 4194304 | tf_op jit(solution)/shard_map/convert_element_type | solution.py:438
  (27 shorter events, 11.3 us)
Async XLA Ops:
  3.0 15.1 %collective-permute-start = (bf16[3,256,256]{2,1,0:T(8,128)(2,1)}, bf16[3,256,256]{2,1,0:T(8,128)(2,1)S(1)}, u32[]{:S(2)}, u32[]{:S(2)}) collective-permute-start(bf16[3,256,256]{2,1,0:T(8,128)(2,1)} %get-tuple-element.51), channel_id=1, source_target_pairs={{0,4},{4,0},{8,12},{12,8},{16,20},{20,16},{24,28},{28,24},{1,5},{5... | collective-permute-start | bytes 1179656 | tf_op jit(solution)/shard_map/ppermute | solution.py:366
  6.0 17.9 %collective-permute-start.1 = (bf16[3,256,256]{2,1,0:T(8,128)(2,1)}, bf16[3,256,256]{2,1,0:T(8,128)(2,1)S(1)}, u32[]{:S(2)}, u32[]{:S(2)}) collective-permute-start(bf16[3,256,256]{2,1,0:T(8,128)(2,1)} %get-tuple-element.52), channel_id=1, source_target_pairs={{0,8},{4,12},{8,0},{12,4},{16,24},{20,28},{24,16},{28,20},{1,9},{5... | collective-permute-start | bytes 1179656 | tf_op jit(solution)/shard_map/ppermute | solution.py:366
  7.5 23.9 %collective-permute-start.2 = (bf16[3,256,256]{2,1,0:T(8,128)(2,1)}, bf16[3,256,256]{2,1,0:T(8,128)(2,1)S(1)}, u32[]{:S(2)}, u32[]{:S(2)}) collective-permute-start(bf16[3,256,256]{2,1,0:T(8,128)(2,1)} %get-tuple-element.53), channel_id=1, source_target_pairs={{0,12},{4,8},{8,4},{12,0},{16,28},{20,24},{24,20},{28,16},{1,13},{... | collective-permute-start | bytes 1179656 | tf_op jit(solution)/shard_map/ppermute | solution.py:366
  7.5 26.8 %collective-permute-start.3 = (bf16[2,256,128]{2,1,0:T(8,128)(2,1)}, bf16[2,256,128]{2,1,0:T(8,128)(2,1)S(1)}, u32[]{:S(2)}, u32[]{:S(2)}) collective-permute-start(bf16[2,256,128]{2,1,0:T(8,128)(2,1)} %get-tuple-element.59), channel_id=1, source_target_pairs={{0,16},{4,20},{8,24},{12,28},{16,0},{20,4},{24,8},{28,12},{1,17},{... | collective-permute-start | bytes 393224 | tf_op jit(solution)/shard_map/ppermute | solution.py:368
  10.5 23.9 %collective-permute-start.4 = (bf16[2,256,128]{2,1,0:T(8,128)(2,1)}, bf16[2,256,128]{2,1,0:T(8,128)(2,1)S(1)}, u32[]{:S(2)}, u32[]{:S(2)}) collective-permute-start(bf16[2,256,128]{2,1,0:T(8,128)(2,1)} %get-tuple-element.60), channel_id=1, source_target_pairs={{0,20},{4,16},{8,28},{12,24},{16,4},{20,0},{24,12},{28,8},{1,21},{... | collective-permute-start | bytes 393224 | tf_op jit(solution)/shard_map/ppermute | solution.py:368
  18.1 19.0 %collective-permute-start.5 = (bf16[2,256,128]{2,1,0:T(8,128)(2,1)}, bf16[2,256,128]{2,1,0:T(8,128)(2,1)S(1)}, u32[]{:S(2)}, u32[]{:S(2)}) collective-permute-start(bf16[2,256,128]{2,1,0:T(8,128)(2,1)} %get-tuple-element.61), channel_id=1, source_target_pairs={{0,24},{4,28},{8,16},{12,20},{16,8},{20,12},{24,0},{28,4},{1,25},{... | collective-permute-start | bytes 393224 | tf_op jit(solution)/shard_map/ppermute | solution.py:368
  23.8 14.6 %collective-permute-start.6 = (bf16[2,256,128]{2,1,0:T(8,128)(2,1)}, bf16[2,256,128]{2,1,0:T(8,128)(2,1)S(1)}, u32[]{:S(2)}, u32[]{:S(2)}) collective-permute-start(bf16[2,256,128]{2,1,0:T(8,128)(2,1)} %get-tuple-element.62), channel_id=1, source_target_pairs={{0,28},{4,24},{8,20},{12,16},{16,12},{20,8},{24,4},{28,0},{1,29},{... | collective-permute-start | bytes 393224 | tf_op jit(solution)/shard_map/ppermute | solution.py:368
  27.4 4.1 %copy-start = (bf16[3,256,256]{2,1,0:T(8,128)(2,1)S(1)}, bf16[3,256,256]{2,1,0:T(8,128)(2,1)}, u32[]{:S(2)}) copy-start(bf16[3,256,256]{2,1,0:T(8,128)(2,1)} %get-tuple-element.50.refs_0_) | copy-start | bytes 1179652
  41.0 9.6 %collective-permute-start.7 = (bf16[272,256]{1,0:T(8,128)(2,1)S(1)}, bf16[272,256]{1,0:T(8,128)(2,1)S(1)}, u32[]{:S(2)}, u32[]{:S(2)}) collective-permute-start(bf16[272,256]{1,0:T(8,128)(2,1)S(1)} %get-tuple-element.68), channel_id=1, source_target_pairs={{0,4},{4,0},{8,12},{12,8},{16,20},{20,16},{24,28},{28,24},{1,5},{5... | collective-permute-start | bytes 417800 | tf_op jit(solution)/shard_map/ppermute | solution.py:399
  42.6 9.4 %collective-permute-start.8 = (bf16[272,128]{1,0:T(8,128)(2,1)S(1)}, bf16[272,128]{1,0:T(8,128)(2,1)S(1)}, u32[]{:S(2)}, u32[]{:S(2)}) collective-permute-start(bf16[272,128]{1,0:T(8,128)(2,1)S(1)} %get-tuple-element.71), channel_id=1, source_target_pairs={{0,16},{4,20},{8,24},{12,28},{1,17},{5,21},{9,25},{13,29},{2,18},{... | collective-permute-start | bytes 208904 | tf_op jit(solution)/shard_map/ppermute | solution.py:403
  46.4 7.9 %collective-permute-start.12 = (bf16[272,256]{1,0:T(8,128)(2,1)S(1)}, bf16[272,256]{1,0:T(8,128)(2,1)S(1)}, u32[]{:S(2)}, u32[]{:S(2)}) collective-permute-start(bf16[272,256]{1,0:T(8,128)(2,1)S(1)} %get-tuple-element.75), channel_id=1, source_target_pairs={{0,8},{4,12},{8,0},{12,4},{16,24},{20,28},{24,16},{28,20},{1,9},{5... | collective-permute-start | bytes 417800 | tf_op jit(solution)/shard_map/ppermute | solution.py:399
  46.6 7.7 %collective-permute-start.13 = (bf16[272,256]{1,0:T(8,128)(2,1)S(1)}, bf16[272,256]{1,0:T(8,128)(2,1)S(1)}, u32[]{:S(2)}, u32[]{:S(2)}) collective-permute-start(bf16[272,256]{1,0:T(8,128)(2,1)S(1)} %get-tuple-element.76), channel_id=1, source_target_pairs={{0,12},{4,8},{8,4},{12,0},{16,28},{20,24},{24,20},{28,16},{1,13},{... | collective-permute-start | bytes 417800 | tf_op jit(solution)/shard_map/ppermute | solution.py:399
  48.5 5.7 %collective-permute-start.9 = (bf16[272,128]{1,0:T(8,128)(2,1)S(1)}, bf16[272,128]{1,0:T(8,128)(2,1)S(1)}, u32[]{:S(2)}, u32[]{:S(2)}) collective-permute-start(bf16[272,128]{1,0:T(8,128)(2,1)S(1)} %get-tuple-element.72), channel_id=1, source_target_pairs={{0,20},{4,16},{8,28},{12,24},{1,21},{5,17},{9,29},{13,25},{2,22},{... | collective-permute-start | bytes 208904 | tf_op jit(solution)/shard_map/ppermute | solution.py:403
  50.7 4.3 %collective-permute-start.11 = (bf16[272,128]{1,0:T(8,128)(2,1)S(1)}, bf16[272,128]{1,0:T(8,128)(2,1)S(1)}, u32[]{:S(2)}, u32[]{:S(2)}) collective-permute-start(bf16[272,128]{1,0:T(8,128)(2,1)S(1)} %get-tuple-element.74), channel_id=1, source_target_pairs={{0,28},{4,24},{8,20},{12,16},{1,29},{5,25},{9,21},{13,17},{2,30},{... | collective-permute-start | bytes 208904 | tf_op jit(solution)/shard_map/ppermute | solution.py:403
  52.0 3.8 %collective-permute-start.10 = (bf16[272,128]{1,0:T(8,128)(2,1)S(1)}, bf16[272,128]{1,0:T(8,128)(2,1)S(1)}, u32[]{:S(2)}, u32[]{:S(2)}) collective-permute-start(bf16[272,128]{1,0:T(8,128)(2,1)S(1)} %get-tuple-element.73), channel_id=1, source_target_pairs={{0,24},{4,28},{8,16},{12,20},{1,25},{5,29},{9,17},{13,21},{2,26},{... | collective-permute-start | bytes 208904 | tf_op jit(solution)/shard_map/ppermute | solution.py:403
  57.6 2.7 %collective-permute-start.14 = (bf16[256,2048]{1,0:T(8,128)(2,1)S(1)}, bf16[256,2048]{1,0:T(8,128)(2,1)S(1)}, u32[]{:S(2)}, u32[]{:S(2)}) collective-permute-start(bf16[256,2048]{1,0:T(8,128)(2,1)S(1)} %get-tuple-element.87), channel_id=1, source_target_pairs={{0,1},{1,0},{2,3},{3,2},{4,5},{5,4},{6,7},{7,6},{8,9},{9,8},{10,11... | collective-permute-start | bytes 3145736 | tf_op jit(solution)/shard_map/ppermute | solution.py:426
  60.7 25.3 %collective-permute-start.17 = (bf16[256,2048]{1,0:T(8,128)(2,1)S(1)}, bf16[256,2048]{1,0:T(8,128)(2,1)S(1)}, u32[]{:S(2)}, u32[]{:S(2)}) collective-permute-start(bf16[256,2048]{1,0:T(8,128)(2,1)S(1)} %add_convert_fusion.1), channel_id=1, source_target_pairs={{0,2},{1,3},{2,0},{3,1},{4,6},{5,7},{6,4},{7,5},{8,10},{9,11},{10,... | collective-permute-start | bytes 3145736 | tf_op jit(solution)/shard_map/ppermute | solution.py:427
  68.9 2.0 %collective-permute-start.15 = (bf16[256,1024]{1,0:T(8,128)(2,1)S(1)}, bf16[256,1024]{1,0:T(8,128)(2,1)S(1)}, u32[]{:S(2)}, u32[]{:S(2)}) collective-permute-start(bf16[256,1024]{1,0:T(8,128)(2,1)S(1)} %get-tuple-element.95), channel_id=1, source_target_pairs={{0,1},{1,0},{2,3},{3,2},{4,5},{5,4},{6,7},{7,6},{8,9},{9,8},{10,11... | collective-permute-start | bytes 1572872 | tf_op jit(solution)/shard_map/ppermute | solution.py:433
  69.0 2.6 %collective-permute-start.16 = (bf16[256,1024]{1,0:T(8,128)(2,1)S(1)}, bf16[256,1024]{1,0:T(8,128)(2,1)S(1)}, u32[]{:S(2)}, u32[]{:S(2)}) collective-permute-start(bf16[256,1024]{1,0:T(8,128)(2,1)S(1)} %get-tuple-element.96), channel_id=1, source_target_pairs={{0,1},{1,0},{2,3},{3,2},{4,5},{5,4},{6,7},{7,6},{8,9},{9,8},{10,11... | collective-permute-start | bytes 1572872 | tf_op jit(solution)/shard_map/ppermute | solution.py:433

commit v5 on v4

--- a/solution.py
+++ b/solution.py
@@ -10,6 +10,7 @@
 HD = 128
 MIB = 1 << 20
 OWN_PARTS = 2
+STEPS = 4
 STAT_ROWS = 16
 T2TIE = (2, 3)
 LOG2E = 1.4426950408889634
@@ -275,6 +276,24 @@
     count = len(refs) // 2
     for weight, out in zip(refs[:count], refs[count:]):
         multiply(heads, weight, out, tile)
+
+
+def last_kernel(keep, *refs):
+    swapped, (whole, out, held, sem) = refs[:OWN_PARTS], refs[OWN_PARTS:]
+    rows, cols = keep.shape
+    step, wide = rows // STEPS, cols // OWN_PARTS
+    copies = []
+    for i in range(STEPS):
+        at = slice(i * step, (i + 1) * step)
+        for j, part in enumerate(swapped):
+            here = slice(j * wide, (j + 1) * wide)
+            total = keep[at, here].astype(jnp.float32) + part[at, :].astype(jnp.float32)
+            held[at, here] = (total + whole[at, here].astype(jnp.float32)).astype(jnp.bfloat16)
+        rows_at = pl.ds(i * step, step)
+        copies.append(pltpu.make_async_copy(held.at[rows_at], out.at[rows_at], sem.at[i]))
+        copies[-1].start()
+    for one in copies:
+        one.wait()
 
 
 def project(heads, weights):
@@ -432,10 +451,21 @@
     swapped = [
         lax.ppermute(give[:, at : at + piece], "tp", swap) for at in range(0, cols, piece)
     ]
-    total = keep.astype(f32) + jnp.concatenate(swapped, axis=1).astype(f32)
-    for one in crossing:
-        total += one.astype(f32)
-    return total.astype(bf16)
+    whole = crossing[0]
+    if len(crossing) > 1:
+        whole = sum(one.astype(f32) for one in crossing)
+    return pl.pallas_call(
+        last_kernel,
+        in_specs=[VMEM] * (2 + OWN_PARTS),
+        out_specs=pl.BlockSpec(memory_space=pl.ANY),
+        out_shape=jax.ShapeDtypeStruct((rows, cols), bf16),
+        scratch_shapes=[
+            pltpu.VMEM((rows, cols), bf16),
+            pltpu.SemaphoreType.DMA((STEPS,)),
+        ],
+        compiler_params=params(16),
+        cost_estimate=COST,
+    )(keep, *swapped, whole)
 
 
 def solution(mesh):

time: 87.9 us -> 87.5 us (level)
  other arithmetic: 2.05 us -> 0.56 us
  Pallas kernels: 21.9 us -> 23 us
    convert_element_type x1 -> x0, other arithmetic: 1.49 us -> none  [heads_form(): return total.astype(bf16)]
    pallas_call x0 -> x1, Pallas kernels: none -> 1.11 us  [heads_form(): pl.pallas_call(last_kernel, in_specs=[VMEM] * (2 + OWN_PARTS), out_specs=...]
where the time goes in v5:
time: 87.5 us; the launch traced here: 87.1 us
  waiting for transfers between devices  32.7 us (37%)
  starting transfers between devices  30.6 us (35%)
  Pallas kernels  23 us (26%)
    ppermute x1, waiting for transfers between devices, heads_form(): crossing.append(lax.ppermute(both, 'tp', perm))  14.4 us
    ppermute x4, starting transfers between devices, heads_form(): lax.ppermute(piece, 'ctx', between(shift, 1, 1))  11.5 us
    ppermute x4, starting transfers between devices, heads_form(): over[shift] = lax.ppermute(over[shift], 'ctx', between(shift, 1, 0))  8.52 us
    ppermute x3, waiting for transfers between devices, heads_form(): inner[shift] = lax.ppermute(inner[shift], 'ctx', within(shift))  8.24 us
    pallas_call x2, Pallas kernels, fetch(): pl.pallas_call(fetch_kernel, in_specs=[pl.BlockSpec(memory_space=pltpu.SM...  8.07 us
    ppermute x3, starting transfers between devices, heads_form(): inner[shift] = lax.ppermute(inner[shift], 'ctx', within(shift))  4.58 us
    ppermute x4, waiting for transfers between devices, heads_form(): lax.ppermute(piece, 'ctx', between(shift, 1, 1))  4.07 us
    ppermute x3, starting transfers between devices, heads_form(): back[shift] = lax.ppermute(back[shift], 'ctx', within(shift))  3.68 us
  transfers between devices with their start and end apart: 18, of which 11 were waited for; matrix products, arithmetic and copies ran while one was open for 0% of the time, Pallas kernels for 17%

profile of v5, /device:TPU:0, one launch (start us, length us, event | category | flops | bytes accessed | tf_op | source)
XLA Modules:
  0.0 87.1 jit_solution(15956318070821211242)
XLA Ops:
  0.0 2.9 %shard_map.46 = (bf16[3,256,256]{2,1,0:T(8,128)(2,1)}, bf16[3,256,256]{2,1,0:T(8,128)(2,1)}, bf16[3,256,256]{2,1,0:T(8,128)(2,1)}, bf16[3,256,256]{2,1,0:T(8,128...) custom-call(s32[1]{0:T(128)} %bitcast.me_ref, ...), custom_call_target="tpu_custom_call" | custom-call | flops 1 | bytes 1 | tf_op jit(solution)/shard_map/pallas_call | solution.py:358
  3.0 3.0 %collective-permute-start = (bf16[3,256,256]{2,1,0:T(8,128)(2,1)}, bf16[3,256,256]{2,1,0:T(8,128)(2,1)S(1)}, u32[]{:S(2)}, u32[]{:S(2)}) collective-permute-start(bf16[3,256,256]{2,1,0:T(8,128)(2,1)} %get-tuple-element.51), channel_id=1, source_target_pairs={{0,4},{4,0},{8,12},{12,8},{16,20},{20,16},{24,28},{28,24},{1,5},{5... | collective-permute-start | bytes 1179656 | tf_op jit(solution)/shard_map/ppermute | solution.py:385
  6.0 1.6 %collective-permute-start.1 = (bf16[3,256,256]{2,1,0:T(8,128)(2,1)}, bf16[3,256,256]{2,1,0:T(8,128)(2,1)S(1)}, u32[]{:S(2)}, u32[]{:S(2)}) collective-permute-start(bf16[3,256,256]{2,1,0:T(8,128)(2,1)} %get-tuple-element.52), channel_id=1, source_target_pairs={{0,8},{4,12},{8,0},{12,4},{16,24},{20,28},{24,16},{28,20},{1,9},{5... | collective-permute-start | bytes 1179656 | tf_op jit(solution)/shard_map/ppermute | solution.py:385
  7.5 2.9 %collective-permute-start.3 = (bf16[2,256,128]{2,1,0:T(8,128)(2,1)}, bf16[2,256,128]{2,1,0:T(8,128)(2,1)S(1)}, u32[]{:S(2)}, u32[]{:S(2)}) collective-permute-start(bf16[2,256,128]{2,1,0:T(8,128)(2,1)} %get-tuple-element.59), channel_id=1, source_target_pairs={{0,16},{4,20},{8,24},{12,28},{16,0},{20,4},{24,8},{28,12},{1,17},{... | collective-permute-start | bytes 393224 | tf_op jit(solution)/shard_map/ppermute | solution.py:387
  11.8 6.3 %collective-permute-done.refs_1_ = bf16[3,256,256]{2,1,0:T(8,128)(2,1)S(1)} collective-permute-done((bf16[3,256,256]{2,1,0:T(8,128)(2,1)}, bf16[3,256,256]{2,1,0:T(8,128)(2,1)S(1)}, u32[]{:S(2)}, u32[]{:S(2)}) %collective-permute-start) | collective-permute-done | bytes 393248 | tf_op jit(solution)/shard_map/ppermute | solution.py:385
  18.1 3.8 %collective-permute-start.5 = (bf16[2,256,128]{2,1,0:T(8,128)(2,1)}, bf16[2,256,128]{2,1,0:T(8,128)(2,1)S(1)}, u32[]{:S(2)}, u32[]{:S(2)}) collective-permute-start(bf16[2,256,128]{2,1,0:T(8,128)(2,1)} %get-tuple-element.61), channel_id=1, source_target_pairs={{0,24},{4,28},{8,16},{12,20},{16,8},{20,12},{24,0},{28,4},{1,25},{... | collective-permute-start | bytes 393224 | tf_op jit(solution)/shard_map/ppermute | solution.py:387
  21.9 2.0 %collective-permute-done.1.refs_2_ = bf16[3,256,256]{2,1,0:T(8,128)(2,1)S(1)} collective-permute-done((bf16[3,256,256]{2,1,0:T(8,128)(2,1)}, bf16[3,256,256]{2,1,0:T(8,128)(2,1)S(1)}, u32[]{:S(2)}, u32[]{:S(2)}) %collective-permute-start.1) | collective-permute-done | bytes 393248 | tf_op jit(solution)/shard_map/ppermute | solution.py:385
  23.8 3.5 %collective-permute-start.6 = (bf16[2,256,128]{2,1,0:T(8,128)(2,1)}, bf16[2,256,128]{2,1,0:T(8,128)(2,1)S(1)}, u32[]{:S(2)}, u32[]{:S(2)}) collective-permute-start(bf16[2,256,128]{2,1,0:T(8,128)(2,1)} %get-tuple-element.62), channel_id=1, source_target_pairs={{0,28},{4,24},{8,20},{12,16},{16,12},{20,8},{24,4},{28,0},{1,29},{... | collective-permute-start | bytes 393224 | tf_op jit(solution)/shard_map/ppermute | solution.py:387
  27.4 4.0 %shard_map.47 = (bf16[1024,2048]{1,0:T(8,128)(2,1)S(1)}, bf16[1024,2048]{1,0:T(8,128)(2,1)S(1)}) custom-call(s32[3]{0:T(128)S(1)} %pad_add_fusion.place_ref, bf16[1024,8192]{1,0:T(8,128)(2,1)} %w_ref.2), custom_call_target="tpu_custom_call" | custom-call | flops 1 | bytes 16777216 | tf_op jit(solution)/shard_map/pallas_call | solution.py:326
  31.5 2.9 %shard_map.48 = (f32[1024,256]{1,0:T(8,128)S(1)}, f32[256,128]{1,0:T(8,128)S(1)}) custom-call(s32[1]{0:T(128)} %bitcast.me_ref, bf16[3,256,256]{2,1,0:T(8,128)(2,1)S(1)} %copy-done, bf16[3,256,256]{2,1,0:T(8,128)(2,1)S(1)} %collective-permute-done.refs_1_, bf16[3,256,256]{2,1,0:T(8,128)(2,1)S(1)} %collective-permute-done.1.refs_2_, ...), custom_call_target="tpu_custom_call" | custom-call | flops 1 | bytes 1 | tf_op jit(solution)/shard_map/pallas_call | solution.py:395
  34.4 2.7 %collective-permute-done.5.refs_6_ = bf16[2,256,128]{2,1,0:T(8,128)(2,1)S(1)} collective-permute-done((bf16[2,256,128]{2,1,0:T(8,128)(2,1)}, bf16[2,256,128]{2,1,0:T(8,128)(2,1)S(1)}, u32[]{:S(2)}, u32[]{:S(2)}) %collective-permute-start.5) | collective-permute-done | bytes 131104 | tf_op jit(solution)/shard_map/ppermute | solution.py:387
  37.0 1.4 %collective-permute-done.6.refs_7_ = bf16[2,256,128]{2,1,0:T(8,128)(2,1)S(1)} collective-permute-done((bf16[2,256,128]{2,1,0:T(8,128)(2,1)}, bf16[2,256,128]{2,1,0:T(8,128)(2,1)S(1)}, u32[]{:S(2)}, u32[]{:S(2)}) %collective-permute-start.6) | collective-permute-done | bytes 131104 | tf_op jit(solution)/shard_map/ppermute | solution.py:387
  38.4 2.6 %shard_map.49 = (bf16[272,256]{1,0:T(8,128)(2,1)S(1)}, bf16[272,256]{1,0:T(8,128)(2,1)S(1)}, bf16[272,256]{1,0:T(8,128)(2,1)S(1)}, bf16[272,256]{1,0:T(8,128)(2,...) custom-call(s32[1]{0:T(128)} %bitcast.me_ref, ...), custom_call_target="tpu_custom_call" | custom-call | flops 1 | bytes 1 | tf_op jit(solution)/shard_map/pallas_call | solution.py:407
  41.0 1.6 %collective-permute-start.7 = (bf16[272,256]{1,0:T(8,128)(2,1)S(1)}, bf16[272,256]{1,0:T(8,128)(2,1)S(1)}, u32[]{:S(2)}, u32[]{:S(2)}) collective-permute-start(bf16[272,256]{1,0:T(8,128)(2,1)S(1)} %get-tuple-element.68), channel_id=1, source_target_pairs={{0,4},{4,0},{8,12},{12,8},{16,20},{20,16},{24,28},{28,24},{1,5},{5... | collective-permute-start | bytes 417800 | tf_op jit(solution)/shard_map/ppermute | solution.py:418
  42.6 3.8 %collective-permute-start.8 = (bf16[272,128]{1,0:T(8,128)(2,1)S(1)}, bf16[272,128]{1,0:T(8,128)(2,1)S(1)}, u32[]{:S(2)}, u32[]{:S(2)}) collective-permute-start(bf16[272,128]{1,0:T(8,128)(2,1)S(1)} %get-tuple-element.71), channel_id=1, source_target_pairs={{0,16},{4,20},{8,24},{12,28},{1,17},{5,21},{9,25},{13,29},{2,18},{... | collective-permute-start | bytes 208904 | tf_op jit(solution)/shard_map/ppermute | solution.py:422
  46.6 1.9 %collective-permute-start.13 = (bf16[272,256]{1,0:T(8,128)(2,1)S(1)}, bf16[272,256]{1,0:T(8,128)(2,1)S(1)}, u32[]{:S(2)}, u32[]{:S(2)}) collective-permute-start(bf16[272,256]{1,0:T(8,128)(2,1)S(1)} %get-tuple-element.76), channel_id=1, source_target_pairs={{0,12},{4,8},{8,4},{12,0},{16,28},{20,24},{24,20},{28,16},{1,13},{... | collective-permute-start | bytes 417800 | tf_op jit(solution)/shard_map/ppermute | solution.py:418
  48.5 2.1 %collective-permute-start.9 = (bf16[272,128]{1,0:T(8,128)(2,1)S(1)}, bf16[272,128]{1,0:T(8,128)(2,1)S(1)}, u32[]{:S(2)}, u32[]{:S(2)}) collective-permute-start(bf16[272,128]{1,0:T(8,128)(2,1)S(1)} %get-tuple-element.72), channel_id=1, source_target_pairs={{0,20},{4,16},{8,28},{12,24},{1,21},{5,17},{9,29},{13,25},{2,22},{... | collective-permute-start | bytes 208904 | tf_op jit(solution)/shard_map/ppermute | solution.py:422
  55.8 1.8 %shard_map.50 = (bf16[256,1024]{1,0:T(8,128)(2,1)S(1)}, bf16[256,2048]{1,0:T(8,128)(2,1)S(1)}) custom-call(s32[1]{0:T(128)} %bitcast.me_ref, bf16[272,256]{1,0:T(8,128)(2,1)S(1)} %get-tuple-element.65.refs_0_, bf16[272,256]{1,0:T(8,128)(2,1)S(1)} %collective-permute-done.7.refs_1_, bf16[272,256]{1,0:T(8,128)(2,1)S(1)} %collective-permute-done.12.refs_2_, ...), custom_call_target="tpu_custom_call" | custom-call | flops 1 | bytes 1 | tf_op jit(solution)/shard_map/pallas_call | solution.py:431
  58.9 1.4 %collective-permute-done.14 = bf16[256,2048]{1,0:T(8,128)(2,1)S(1)} collective-permute-done((bf16[256,2048]{1,0:T(8,128)(2,1)S(1)}, bf16[256,2048]{1,0:T(8,128)(2,1)S(1)}, u32[]{:S(2)}, u32[]{:S(2)}) %collective-permute-start.14) | collective-permute-done | bytes 1048608 | tf_op jit(solution)/shard_map/ppermute | solution.py:445
  60.7 1.6 %collective-permute-start.17 = (bf16[256,2048]{1,0:T(8,128)(2,1)S(1)}, bf16[256,2048]{1,0:T(8,128)(2,1)S(1)}, u32[]{:S(2)}, u32[]{:S(2)}) collective-permute-start(bf16[256,2048]{1,0:T(8,128)(2,1)S(1)} %add_convert_fusion), channel_id=1, source_target_pairs={{0,2},{1,3},{2,0},{3,1},{4,6},{5,7},{6,4},{7,5},{8,10},{9,11},{10,... | collective-permute-start | bytes 3145736 | tf_op jit(solution)/shard_map/ppermute | solution.py:446
  62.4 4.0 %shard_map.52 = (bf16[1024,2048]{1,0:T(8,128)(2,1)S(1)}, bf16[1024,2048]{1,0:T(8,128)(2,1)S(1)}) custom-call(s32[3]{0:T(128)S(1)} %pad_add_fusion.1.place_ref, bf16[1024,8192]{1,0:T(8,128)(2,1)} %w_ref.2), custom_call_target="tpu_custom_call" | custom-call | flops 1 | bytes 16777216 | tf_op jit(solution)/shard_map/pallas_call | solution.py:326
  66.4 2.4 %shard_map.53 = (bf16[256,2048]{1,0:T(8,128)(2,1)S(1)}, bf16[256,2048]{1,0:T(8,128)(2,1)S(1)}) custom-call(bf16[256,1024]{1,0:T(8,128)(2,1)S(1)} %get-tuple-element.89.heads, bf16[1024,2048]{1,0:T(8,128)(2,1)S(1)} %get-tuple-element.91.refs_0_, bf16[1024,2048]{1,0:T(8,128)(2,1)S(1)} %get-tuple-element.92.refs_1_), custom_call_target="tpu_custom_call" | custom-call | flops 1 | bytes 1 | tf_op jit(solution)/shard_map/pallas_call | solution.py:301
  69.5 1.4 %collective-permute-done.16.refs_1_ = bf16[256,1024]{1,0:T(8,128)(2,1)S(1)} collective-permute-done((bf16[256,1024]{1,0:T(8,128)(2,1)S(1)}, bf16[256,1024]{1,0:T(8,128)(2,1)S(1)}, u32[]{:S(2)}, u32[]{:S(2)}) %collective-permute-start.16) | collective-permute-done | bytes 524320 | tf_op jit(solution)/shard_map/ppermute | solution.py:452
  71.6 14.4 %collective-permute-done.17.refs_2_ = bf16[256,2048]{1,0:T(8,128)(2,1)S(1)} collective-permute-done((bf16[256,2048]{1,0:T(8,128)(2,1)S(1)}, bf16[256,2048]{1,0:T(8,128)(2,1)S(1)}, u32[]{:S(2)}, u32[]{:S(2)}) %collective-permute-start.17) | collective-permute-done | bytes 1048608 | tf_op jit(solution)/shard_map/ppermute | solution.py:446
  (27 shorter events, 11.0 us)
Async XLA Ops:
  3.0 15.1 %collective-permute-start = (bf16[3,256,256]{2,1,0:T(8,128)(2,1)}, bf16[3,256,256]{2,1,0:T(8,128)(2,1)S(1)}, u32[]{:S(2)}, u32[]{:S(2)}) collective-permute-start(bf16[3,256,256]{2,1,0:T(8,128)(2,1)} %get-tuple-element.51), channel_id=1, source_target_pairs={{0,4},{4,0},{8,12},{12,8},{16,20},{20,16},{24,28},{28,24},{1,5},{5... | collective-permute-start | bytes 1179656 | tf_op jit(solution)/shard_map/ppermute | solution.py:385
  6.0 17.9 %collective-permute-start.1 = (bf16[3,256,256]{2,1,0:T(8,128)(2,1)}, bf16[3,256,256]{2,1,0:T(8,128)(2,1)S(1)}, u32[]{:S(2)}, u32[]{:S(2)}) collective-permute-start(bf16[3,256,256]{2,1,0:T(8,128)(2,1)} %get-tuple-element.52), channel_id=1, source_target_pairs={{0,8},{4,12},{8,0},{12,4},{16,24},{20,28},{24,16},{28,20},{1,9},{5... | collective-permute-start | bytes 1179656 | tf_op jit(solution)/shard_map/ppermute | solution.py:385
  7.5 23.9 %collective-permute-start.2 = (bf16[3,256,256]{2,1,0:T(8,128)(2,1)}, bf16[3,256,256]{2,1,0:T(8,128)(2,1)S(1)}, u32[]{:S(2)}, u32[]{:S(2)}) collective-permute-start(bf16[3,256,256]{2,1,0:T(8,128)(2,1)} %get-tuple-element.53), channel_id=1, source_target_pairs={{0,12},{4,8},{8,4},{12,0},{16,28},{20,24},{24,20},{28,16},{1,13},{... | collective-permute-start | bytes 1179656 | tf_op jit(solution)/shard_map/ppermute | solution.py:385
  7.5 26.8 %collective-permute-start.3 = (bf16[2,256,128]{2,1,0:T(8,128)(2,1)}, bf16[2,256,128]{2,1,0:T(8,128)(2,1)S(1)}, u32[]{:S(2)}, u32[]{:S(2)}) collective-permute-start(bf16[2,256,128]{2,1,0:T(8,128)(2,1)} %get-tuple-element.59), channel_id=1, source_target_pairs={{0,16},{4,20},{8,24},{12,28},{16,0},{20,4},{24,8},{28,12},{1,17},{... | collective-permute-start | bytes 393224 | tf_op jit(solution)/shard_map/ppermute | solution.py:387
  10.5 23.9 %collective-permute-start.4 = (bf16[2,256,128]{2,1,0:T(8,128)(2,1)}, bf16[2,256,128]{2,1,0:T(8,128)(2,1)S(1)}, u32[]{:S(2)}, u32[]{:S(2)}) collective-permute-start(bf16[2,256,128]{2,1,0:T(8,128)(2,1)} %get-tuple-element.60), channel_id=1, source_target_pairs={{0,20},{4,16},{8,28},{12,24},{16,4},{20,0},{24,12},{28,8},{1,21},{... | collective-permute-start | bytes 393224 | tf_op jit(solution)/shard_map/ppermute | solution.py:387
  18.1 19.0 %collective-permute-start.5 = (bf16[2,256,128]{2,1,0:T(8,128)(2,1)}, bf16[2,256,128]{2,1,0:T(8,128)(2,1)S(1)}, u32[]{:S(2)}, u32[]{:S(2)}) collective-permute-start(bf16[2,256,128]{2,1,0:T(8,128)(2,1)} %get-tuple-element.61), channel_id=1, source_target_pairs={{0,24},{4,28},{8,16},{12,20},{16,8},{20,12},{24,0},{28,4},{1,25},{... | collective-permute-start | bytes 393224 | tf_op jit(solution)/shard_map/ppermute | solution.py:387
  23.8 14.6 %collective-permute-start.6 = (bf16[2,256,128]{2,1,0:T(8,128)(2,1)}, bf16[2,256,128]{2,1,0:T(8,128)(2,1)S(1)}, u32[]{:S(2)}, u32[]{:S(2)}) collective-permute-start(bf16[2,256,128]{2,1,0:T(8,128)(2,1)} %get-tuple-element.62), channel_id=1, source_target_pairs={{0,28},{4,24},{8,20},{12,16},{16,12},{20,8},{24,4},{28,0},{1,29},{... | collective-permute-start | bytes 393224 | tf_op jit(solution)/shard_map/ppermute | solution.py:387
  27.4 4.1 %copy-start = (bf16[3,256,256]{2,1,0:T(8,128)(2,1)S(1)}, bf16[3,256,256]{2,1,0:T(8,128)(2,1)}, u32[]{:S(2)}) copy-start(bf16[3,256,256]{2,1,0:T(8,128)(2,1)} %get-tuple-element.50.refs_0_) | copy-start | bytes 1179652
  41.0 9.6 %collective-permute-start.7 = (bf16[272,256]{1,0:T(8,128)(2,1)S(1)}, bf16[272,256]{1,0:T(8,128)(2,1)S(1)}, u32[]{:S(2)}, u32[]{:S(2)}) collective-permute-start(bf16[272,256]{1,0:T(8,128)(2,1)S(1)} %get-tuple-element.68), channel_id=1, source_target_pairs={{0,4},{4,0},{8,12},{12,8},{16,20},{20,16},{24,28},{28,24},{1,5},{5... | collective-permute-start | bytes 417800 | tf_op jit(solution)/shard_map/ppermute | solution.py:418
  42.6 9.4 %collective-permute-start.8 = (bf16[272,128]{1,0:T(8,128)(2,1)S(1)}, bf16[272,128]{1,0:T(8,128)(2,1)S(1)}, u32[]{:S(2)}, u32[]{:S(2)}) collective-permute-start(bf16[272,128]{1,0:T(8,128)(2,1)S(1)} %get-tuple-element.71), channel_id=1, source_target_pairs={{0,16},{4,20},{8,24},{12,28},{1,17},{5,21},{9,25},{13,29},{2,18},{... | collective-permute-start | bytes 208904 | tf_op jit(solution)/shard_map/ppermute | solution.py:422
  46.4 7.9 %collective-permute-start.12 = (bf16[272,256]{1,0:T(8,128)(2,1)S(1)}, bf16[272,256]{1,0:T(8,128)(2,1)S(1)}, u32[]{:S(2)}, u32[]{:S(2)}) collective-permute-start(bf16[272,256]{1,0:T(8,128)(2,1)S(1)} %get-tuple-element.75), channel_id=1, source_target_pairs={{0,8},{4,12},{8,0},{12,4},{16,24},{20,28},{24,16},{28,20},{1,9},{5... | collective-permute-start | bytes 417800 | tf_op jit(solution)/shard_map/ppermute | solution.py:418
  46.6 7.7 %collective-permute-start.13 = (bf16[272,256]{1,0:T(8,128)(2,1)S(1)}, bf16[272,256]{1,0:T(8,128)(2,1)S(1)}, u32[]{:S(2)}, u32[]{:S(2)}) collective-permute-start(bf16[272,256]{1,0:T(8,128)(2,1)S(1)} %get-tuple-element.76), channel_id=1, source_target_pairs={{0,12},{4,8},{8,4},{12,0},{16,28},{20,24},{24,20},{28,16},{1,13},{... | collective-permute-start | bytes 417800 | tf_op jit(solution)/shard_map/ppermute | solution.py:418
  48.5 5.7 %collective-permute-start.9 = (bf16[272,128]{1,0:T(8,128)(2,1)S(1)}, bf16[272,128]{1,0:T(8,128)(2,1)S(1)}, u32[]{:S(2)}, u32[]{:S(2)}) collective-permute-start(bf16[272,128]{1,0:T(8,128)(2,1)S(1)} %get-tuple-element.72), channel_id=1, source_target_pairs={{0,20},{4,16},{8,28},{12,24},{1,21},{5,17},{9,29},{13,25},{2,22},{... | collective-permute-start | bytes 208904 | tf_op jit(solution)/shard_map/ppermute | solution.py:422
  50.7 4.3 %collective-permute-start.11 = (bf16[272,128]{1,0:T(8,128)(2,1)S(1)}, bf16[272,128]{1,0:T(8,128)(2,1)S(1)}, u32[]{:S(2)}, u32[]{:S(2)}) collective-permute-start(bf16[272,128]{1,0:T(8,128)(2,1)S(1)} %get-tuple-element.74), channel_id=1, source_target_pairs={{0,28},{4,24},{8,20},{12,16},{1,29},{5,25},{9,21},{13,17},{2,30},{... | collective-permute-start | bytes 208904 | tf_op jit(solution)/shard_map/ppermute | solution.py:422
  52.0 3.8 %collective-permute-start.10 = (bf16[272,128]{1,0:T(8,128)(2,1)S(1)}, bf16[272,128]{1,0:T(8,128)(2,1)S(1)}, u32[]{:S(2)}, u32[]{:S(2)}) collective-permute-start(bf16[272,128]{1,0:T(8,128)(2,1)S(1)} %get-tuple-element.73), channel_id=1, source_target_pairs={{0,24},{4,28},{8,16},{12,20},{1,25},{5,29},{9,17},{13,21},{2,26},{... | collective-permute-start | bytes 208904 | tf_op jit(solution)/shard_map/ppermute | solution.py:422
  57.6 2.7 %collective-permute-start.14 = (bf16[256,2048]{1,0:T(8,128)(2,1)S(1)}, bf16[256,2048]{1,0:T(8,128)(2,1)S(1)}, u32[]{:S(2)}, u32[]{:S(2)}) collective-permute-start(bf16[256,2048]{1,0:T(8,128)(2,1)S(1)} %get-tuple-element.87), channel_id=1, source_target_pairs={{0,1},{1,0},{2,3},{3,2},{4,5},{5,4},{6,7},{7,6},{8,9},{9,8},{10,11... | collective-permute-start | bytes 3145736 | tf_op jit(solution)/shard_map/ppermute | solution.py:445
  60.7 25.3 %collective-permute-start.17 = (bf16[256,2048]{1,0:T(8,128)(2,1)S(1)}, bf16[256,2048]{1,0:T(8,128)(2,1)S(1)}, u32[]{:S(2)}, u32[]{:S(2)}) collective-permute-start(bf16[256,2048]{1,0:T(8,128)(2,1)S(1)} %add_convert_fusion), channel_id=1, source_target_pairs={{0,2},{1,3},{2,0},{3,1},{4,6},{5,7},{6,4},{7,5},{8,10},{9,11},{10,... | collective-permute-start | bytes 3145736 | tf_op jit(solution)/shard_map/ppermute | solution.py:446
  68.9 2.0 %collective-permute-start.16 = (bf16[256,1024]{1,0:T(8,128)(2,1)S(1)}, bf16[256,1024]{1,0:T(8,128)(2,1)S(1)}, u32[]{:S(2)}, u32[]{:S(2)}) collective-permute-start(bf16[256,1024]{1,0:T(8,128)(2,1)S(1)} %get-tuple-element.95), channel_id=1, source_target_pairs={{0,1},{1,0},{2,3},{3,2},{4,5},{5,4},{6,7},{7,6},{8,9},{9,8},{10,11... | collective-permute-start | bytes 1572872 | tf_op jit(solution)/shard_map/ppermute | solution.py:452
  69.0 2.6 %collective-permute-start.15 = (bf16[256,1024]{1,0:T(8,128)(2,1)S(1)}, bf16[256,1024]{1,0:T(8,128)(2,1)S(1)}, u32[]{:S(2)}, u32[]{:S(2)}) collective-permute-start(bf16[256,1024]{1,0:T(8,128)(2,1)S(1)} %get-tuple-element.96), channel_id=1, source_target_pairs={{0,1},{1,0},{2,3},{3,2},{4,5},{5,4},{6,7},{7,6},{8,9},{9,8},{10,11... | collective-permute-start | bytes 1572872 | tf_op jit(solution)/shard_map/ppermute | solution.py:452

commit v6 on v5

--- a/solution.py
+++ b/solution.py
@@ -127,7 +127,8 @@
     for shift in range(half):
         source = place ^ shift
         at = pl.ds(pl.multiple_of(source * rows, rows), rows)
-        out[at, :] = pieces[shift][part, :, cols]
+        piece = pieces[shift][part, :, cols]
+        out[at, : piece.shape[1]] = piece
 
 
 def scores(query, keys):
@@ -137,9 +138,8 @@
 
 def weigh(raw, top, values):
     weights = jnp.exp2((raw - top) * (HD ** (-0.5) * LOG2E))
-    total = jnp.sum(weights, axis=1, keepdims=True)
     acc = jnp.dot(weights.astype(jnp.bfloat16), values, preferred_element_type=jnp.float32)
-    return total, acc
+    return acc[:, HD : HD + 1], acc[:, :HD]
 
 
 def log_sum(top, total):
@@ -147,11 +147,16 @@
 
 
 def inner_kernel(half, me_ref, *refs):
-    inner, (o_ref, table_ref), (q_all, k_all, v_all) = refs[:half], refs[half:-3], refs[-3:]
+    inner, (even_ref, odd_ref, table_ref) = refs[:half], refs[half:-3]
+    q_all, k_all, v_all = refs[-3:]
     rows = inner[0].shape[1]
     place = lax.rem(me_ref[0], half)
-    for part, out in enumerate((q_all, k_all, v_all)):
-        gather(half, place, rows, inner, part, out)
+    gather(half, place, rows, inner, 0, q_all)
+    gather(half, place, rows, inner, 1, k_all)
+    for head in range(2):
+        one = v_all.at[head]
+        gather(half, place, rows, inner, 2, one, slice(head * HD, (head + 1) * HD))
+        one[:, HD:] = jnp.ones((half * rows, HD), jnp.bfloat16)
     diag = lax.broadcasted_iota(jnp.int32, (rows, rows), 1) <= lax.broadcasted_iota(
         jnp.int32, (rows, rows), 0
     )
@@ -167,19 +172,23 @@
             if block:
                 early = scores(query, k_all[0:lo, at])
                 top = jnp.maximum(top, jnp.max(early, axis=1, keepdims=True))
-            total, acc = weigh(last, top, v_all[lo:hi, at])
+            total, acc = weigh(last, top, v_all[head, lo:hi, :])
             if block:
-                total_early, acc_early = weigh(early, top, v_all[0:lo, at])
+                total_early, acc_early = weigh(early, top, v_all[head, 0:lo, :])
                 total, acc = total + total_early, acc + acc_early
-            o_ref[lo:hi, at] = acc / total
+            if head == 0:
+                even_ref[lo:hi, :] = (acc / total).astype(jnp.bfloat16)
+            else:
+                odd_ref[lo:hi, :] = acc / total
             table = jnp.where(lane == head * half + block, log_sum(top, total), table)
     table_ref[...] = table
 
 
 def cross_kernel(half, me_ref, *refs):
-    inner, cross, (o_ref, table_ref) = refs[:half], refs[half : 2 * half], refs[2 * half : 2 * half + 2]
-    back, over = refs[2 * half + 2 : 3 * half + 2], refs[3 * half + 2 : 4 * half + 2]
-    q_x, k_x, v_x, o_all, o_x, stats = refs[4 * half + 2 :]
+    inner, cross, refs = refs[:half], refs[half : 2 * half], refs[2 * half :]
+    (even_ref, odd_ref, table_ref), refs = refs[:3], refs[3:]
+    back, over = refs[:half], refs[half : 2 * half]
+    q_x, k_x, v_x, o_odd, o_x, stats = refs[2 * half :]
     rows = inner[0].shape[1]
     upper, place = me_ref[0] // half, lax.rem(me_ref[0], half)
 
@@ -195,6 +204,7 @@
         gather(half, place, rows, cross, 0, k_x)
         gather(half, place, rows, cross, 1, v_x)
 
+    v_x[:, HD:] = jnp.ones((half * rows, HD), jnp.bfloat16)
     lane = lax.broadcasted_iota(jnp.int32, (rows, HD), 1)
     logs = table_ref[...]
     table = logs
@@ -209,16 +219,17 @@
         table = jnp.where(lane == half + block, log_x, table)
         gap = jnp.where(upper == 1, log_x - logs[:, half + block : half + block + 1], -1e30)
         near, far = 1.0 / (1.0 + jnp.exp2(gap)), 1.0 / (1.0 + jnp.exp2(-gap))
-        o_all[lo:hi, :HD] = o_ref[lo:hi, :HD].astype(jnp.bfloat16)
-        o_all[lo:hi, HD:] = (near * o_ref[lo:hi, HD:] + far * result).astype(jnp.bfloat16)
+        o_odd[lo:hi, :] = (near * odd_ref[lo:hi, :] + far * result).astype(jnp.bfloat16)
     turned = jnp.transpose(table)
     for i, part in enumerate(split3(turned[0 : 2 * half, :])):
         stats[i] = part.astype(jnp.float32)
     for shift in range(half):
         goal = place ^ shift
         at = pl.ds(pl.multiple_of(goal * rows, rows), rows)
-        for out, source, first in ((back[shift], o_all, 0), (over[shift], o_x, half)):
-            out[0:rows, :] = source[at, :]
+        back[shift][0:rows, :HD] = even_ref[at, :]
+        back[shift][0:rows, HD:] = o_odd[at, :]
+        over[shift][0:rows, :] = o_x[at, :]
+        for out, first in ((back[shift], 0), (over[shift], half)):
             wide = out.shape[1]
             lines = [stats[i, pl.ds(first + goal, 1), :] for i in range(3)]
             lines = [line[:, at : at + wide] for line in lines for at in range(0, rows, wide)]
@@ -395,21 +406,22 @@
     results = pl.pallas_call(
         functools.partial(inner_kernel, half),
         in_specs=[smem] + [VMEM] * half,
-        out_specs=[VMEM] * 2,
+        out_specs=[VMEM] * 3,
         out_shape=[
-            jax.ShapeDtypeStruct((half * rows, 2 * HD), f32),
+            jax.ShapeDtypeStruct((half * rows, HD), bf16),
+            jax.ShapeDtypeStruct((half * rows, HD), f32),
             jax.ShapeDtypeStruct((rows, HD), f32),
         ],
-        scratch_shapes=[big] * 3,
+        scratch_shapes=[big] * 2 + [pltpu.VMEM((2, half * rows, 2 * HD), bf16)],
         compiler_params=params(24),
         cost_estimate=COST,
     )(place, *inner)
     outs = pl.pallas_call(
         functools.partial(cross_kernel, half),
-        in_specs=[smem] + [VMEM] * (n + 2),
+        in_specs=[smem] + [VMEM] * (n + 3),
         out_specs=[VMEM] * n,
         out_shape=[back_shape] * half + [over_shape] * half,
-        scratch_shapes=[small] * 3 + [big, small, pltpu.VMEM((3, n, rows), f32)],
+        scratch_shapes=[small] * 2 + [big] + [small] * 2 + [ pltpu.VMEM((3, n, rows), f32)],
         compiler_params=params(24),
         cost_estimate=COST,
     )(place, *inner, *cross, *results)

time: 87.5 us -> 87.2 us (level)
  no operation moved by 1% of the time
where the time goes in v6:
time: 87.2 us; the launch traced here: 86.8 us
  waiting for transfers between devices  32.6 us (37%)
  starting transfers between devices  30.6 us (35%)
  Pallas kernels  22.8 us (26%)
    ppermute x1, waiting for transfers between devices, heads_form(): crossing.append(lax.ppermute(both, 'tp', perm))  14.4 us
    ppermute x4, starting transfers between devices, heads_form(): lax.ppermute(piece, 'ctx', between(shift, 1, 1))  11.5 us
    ppermute x4, starting transfers between devices, heads_form(): over[shift] = lax.ppermute(over[shift], 'ctx', between(shift, 1, 0))  8.55 us
    ppermute x3, waiting for transfers between devices, heads_form(): inner[shift] = lax.ppermute(inner[shift], 'ctx', within(shift))  8.24 us
    pallas_call x2, Pallas kernels, fetch(): pl.pallas_call(fetch_kernel, in_specs=[pl.BlockSpec(memory_space=pltpu.SM...  8.07 us
    ppermute x3, starting transfers between devices, heads_form(): inner[shift] = lax.ppermute(inner[shift], 'ctx', within(shift))  4.58 us
    ppermute x4, waiting for transfers between devices, heads_form(): lax.ppermute(piece, 'ctx', between(shift, 1, 1))  3.96 us
    ppermute x3, starting transfers between devices, heads_form(): back[shift] = lax.ppermute(back[shift], 'ctx', within(shift))  3.69 us
  transfers between devices with their start and end apart: 18, of which 11 were waited for; matrix products, arithmetic and copies ran while one was open for 0% of the time, Pallas kernels for 17%

profile of v6, /device:TPU:0, one launch (start us, length us, event | category | flops | bytes accessed | tf_op | source)
XLA Modules:
  0.0 86.8 jit_solution(10773495470633594310)
XLA Ops:
  0.0 2.9 %shard_map.46 = (bf16[3,256,256]{2,1,0:T(8,128)(2,1)}, bf16[3,256,256]{2,1,0:T(8,128)(2,1)}, bf16[3,256,256]{2,1,0:T(8,128)(2,1)}, bf16[3,256,256]{2,1,0:T(8,128...) custom-call(s32[1]{0:T(128)} %bitcast.me_ref, ...), custom_call_target="tpu_custom_call" | custom-call | flops 1 | bytes 1 | tf_op jit(solution)/shard_map/pallas_call | solution.py:369
  3.0 3.0 %collective-permute-start = (bf16[3,256,256]{2,1,0:T(8,128)(2,1)}, bf16[3,256,256]{2,1,0:T(8,128)(2,1)S(1)}, u32[]{:S(2)}, u32[]{:S(2)}) collective-permute-start(bf16[3,256,256]{2,1,0:T(8,128)(2,1)} %get-tuple-element.52), channel_id=1, source_target_pairs={{0,4},{4,0},{8,12},{12,8},{16,20},{20,16},{24,28},{28,24},{1,5},{5... | collective-permute-start | bytes 1179656 | tf_op jit(solution)/shard_map/ppermute | solution.py:396
  6.0 1.6 %collective-permute-start.1 = (bf16[3,256,256]{2,1,0:T(8,128)(2,1)}, bf16[3,256,256]{2,1,0:T(8,128)(2,1)S(1)}, u32[]{:S(2)}, u32[]{:S(2)}) collective-permute-start(bf16[3,256,256]{2,1,0:T(8,128)(2,1)} %get-tuple-element.53), channel_id=1, source_target_pairs={{0,8},{4,12},{8,0},{12,4},{16,24},{20,28},{24,16},{28,20},{1,9},{5... | collective-permute-start | bytes 1179656 | tf_op jit(solution)/shard_map/ppermute | solution.py:396
  7.5 2.9 %collective-permute-start.3 = (bf16[2,256,128]{2,1,0:T(8,128)(2,1)}, bf16[2,256,128]{2,1,0:T(8,128)(2,1)S(1)}, u32[]{:S(2)}, u32[]{:S(2)}) collective-permute-start(bf16[2,256,128]{2,1,0:T(8,128)(2,1)} %get-tuple-element.60), channel_id=1, source_target_pairs={{0,16},{4,20},{8,24},{12,28},{16,0},{20,4},{24,8},{28,12},{1,17},{... | collective-permute-start | bytes 393224 | tf_op jit(solution)/shard_map/ppermute | solution.py:398
  11.8 6.3 %collective-permute-done.refs_1_ = bf16[3,256,256]{2,1,0:T(8,128)(2,1)S(1)} collective-permute-done((bf16[3,256,256]{2,1,0:T(8,128)(2,1)}, bf16[3,256,256]{2,1,0:T(8,128)(2,1)S(1)}, u32[]{:S(2)}, u32[]{:S(2)}) %collective-permute-start) | collective-permute-done | bytes 393248 | tf_op jit(solution)/shard_map/ppermute | solution.py:396
  18.1 3.8 %collective-permute-start.5 = (bf16[2,256,128]{2,1,0:T(8,128)(2,1)}, bf16[2,256,128]{2,1,0:T(8,128)(2,1)S(1)}, u32[]{:S(2)}, u32[]{:S(2)}) collective-permute-start(bf16[2,256,128]{2,1,0:T(8,128)(2,1)} %get-tuple-element.62), channel_id=1, source_target_pairs={{0,24},{4,28},{8,16},{12,20},{16,8},{20,12},{24,0},{28,4},{1,25},{... | collective-permute-start | bytes 393224 | tf_op jit(solution)/shard_map/ppermute | solution.py:398
  21.9 2.0 %collective-permute-done.1.refs_2_ = bf16[3,256,256]{2,1,0:T(8,128)(2,1)S(1)} collective-permute-done((bf16[3,256,256]{2,1,0:T(8,128)(2,1)}, bf16[3,256,256]{2,1,0:T(8,128)(2,1)S(1)}, u32[]{:S(2)}, u32[]{:S(2)}) %collective-permute-start.1) | collective-permute-done | bytes 393248 | tf_op jit(solution)/shard_map/ppermute | solution.py:396
  23.8 3.5 %collective-permute-start.6 = (bf16[2,256,128]{2,1,0:T(8,128)(2,1)}, bf16[2,256,128]{2,1,0:T(8,128)(2,1)S(1)}, u32[]{:S(2)}, u32[]{:S(2)}) collective-permute-start(bf16[2,256,128]{2,1,0:T(8,128)(2,1)} %get-tuple-element.63), channel_id=1, source_target_pairs={{0,28},{4,24},{8,20},{12,16},{16,12},{20,8},{24,4},{28,0},{1,29},{... | collective-permute-start | bytes 393224 | tf_op jit(solution)/shard_map/ppermute | solution.py:398
  27.4 4.0 %shard_map.47 = (bf16[1024,2048]{1,0:T(8,128)(2,1)S(1)}, bf16[1024,2048]{1,0:T(8,128)(2,1)S(1)}) custom-call(s32[3]{0:T(128)S(1)} %pad_add_fusion.place_ref, bf16[1024,8192]{1,0:T(8,128)(2,1)} %w_ref.2), custom_call_target="tpu_custom_call" | custom-call | flops 1 | bytes 16777216 | tf_op jit(solution)/shard_map/pallas_call | solution.py:337
  31.5 3.0 %shard_map.48 = (bf16[1024,128]{1,0:T(8,128)(2,1)S(1)}, f32[1024,128]{1,0:T(8,128)S(1)}, f32[256,128]{1,0:T(8,128)S(1)}) custom-call(s32[1]{0:T(128)} %bitcast.me_ref, bf16[3,256,256]{2,1,0:T(8,128)(2,1)S(1)} %copy-done, bf16[3,256,256]{2,1,0:T(8,128)(2,1)S(1)} %collective-permute-done.refs_1_, bf16[3,256,256]{2,1,0:T(8,128)(2,1)S(1)} %collective-permute-done.1.refs_2_, ...), custom_call_target="tpu_custom_call" | custom-call | flops 1 | bytes 1 | tf_op jit(solution)/shard_map/pallas_call | solution.py:406
  34.5 2.6 %collective-permute-done.5.refs_6_ = bf16[2,256,128]{2,1,0:T(8,128)(2,1)S(1)} collective-permute-done((bf16[2,256,128]{2,1,0:T(8,128)(2,1)}, bf16[2,256,128]{2,1,0:T(8,128)(2,1)S(1)}, u32[]{:S(2)}, u32[]{:S(2)}) %collective-permute-start.5) | collective-permute-done | bytes 131104 | tf_op jit(solution)/shard_map/ppermute | solution.py:398
  37.0 1.4 %collective-permute-done.6.refs_7_ = bf16[2,256,128]{2,1,0:T(8,128)(2,1)S(1)} collective-permute-done((bf16[2,256,128]{2,1,0:T(8,128)(2,1)}, bf16[2,256,128]{2,1,0:T(8,128)(2,1)S(1)}, u32[]{:S(2)}, u32[]{:S(2)}) %collective-permute-start.6) | collective-permute-done | bytes 131104 | tf_op jit(solution)/shard_map/ppermute | solution.py:398
  38.4 2.2 %shard_map.49 = (bf16[272,256]{1,0:T(8,128)(2,1)S(1)}, bf16[272,256]{1,0:T(8,128)(2,1)S(1)}, bf16[272,256]{1,0:T(8,128)(2,1)S(1)}, bf16[272,256]{1,0:T(8,128)(2,...) custom-call(s32[1]{0:T(128)} %bitcast.me_ref, ...), custom_call_target="tpu_custom_call" | custom-call | flops 1 | bytes 1 | tf_op jit(solution)/shard_map/pallas_call | solution.py:419
  40.6 1.6 %collective-permute-start.7 = (bf16[272,256]{1,0:T(8,128)(2,1)S(1)}, bf16[272,256]{1,0:T(8,128)(2,1)S(1)}, u32[]{:S(2)}, u32[]{:S(2)}) collective-permute-start(bf16[272,256]{1,0:T(8,128)(2,1)S(1)} %get-tuple-element.70), channel_id=1, source_target_pairs={{0,4},{4,0},{8,12},{12,8},{16,20},{20,16},{24,28},{28,24},{1,5},{5... | collective-permute-start | bytes 417800 | tf_op jit(solution)/shard_map/ppermute | solution.py:430
  42.2 3.8 %collective-permute-start.8 = (bf16[272,128]{1,0:T(8,128)(2,1)S(1)}, bf16[272,128]{1,0:T(8,128)(2,1)S(1)}, u32[]{:S(2)}, u32[]{:S(2)}) collective-permute-start(bf16[272,128]{1,0:T(8,128)(2,1)S(1)} %get-tuple-element.73), channel_id=1, source_target_pairs={{0,16},{4,20},{8,24},{12,28},{1,17},{5,21},{9,25},{13,29},{2,18},{... | collective-permute-start | bytes 208904 | tf_op jit(solution)/shard_map/ppermute | solution.py:434
  46.2 1.9 %collective-permute-start.13 = (bf16[272,256]{1,0:T(8,128)(2,1)S(1)}, bf16[272,256]{1,0:T(8,128)(2,1)S(1)}, u32[]{:S(2)}, u32[]{:S(2)}) collective-permute-start(bf16[272,256]{1,0:T(8,128)(2,1)S(1)} %get-tuple-element.78), channel_id=1, source_target_pairs={{0,12},{4,8},{8,4},{12,0},{16,28},{20,24},{24,20},{28,16},{1,13},{... | collective-permute-start | bytes 417800 | tf_op jit(solution)/shard_map/ppermute | solution.py:430
  48.2 2.1 %collective-permute-start.9 = (bf16[272,128]{1,0:T(8,128)(2,1)S(1)}, bf16[272,128]{1,0:T(8,128)(2,1)S(1)}, u32[]{:S(2)}, u32[]{:S(2)}) collective-permute-start(bf16[272,128]{1,0:T(8,128)(2,1)S(1)} %get-tuple-element.74), channel_id=1, source_target_pairs={{0,20},{4,16},{8,28},{12,24},{1,21},{5,17},{9,29},{13,25},{2,22},{... | collective-permute-start | bytes 208904 | tf_op jit(solution)/shard_map/ppermute | solution.py:434
  55.4 1.8 %shard_map.50 = (bf16[256,1024]{1,0:T(8,128)(2,1)S(1)}, bf16[256,2048]{1,0:T(8,128)(2,1)S(1)}) custom-call(s32[1]{0:T(128)} %bitcast.me_ref, bf16[272,256]{1,0:T(8,128)(2,1)S(1)} %get-tuple-element.67.refs_0_, bf16[272,256]{1,0:T(8,128)(2,1)S(1)} %collective-permute-done.7.refs_1_, bf16[272,256]{1,0:T(8,128)(2,1)S(1)} %collective-permute-done.12.refs_2_, ...), custom_call_target="tpu_custom_call" | custom-call | flops 1 | bytes 1 | tf_op jit(solution)/shard_map/pallas_call | solution.py:443
  58.6 1.4 %collective-permute-done.14 = bf16[256,2048]{1,0:T(8,128)(2,1)S(1)} collective-permute-done((bf16[256,2048]{1,0:T(8,128)(2,1)S(1)}, bf16[256,2048]{1,0:T(8,128)(2,1)S(1)}, u32[]{:S(2)}, u32[]{:S(2)}) %collective-permute-start.14) | collective-permute-done | bytes 1048608 | tf_op jit(solution)/shard_map/ppermute | solution.py:457
  60.4 1.6 %collective-permute-start.17 = (bf16[256,2048]{1,0:T(8,128)(2,1)S(1)}, bf16[256,2048]{1,0:T(8,128)(2,1)S(1)}, u32[]{:S(2)}, u32[]{:S(2)}) collective-permute-start(bf16[256,2048]{1,0:T(8,128)(2,1)S(1)} %add_convert_fusion), channel_id=1, source_target_pairs={{0,2},{1,3},{2,0},{3,1},{4,6},{5,7},{6,4},{7,5},{8,10},{9,11},{10,... | collective-permute-start | bytes 3145736 | tf_op jit(solution)/shard_map/ppermute | solution.py:458
  62.0 4.0 %shard_map.52 = (bf16[1024,2048]{1,0:T(8,128)(2,1)S(1)}, bf16[1024,2048]{1,0:T(8,128)(2,1)S(1)}) custom-call(s32[3]{0:T(128)S(1)} %pad_add_fusion.1.place_ref, bf16[1024,8192]{1,0:T(8,128)(2,1)} %w_ref.2), custom_call_target="tpu_custom_call" | custom-call | flops 1 | bytes 16777216 | tf_op jit(solution)/shard_map/pallas_call | solution.py:337
  66.1 2.4 %shard_map.53 = (bf16[256,2048]{1,0:T(8,128)(2,1)S(1)}, bf16[256,2048]{1,0:T(8,128)(2,1)S(1)}) custom-call(bf16[256,1024]{1,0:T(8,128)(2,1)S(1)} %get-tuple-element.91.heads, bf16[1024,2048]{1,0:T(8,128)(2,1)S(1)} %get-tuple-element.93.refs_0_, bf16[1024,2048]{1,0:T(8,128)(2,1)S(1)} %get-tuple-element.94.refs_1_), custom_call_target="tpu_custom_call" | custom-call | flops 1 | bytes 1 | tf_op jit(solution)/shard_map/pallas_call | solution.py:312
  69.1 1.4 %collective-permute-done.16.refs_1_ = bf16[256,1024]{1,0:T(8,128)(2,1)S(1)} collective-permute-done((bf16[256,1024]{1,0:T(8,128)(2,1)S(1)}, bf16[256,1024]{1,0:T(8,128)(2,1)S(1)}, u32[]{:S(2)}, u32[]{:S(2)}) %collective-permute-start.16) | collective-permute-done | bytes 524320 | tf_op jit(solution)/shard_map/ppermute | solution.py:464
  71.3 14.4 %collective-permute-done.17.refs_2_ = bf16[256,2048]{1,0:T(8,128)(2,1)S(1)} collective-permute-done((bf16[256,2048]{1,0:T(8,128)(2,1)S(1)}, bf16[256,2048]{1,0:T(8,128)(2,1)S(1)}, u32[]{:S(2)}, u32[]{:S(2)}) %collective-permute-start.17) | collective-permute-done | bytes 1048608 | tf_op jit(solution)/shard_map/ppermute | solution.py:458
  (27 shorter events, 11.0 us)
Async XLA Ops:
  3.0 15.1 %collective-permute-start = (bf16[3,256,256]{2,1,0:T(8,128)(2,1)}, bf16[3,256,256]{2,1,0:T(8,128)(2,1)S(1)}, u32[]{:S(2)}, u32[]{:S(2)}) collective-permute-start(bf16[3,256,256]{2,1,0:T(8,128)(2,1)} %get-tuple-element.52), channel_id=1, source_target_pairs={{0,4},{4,0},{8,12},{12,8},{16,20},{20,16},{24,28},{28,24},{1,5},{5... | collective-permute-start | bytes 1179656 | tf_op jit(solution)/shard_map/ppermute | solution.py:396
  6.0 17.9 %collective-permute-start.1 = (bf16[3,256,256]{2,1,0:T(8,128)(2,1)}, bf16[3,256,256]{2,1,0:T(8,128)(2,1)S(1)}, u32[]{:S(2)}, u32[]{:S(2)}) collective-permute-start(bf16[3,256,256]{2,1,0:T(8,128)(2,1)} %get-tuple-element.53), channel_id=1, source_target_pairs={{0,8},{4,12},{8,0},{12,4},{16,24},{20,28},{24,16},{28,20},{1,9},{5... | collective-permute-start | bytes 1179656 | tf_op jit(solution)/shard_map/ppermute | solution.py:396
  7.5 23.9 %collective-permute-start.2 = (bf16[3,256,256]{2,1,0:T(8,128)(2,1)}, bf16[3,256,256]{2,1,0:T(8,128)(2,1)S(1)}, u32[]{:S(2)}, u32[]{:S(2)}) collective-permute-start(bf16[3,256,256]{2,1,0:T(8,128)(2,1)} %get-tuple-element.54), channel_id=1, source_target_pairs={{0,12},{4,8},{8,4},{12,0},{16,28},{20,24},{24,20},{28,16},{1,13},{... | collective-permute-start | bytes 1179656 | tf_op jit(solution)/shard_map/ppermute | solution.py:396
  7.5 26.9 %collective-permute-start.3 = (bf16[2,256,128]{2,1,0:T(8,128)(2,1)}, bf16[2,256,128]{2,1,0:T(8,128)(2,1)S(1)}, u32[]{:S(2)}, u32[]{:S(2)}) collective-permute-start(bf16[2,256,128]{2,1,0:T(8,128)(2,1)} %get-tuple-element.60), channel_id=1, source_target_pairs={{0,16},{4,20},{8,24},{12,28},{16,0},{20,4},{24,8},{28,12},{1,17},{... | collective-permute-start | bytes 393224 | tf_op jit(solution)/shard_map/ppermute | solution.py:398
  10.5 24.0 %collective-permute-start.4 = (bf16[2,256,128]{2,1,0:T(8,128)(2,1)}, bf16[2,256,128]{2,1,0:T(8,128)(2,1)S(1)}, u32[]{:S(2)}, u32[]{:S(2)}) collective-permute-start(bf16[2,256,128]{2,1,0:T(8,128)(2,1)} %get-tuple-element.61), channel_id=1, source_target_pairs={{0,20},{4,16},{8,28},{12,24},{16,4},{20,0},{24,12},{28,8},{1,21},{... | collective-permute-start | bytes 393224 | tf_op jit(solution)/shard_map/ppermute | solution.py:398
  18.1 19.0 %collective-permute-start.5 = (bf16[2,256,128]{2,1,0:T(8,128)(2,1)}, bf16[2,256,128]{2,1,0:T(8,128)(2,1)S(1)}, u32[]{:S(2)}, u32[]{:S(2)}) collective-permute-start(bf16[2,256,128]{2,1,0:T(8,128)(2,1)} %get-tuple-element.62), channel_id=1, source_target_pairs={{0,24},{4,28},{8,16},{12,20},{16,8},{20,12},{24,0},{28,4},{1,25},{... | collective-permute-start | bytes 393224 | tf_op jit(solution)/shard_map/ppermute | solution.py:398
  23.8 14.6 %collective-permute-start.6 = (bf16[2,256,128]{2,1,0:T(8,128)(2,1)}, bf16[2,256,128]{2,1,0:T(8,128)(2,1)S(1)}, u32[]{:S(2)}, u32[]{:S(2)}) collective-permute-start(bf16[2,256,128]{2,1,0:T(8,128)(2,1)} %get-tuple-element.63), channel_id=1, source_target_pairs={{0,28},{4,24},{8,20},{12,16},{16,12},{20,8},{24,4},{28,0},{1,29},{... | collective-permute-start | bytes 393224 | tf_op jit(solution)/shard_map/ppermute | solution.py:398
  27.4 4.1 %copy-start = (bf16[3,256,256]{2,1,0:T(8,128)(2,1)S(1)}, bf16[3,256,256]{2,1,0:T(8,128)(2,1)}, u32[]{:S(2)}) copy-start(bf16[3,256,256]{2,1,0:T(8,128)(2,1)} %get-tuple-element.51.refs_0_) | copy-start | bytes 1179652
  40.6 9.7 %collective-permute-start.7 = (bf16[272,256]{1,0:T(8,128)(2,1)S(1)}, bf16[272,256]{1,0:T(8,128)(2,1)S(1)}, u32[]{:S(2)}, u32[]{:S(2)}) collective-permute-start(bf16[272,256]{1,0:T(8,128)(2,1)S(1)} %get-tuple-element.70), channel_id=1, source_target_pairs={{0,4},{4,0},{8,12},{12,8},{16,20},{20,16},{24,28},{28,24},{1,5},{5... | collective-permute-start | bytes 417800 | tf_op jit(solution)/shard_map/ppermute | solution.py:430
  42.2 9.4 %collective-permute-start.8 = (bf16[272,128]{1,0:T(8,128)(2,1)S(1)}, bf16[272,128]{1,0:T(8,128)(2,1)S(1)}, u32[]{:S(2)}, u32[]{:S(2)}) collective-permute-start(bf16[272,128]{1,0:T(8,128)(2,1)S(1)} %get-tuple-element.73), channel_id=1, source_target_pairs={{0,16},{4,20},{8,24},{12,28},{1,17},{5,21},{9,25},{13,29},{2,18},{... | collective-permute-start | bytes 208904 | tf_op jit(solution)/shard_map/ppermute | solution.py:434
  46.0 7.9 %collective-permute-start.12 = (bf16[272,256]{1,0:T(8,128)(2,1)S(1)}, bf16[272,256]{1,0:T(8,128)(2,1)S(1)}, u32[]{:S(2)}, u32[]{:S(2)}) collective-permute-start(bf16[272,256]{1,0:T(8,128)(2,1)S(1)} %get-tuple-element.77), channel_id=1, source_target_pairs={{0,8},{4,12},{8,0},{12,4},{16,24},{20,28},{24,16},{28,20},{1,9},{5... | collective-permute-start | bytes 417800 | tf_op jit(solution)/shard_map/ppermute | solution.py:430
  46.2 7.7 %collective-permute-start.13 = (bf16[272,256]{1,0:T(8,128)(2,1)S(1)}, bf16[272,256]{1,0:T(8,128)(2,1)S(1)}, u32[]{:S(2)}, u32[]{:S(2)}) collective-permute-start(bf16[272,256]{1,0:T(8,128)(2,1)S(1)} %get-tuple-element.78), channel_id=1, source_target_pairs={{0,12},{4,8},{8,4},{12,0},{16,28},{20,24},{24,20},{28,16},{1,13},{... | collective-permute-start | bytes 417800 | tf_op jit(solution)/shard_map/ppermute | solution.py:430
  48.2 5.7 %collective-permute-start.9 = (bf16[272,128]{1,0:T(8,128)(2,1)S(1)}, bf16[272,128]{1,0:T(8,128)(2,1)S(1)}, u32[]{:S(2)}, u32[]{:S(2)}) collective-permute-start(bf16[272,128]{1,0:T(8,128)(2,1)S(1)} %get-tuple-element.74), channel_id=1, source_target_pairs={{0,20},{4,16},{8,28},{12,24},{1,21},{5,17},{9,29},{13,25},{2,22},{... | collective-permute-start | bytes 208904 | tf_op jit(solution)/shard_map/ppermute | solution.py:434
  50.3 4.3 %collective-permute-start.11 = (bf16[272,128]{1,0:T(8,128)(2,1)S(1)}, bf16[272,128]{1,0:T(8,128)(2,1)S(1)}, u32[]{:S(2)}, u32[]{:S(2)}) collective-permute-start(bf16[272,128]{1,0:T(8,128)(2,1)S(1)} %get-tuple-element.76), channel_id=1, source_target_pairs={{0,28},{4,24},{8,20},{12,16},{1,29},{5,25},{9,21},{13,17},{2,30},{... | collective-permute-start | bytes 208904 | tf_op jit(solution)/shard_map/ppermute | solution.py:434
  51.6 3.8 %collective-permute-start.10 = (bf16[272,128]{1,0:T(8,128)(2,1)S(1)}, bf16[272,128]{1,0:T(8,128)(2,1)S(1)}, u32[]{:S(2)}, u32[]{:S(2)}) collective-permute-start(bf16[272,128]{1,0:T(8,128)(2,1)S(1)} %get-tuple-element.75), channel_id=1, source_target_pairs={{0,24},{4,28},{8,16},{12,20},{1,25},{5,29},{9,17},{13,21},{2,26},{... | collective-permute-start | bytes 208904 | tf_op jit(solution)/shard_map/ppermute | solution.py:434
  57.2 2.7 %collective-permute-start.14 = (bf16[256,2048]{1,0:T(8,128)(2,1)S(1)}, bf16[256,2048]{1,0:T(8,128)(2,1)S(1)}, u32[]{:S(2)}, u32[]{:S(2)}) collective-permute-start(bf16[256,2048]{1,0:T(8,128)(2,1)S(1)} %get-tuple-element.89), channel_id=1, source_target_pairs={{0,1},{1,0},{2,3},{3,2},{4,5},{5,4},{6,7},{7,6},{8,9},{9,8},{10,11... | collective-permute-start | bytes 3145736 | tf_op jit(solution)/shard_map/ppermute | solution.py:457
  60.4 25.3 %collective-permute-start.17 = (bf16[256,2048]{1,0:T(8,128)(2,1)S(1)}, bf16[256,2048]{1,0:T(8,128)(2,1)S(1)}, u32[]{:S(2)}, u32[]{:S(2)}) collective-permute-start(bf16[256,2048]{1,0:T(8,128)(2,1)S(1)} %add_convert_fusion), channel_id=1, source_target_pairs={{0,2},{1,3},{2,0},{3,1},{4,6},{5,7},{6,4},{7,5},{8,10},{9,11},{10,... | collective-permute-start | bytes 3145736 | tf_op jit(solution)/shard_map/ppermute | solution.py:458
  68.6 2.0 %collective-permute-start.16 = (bf16[256,1024]{1,0:T(8,128)(2,1)S(1)}, bf16[256,1024]{1,0:T(8,128)(2,1)S(1)}, u32[]{:S(2)}, u32[]{:S(2)}) collective-permute-start(bf16[256,1024]{1,0:T(8,128)(2,1)S(1)} %get-tuple-element.97), channel_id=1, source_target_pairs={{0,1},{1,0},{2,3},{3,2},{4,5},{5,4},{6,7},{7,6},{8,9},{9,8},{10,11... | collective-permute-start | bytes 1572872 | tf_op jit(solution)/shard_map/ppermute | solution.py:464
  68.6 2.6 %collective-permute-start.15 = (bf16[256,1024]{1,0:T(8,128)(2,1)S(1)}, bf16[256,1024]{1,0:T(8,128)(2,1)S(1)}, u32[]{:S(2)}, u32[]{:S(2)}) collective-permute-start(bf16[256,1024]{1,0:T(8,128)(2,1)S(1)} %get-tuple-element.98), channel_id=1, source_target_pairs={{0,1},{1,0},{2,3},{3,2},{4,5},{5,4},{6,7},{7,6},{8,9},{9,8},{10,11... | collective-permute-start | bytes 1572872 | tf_op jit(solution)/shard_map/ppermute | solution.py:464

commit v7 on v6

--- a/solution.py
+++ b/solution.py
@@ -10,7 +10,7 @@
 HD = 128
 MIB = 1 << 20
 OWN_PARTS = 2
-STEPS = 4
+STEPS = 8
 STAT_ROWS = 16
 T2TIE = (2, 3)
 LOG2E = 1.4426950408889634
@@ -251,23 +251,27 @@
         ]
         return jnp.concatenate(sums, axis=1)
 
-    gaps = []
-    for shift in range(half):
-        gap = read_log(over[shift]) - read_log(back[shift])
-        gaps.append(jnp.where(upper == 1, gap, -1e30))
-    table = jnp.concatenate(gaps + [jnp.zeros((HD - half, rows), jnp.float32)], axis=0)
-    table = jnp.transpose(table)
-    for shift in range(half):
-        source = place ^ shift
-        even = pl.ds(pl.multiple_of(source * 2 * HD, HD), HD)
-        odd = pl.ds(pl.multiple_of(source * 2 * HD + HD, HD), HD)
-        gap = table[:, shift : shift + 1]
-        near = 1.0 / (1.0 + jnp.exp2(gap))
-        far = 1.0 / (1.0 + jnp.exp2(-gap))
-        merged = near * back[shift][0:rows, 0:HD].astype(jnp.float32)
-        merged += far * over[shift][0:rows, :].astype(jnp.float32)
-        heads[:, even] = merged.astype(jnp.bfloat16)
-        heads[:, odd] = back[shift][0:rows, HD:]
+    @pl.when(upper == 0)
+    def _():
+        for shift in range(half):
+            wide = pl.ds(pl.multiple_of((place ^ shift) * 2 * HD, 2 * HD), 2 * HD)
+            heads[:, wide] = back[shift][0:rows, :]
+
+    @pl.when(upper == 1)
+    def _():
+        gaps = [read_log(over[shift]) - read_log(back[shift]) for shift in range(half)]
+        table = jnp.concatenate(gaps + [jnp.zeros((HD - half, rows), jnp.float32)], axis=0)
+        table = jnp.transpose(table)
+        for shift in range(half):
+            even = pl.ds(pl.multiple_of((place ^ shift) * 2 * HD, HD), HD)
+            odd = pl.ds(pl.multiple_of((place ^ shift) * 2 * HD + HD, HD), HD)
+            gap = table[:, shift : shift + 1]
+            near = 1.0 / (1.0 + jnp.exp2(gap))
+            far = 1.0 / (1.0 + jnp.exp2(-gap))
+            merged = near * back[shift][0:rows, 0:HD].astype(jnp.float32)
+            merged += far * over[shift][0:rows, :].astype(jnp.float32)
+            heads[:, even] = merged.astype(jnp.bfloat16)
+            heads[:, odd] = back[shift][0:rows, HD:]
 
 
 def multiply(heads, weight, out, tile):
@@ -310,7 +314,7 @@
 def project(heads, weights):
     out = jax.ShapeDtypeStruct((heads.shape[0], weights[0].shape[1]), jnp.bfloat16)
     return pl.pallas_call(
-        functools.partial(later_kernel, 512),
+        functools.partial(later_kernel, weights[0].shape[1]),
         in_specs=[VMEM] * (1 + len(weights)),
         out_specs=[VMEM] * len(weights),
         out_shape=[out] * len(weights),
@@ -441,7 +445,7 @@
         perm = [(i, (i + 2 * shift) % tp) for i in range(tp)]
         if heads is None:
             heads, give = pl.pallas_call(
-                functools.partial(first_kernel, half, 512),
+                functools.partial(first_kernel, half, cols),
                 in_specs=[smem] + [VMEM] * (n + 1),
                 out_specs=[VMEM] * 2,
                 out_shape=[

time: 87.2 us -> 87.2 us (level)
  no operation moved by 1% of the time
where the time goes in v7:
time: 87.2 us; the launch traced here: 86.3 us
  waiting for transfers between devices  32.6 us (37%)
  starting transfers between devices  30.6 us (35%)
  Pallas kernels  22.3 us (26%)
    ppermute x1, waiting for transfers between devices, heads_form(): crossing.append(lax.ppermute(both, 'tp', perm))  14.4 us
    ppermute x4, starting transfers between devices, heads_form(): lax.ppermute(piece, 'ctx', between(shift, 1, 1))  11.5 us
    ppermute x4, starting transfers between devices, heads_form(): over[shift] = lax.ppermute(over[shift], 'ctx', between(shift, 1, 0))  8.55 us
    ppermute x3, waiting for transfers between devices, heads_form(): inner[shift] = lax.ppermute(inner[shift], 'ctx', within(shift))  8.24 us
    pallas_call x2, Pallas kernels, fetch(): pl.pallas_call(fetch_kernel, in_specs=[pl.BlockSpec(memory_space=pltpu.SM...  8.07 us
    ppermute x3, starting transfers between devices, heads_form(): inner[shift] = lax.ppermute(inner[shift], 'ctx', within(shift))  4.58 us
    ppermute x4, waiting for transfers between devices, heads_form(): lax.ppermute(piece, 'ctx', between(shift, 1, 1))  3.96 us
    ppermute x3, starting transfers between devices, heads_form(): back[shift] = lax.ppermute(back[shift], 'ctx', within(shift))  3.69 us
  transfers between devices with their start and end apart: 18, of which 11 were waited for; matrix products, arithmetic and copies ran while one was open for 0% of the time, Pallas kernels for 17%

profile of v7, /device:TPU:0, one launch (start us, length us, event | category | flops | bytes accessed | tf_op | source)
XLA Modules:
  0.0 86.3 jit_solution(5078713799855774342)
XLA Ops:
  0.0 2.9 %shard_map.46 = (bf16[3,256,256]{2,1,0:T(8,128)(2,1)}, bf16[3,256,256]{2,1,0:T(8,128)(2,1)}, bf16[3,256,256]{2,1,0:T(8,128)(2,1)}, bf16[3,256,256]{2,1,0:T(8,128...) custom-call(s32[1]{0:T(128)} %bitcast.me_ref, ...), custom_call_target="tpu_custom_call" | custom-call | flops 1 | bytes 1 | tf_op jit(solution)/shard_map/pallas_call | solution.py:373
  3.0 3.0 %collective-permute-start = (bf16[3,256,256]{2,1,0:T(8,128)(2,1)}, bf16[3,256,256]{2,1,0:T(8,128)(2,1)S(1)}, u32[]{:S(2)}, u32[]{:S(2)}) collective-permute-start(bf16[3,256,256]{2,1,0:T(8,128)(2,1)} %get-tuple-element.52), channel_id=1, source_target_pairs={{0,4},{4,0},{8,12},{12,8},{16,20},{20,16},{24,28},{28,24},{1,5},{5... | collective-permute-start | bytes 1179656 | tf_op jit(solution)/shard_map/ppermute | solution.py:400
  6.0 1.6 %collective-permute-start.1 = (bf16[3,256,256]{2,1,0:T(8,128)(2,1)}, bf16[3,256,256]{2,1,0:T(8,128)(2,1)S(1)}, u32[]{:S(2)}, u32[]{:S(2)}) collective-permute-start(bf16[3,256,256]{2,1,0:T(8,128)(2,1)} %get-tuple-element.53), channel_id=1, source_target_pairs={{0,8},{4,12},{8,0},{12,4},{16,24},{20,28},{24,16},{28,20},{1,9},{5... | collective-permute-start | bytes 1179656 | tf_op jit(solution)/shard_map/ppermute | solution.py:400
  7.5 2.9 %collective-permute-start.3 = (bf16[2,256,128]{2,1,0:T(8,128)(2,1)}, bf16[2,256,128]{2,1,0:T(8,128)(2,1)S(1)}, u32[]{:S(2)}, u32[]{:S(2)}) collective-permute-start(bf16[2,256,128]{2,1,0:T(8,128)(2,1)} %get-tuple-element.60), channel_id=1, source_target_pairs={{0,16},{4,20},{8,24},{12,28},{16,0},{20,4},{24,8},{28,12},{1,17},{... | collective-permute-start | bytes 393224 | tf_op jit(solution)/shard_map/ppermute | solution.py:402
  10.5 1.3 %collective-permute-start.4 = (bf16[2,256,128]{2,1,0:T(8,128)(2,1)}, bf16[2,256,128]{2,1,0:T(8,128)(2,1)S(1)}, u32[]{:S(2)}, u32[]{:S(2)}) collective-permute-start(bf16[2,256,128]{2,1,0:T(8,128)(2,1)} %get-tuple-element.61), channel_id=1, source_target_pairs={{0,20},{4,16},{8,28},{12,24},{16,4},{20,0},{24,12},{28,8},{1,21},{... | collective-permute-start | bytes 393224 | tf_op jit(solution)/shard_map/ppermute | solution.py:402
  11.8 6.3 %collective-permute-done.refs_1_ = bf16[3,256,256]{2,1,0:T(8,128)(2,1)S(1)} collective-permute-done((bf16[3,256,256]{2,1,0:T(8,128)(2,1)}, bf16[3,256,256]{2,1,0:T(8,128)(2,1)S(1)}, u32[]{:S(2)}, u32[]{:S(2)}) %collective-permute-start) | collective-permute-done | bytes 393248 | tf_op jit(solution)/shard_map/ppermute | solution.py:400
  18.1 3.8 %collective-permute-start.5 = (bf16[2,256,128]{2,1,0:T(8,128)(2,1)}, bf16[2,256,128]{2,1,0:T(8,128)(2,1)S(1)}, u32[]{:S(2)}, u32[]{:S(2)}) collective-permute-start(bf16[2,256,128]{2,1,0:T(8,128)(2,1)} %get-tuple-element.62), channel_id=1, source_target_pairs={{0,24},{4,28},{8,16},{12,20},{16,8},{20,12},{24,0},{28,4},{1,25},{... | collective-permute-start | bytes 393224 | tf_op jit(solution)/shard_map/ppermute | solution.py:402
  21.9 2.0 %collective-permute-done.1.refs_2_ = bf16[3,256,256]{2,1,0:T(8,128)(2,1)S(1)} collective-permute-done((bf16[3,256,256]{2,1,0:T(8,128)(2,1)}, bf16[3,256,256]{2,1,0:T(8,128)(2,1)S(1)}, u32[]{:S(2)}, u32[]{:S(2)}) %collective-permute-start.1) | collective-permute-done | bytes 393248 | tf_op jit(solution)/shard_map/ppermute | solution.py:400
  23.8 3.5 %collective-permute-start.6 = (bf16[2,256,128]{2,1,0:T(8,128)(2,1)}, bf16[2,256,128]{2,1,0:T(8,128)(2,1)S(1)}, u32[]{:S(2)}, u32[]{:S(2)}) collective-permute-start(bf16[2,256,128]{2,1,0:T(8,128)(2,1)} %get-tuple-element.63), channel_id=1, source_target_pairs={{0,28},{4,24},{8,20},{12,16},{16,12},{20,8},{24,4},{28,0},{1,29},{... | collective-permute-start | bytes 393224 | tf_op jit(solution)/shard_map/ppermute | solution.py:402
  27.4 4.0 %shard_map.47 = (bf16[1024,2048]{1,0:T(8,128)(2,1)S(1)}, bf16[1024,2048]{1,0:T(8,128)(2,1)S(1)}) custom-call(s32[3]{0:T(128)S(1)} %pad_add_fusion.place_ref, bf16[1024,8192]{1,0:T(8,128)(2,1)} %w_ref.2), custom_call_target="tpu_custom_call" | custom-call | flops 1 | bytes 16777216 | tf_op jit(solution)/shard_map/pallas_call | solution.py:341
  31.5 3.0 %shard_map.48 = (bf16[1024,128]{1,0:T(8,128)(2,1)S(1)}, f32[1024,128]{1,0:T(8,128)S(1)}, f32[256,128]{1,0:T(8,128)S(1)}) custom-call(s32[1]{0:T(128)} %bitcast.me_ref, bf16[3,256,256]{2,1,0:T(8,128)(2,1)S(1)} %copy-done, bf16[3,256,256]{2,1,0:T(8,128)(2,1)S(1)} %collective-permute-done.refs_1_, bf16[3,256,256]{2,1,0:T(8,128)(2,1)S(1)} %collective-permute-done.1.refs_2_, ...), custom_call_target="tpu_custom_call" | custom-call | flops 1 | bytes 1 | tf_op jit(solution)/shard_map/pallas_call | solution.py:410
  34.5 2.6 %collective-permute-done.5.refs_6_ = bf16[2,256,128]{2,1,0:T(8,128)(2,1)S(1)} collective-permute-done((bf16[2,256,128]{2,1,0:T(8,128)(2,1)}, bf16[2,256,128]{2,1,0:T(8,128)(2,1)S(1)}, u32[]{:S(2)}, u32[]{:S(2)}) %collective-permute-start.5) | collective-permute-done | bytes 131104 | tf_op jit(solution)/shard_map/ppermute | solution.py:402
  37.0 1.4 %collective-permute-done.6.refs_7_ = bf16[2,256,128]{2,1,0:T(8,128)(2,1)S(1)} collective-permute-done((bf16[2,256,128]{2,1,0:T(8,128)(2,1)}, bf16[2,256,128]{2,1,0:T(8,128)(2,1)S(1)}, u32[]{:S(2)}, u32[]{:S(2)}) %collective-permute-start.6) | collective-permute-done | bytes 131104 | tf_op jit(solution)/shard_map/ppermute | solution.py:402
  38.4 2.2 %shard_map.49 = (bf16[272,256]{1,0:T(8,128)(2,1)S(1)}, bf16[272,256]{1,0:T(8,128)(2,1)S(1)}, bf16[272,256]{1,0:T(8,128)(2,1)S(1)}, bf16[272,256]{1,0:T(8,128)(2,...) custom-call(s32[1]{0:T(128)} %bitcast.me_ref, ...), custom_call_target="tpu_custom_call" | custom-call | flops 1 | bytes 1 | tf_op jit(solution)/shard_map/pallas_call | solution.py:423
  40.6 1.6 %collective-permute-start.7 = (bf16[272,256]{1,0:T(8,128)(2,1)S(1)}, bf16[272,256]{1,0:T(8,128)(2,1)S(1)}, u32[]{:S(2)}, u32[]{:S(2)}) collective-permute-start(bf16[272,256]{1,0:T(8,128)(2,1)S(1)} %get-tuple-element.70), channel_id=1, source_target_pairs={{0,4},{4,0},{8,12},{12,8},{16,20},{20,16},{24,28},{28,24},{1,5},{5... | collective-permute-start | bytes 417800 | tf_op jit(solution)/shard_map/ppermute | solution.py:434
  42.2 3.8 %collective-permute-start.8 = (bf16[272,128]{1,0:T(8,128)(2,1)S(1)}, bf16[272,128]{1,0:T(8,128)(2,1)S(1)}, u32[]{:S(2)}, u32[]{:S(2)}) collective-permute-start(bf16[272,128]{1,0:T(8,128)(2,1)S(1)} %get-tuple-element.73), channel_id=1, source_target_pairs={{0,16},{4,20},{8,24},{12,28},{1,17},{5,21},{9,25},{13,29},{2,18},{... | collective-permute-start | bytes 208904 | tf_op jit(solution)/shard_map/ppermute | solution.py:438
  46.2 1.9 %collective-permute-start.13 = (bf16[272,256]{1,0:T(8,128)(2,1)S(1)}, bf16[272,256]{1,0:T(8,128)(2,1)S(1)}, u32[]{:S(2)}, u32[]{:S(2)}) collective-permute-start(bf16[272,256]{1,0:T(8,128)(2,1)S(1)} %get-tuple-element.78), channel_id=1, source_target_pairs={{0,12},{4,8},{8,4},{12,0},{16,28},{20,24},{24,20},{28,16},{1,13},{... | collective-permute-start | bytes 417800 | tf_op jit(solution)/shard_map/ppermute | solution.py:434
  48.2 2.1 %collective-permute-start.9 = (bf16[272,128]{1,0:T(8,128)(2,1)S(1)}, bf16[272,128]{1,0:T(8,128)(2,1)S(1)}, u32[]{:S(2)}, u32[]{:S(2)}) collective-permute-start(bf16[272,128]{1,0:T(8,128)(2,1)S(1)} %get-tuple-element.74), channel_id=1, source_target_pairs={{0,20},{4,16},{8,28},{12,24},{1,21},{5,17},{9,29},{13,25},{2,22},{... | collective-permute-start | bytes 208904 | tf_op jit(solution)/shard_map/ppermute | solution.py:438
  58.1 1.4 %collective-permute-done.14 = bf16[256,2048]{1,0:T(8,128)(2,1)S(1)} collective-permute-done((bf16[256,2048]{1,0:T(8,128)(2,1)S(1)}, bf16[256,2048]{1,0:T(8,128)(2,1)S(1)}, u32[]{:S(2)}, u32[]{:S(2)}) %collective-permute-start.14) | collective-permute-done | bytes 1048608 | tf_op jit(solution)/shard_map/ppermute | solution.py:461
  59.9 1.6 %collective-permute-start.17 = (bf16[256,2048]{1,0:T(8,128)(2,1)S(1)}, bf16[256,2048]{1,0:T(8,128)(2,1)S(1)}, u32[]{:S(2)}, u32[]{:S(2)}) collective-permute-start(bf16[256,2048]{1,0:T(8,128)(2,1)S(1)} %add_convert_fusion), channel_id=1, source_target_pairs={{0,2},{1,3},{2,0},{3,1},{4,6},{5,7},{6,4},{7,5},{8,10},{9,11},{10,... | collective-permute-start | bytes 3145736 | tf_op jit(solution)/shard_map/ppermute | solution.py:462
  61.6 4.0 %shard_map.52 = (bf16[1024,2048]{1,0:T(8,128)(2,1)S(1)}, bf16[1024,2048]{1,0:T(8,128)(2,1)S(1)}) custom-call(s32[3]{0:T(128)S(1)} %pad_add_fusion.1.place_ref, bf16[1024,8192]{1,0:T(8,128)(2,1)} %w_ref.2), custom_call_target="tpu_custom_call" | custom-call | flops 1 | bytes 16777216 | tf_op jit(solution)/shard_map/pallas_call | solution.py:341
  65.6 2.4 %shard_map.53 = (bf16[256,2048]{1,0:T(8,128)(2,1)S(1)}, bf16[256,2048]{1,0:T(8,128)(2,1)S(1)}) custom-call(bf16[256,1024]{1,0:T(8,128)(2,1)S(1)} %get-tuple-element.91.heads, bf16[1024,2048]{1,0:T(8,128)(2,1)S(1)} %get-tuple-element.93.refs_0_, bf16[1024,2048]{1,0:T(8,128)(2,1)S(1)} %get-tuple-element.94.refs_1_), custom_call_target="tpu_custom_call" | custom-call | flops 1 | bytes 1 | tf_op jit(solution)/shard_map/pallas_call | solution.py:316
  68.7 1.4 %collective-permute-done.16.refs_1_ = bf16[256,1024]{1,0:T(8,128)(2,1)S(1)} collective-permute-done((bf16[256,1024]{1,0:T(8,128)(2,1)S(1)}, bf16[256,1024]{1,0:T(8,128)(2,1)S(1)}, u32[]{:S(2)}, u32[]{:S(2)}) %collective-permute-start.16) | collective-permute-done | bytes 524320 | tf_op jit(solution)/shard_map/ppermute | solution.py:468
  70.8 14.4 %collective-permute-done.17.refs_2_ = bf16[256,2048]{1,0:T(8,128)(2,1)S(1)} collective-permute-done((bf16[256,2048]{1,0:T(8,128)(2,1)S(1)}, bf16[256,2048]{1,0:T(8,128)(2,1)S(1)}, u32[]{:S(2)}, u32[]{:S(2)}) %collective-permute-start.17) | collective-permute-done | bytes 1048608 | tf_op jit(solution)/shard_map/ppermute | solution.py:462
  (27 shorter events, 11.0 us)
Async XLA Ops:
  3.0 15.1 %collective-permute-start = (bf16[3,256,256]{2,1,0:T(8,128)(2,1)}, bf16[3,256,256]{2,1,0:T(8,128)(2,1)S(1)}, u32[]{:S(2)}, u32[]{:S(2)}) collective-permute-start(bf16[3,256,256]{2,1,0:T(8,128)(2,1)} %get-tuple-element.52), channel_id=1, source_target_pairs={{0,4},{4,0},{8,12},{12,8},{16,20},{20,16},{24,28},{28,24},{1,5},{5... | collective-permute-start | bytes 1179656 | tf_op jit(solution)/shard_map/ppermute | solution.py:400
  6.0 17.9 %collective-permute-start.1 = (bf16[3,256,256]{2,1,0:T(8,128)(2,1)}, bf16[3,256,256]{2,1,0:T(8,128)(2,1)S(1)}, u32[]{:S(2)}, u32[]{:S(2)}) collective-permute-start(bf16[3,256,256]{2,1,0:T(8,128)(2,1)} %get-tuple-element.53), channel_id=1, source_target_pairs={{0,8},{4,12},{8,0},{12,4},{16,24},{20,28},{24,16},{28,20},{1,9},{5... | collective-permute-start | bytes 1179656 | tf_op jit(solution)/shard_map/ppermute | solution.py:400
  7.5 23.9 %collective-permute-start.2 = (bf16[3,256,256]{2,1,0:T(8,128)(2,1)}, bf16[3,256,256]{2,1,0:T(8,128)(2,1)S(1)}, u32[]{:S(2)}, u32[]{:S(2)}) collective-permute-start(bf16[3,256,256]{2,1,0:T(8,128)(2,1)} %get-tuple-element.54), channel_id=1, source_target_pairs={{0,12},{4,8},{8,4},{12,0},{16,28},{20,24},{24,20},{28,16},{1,13},{... | collective-permute-start | bytes 1179656 | tf_op jit(solution)/shard_map/ppermute | solution.py:400
  7.5 26.9 %collective-permute-start.3 = (bf16[2,256,128]{2,1,0:T(8,128)(2,1)}, bf16[2,256,128]{2,1,0:T(8,128)(2,1)S(1)}, u32[]{:S(2)}, u32[]{:S(2)}) collective-permute-start(bf16[2,256,128]{2,1,0:T(8,128)(2,1)} %get-tuple-element.60), channel_id=1, source_target_pairs={{0,16},{4,20},{8,24},{12,28},{16,0},{20,4},{24,8},{28,12},{1,17},{... | collective-permute-start | bytes 393224 | tf_op jit(solution)/shard_map/ppermute | solution.py:402
  10.5 24.0 %collective-permute-start.4 = (bf16[2,256,128]{2,1,0:T(8,128)(2,1)}, bf16[2,256,128]{2,1,0:T(8,128)(2,1)S(1)}, u32[]{:S(2)}, u32[]{:S(2)}) collective-permute-start(bf16[2,256,128]{2,1,0:T(8,128)(2,1)} %get-tuple-element.61), channel_id=1, source_target_pairs={{0,20},{4,16},{8,28},{12,24},{16,4},{20,0},{24,12},{28,8},{1,21},{... | collective-permute-start | bytes 393224 | tf_op jit(solution)/shard_map/ppermute | solution.py:402
  18.1 19.0 %collective-permute-start.5 = (bf16[2,256,128]{2,1,0:T(8,128)(2,1)}, bf16[2,256,128]{2,1,0:T(8,128)(2,1)S(1)}, u32[]{:S(2)}, u32[]{:S(2)}) collective-permute-start(bf16[2,256,128]{2,1,0:T(8,128)(2,1)} %get-tuple-element.62), channel_id=1, source_target_pairs={{0,24},{4,28},{8,16},{12,20},{16,8},{20,12},{24,0},{28,4},{1,25},{... | collective-permute-start | bytes 393224 | tf_op jit(solution)/shard_map/ppermute | solution.py:402
  23.8 14.6 %collective-permute-start.6 = (bf16[2,256,128]{2,1,0:T(8,128)(2,1)}, bf16[2,256,128]{2,1,0:T(8,128)(2,1)S(1)}, u32[]{:S(2)}, u32[]{:S(2)}) collective-permute-start(bf16[2,256,128]{2,1,0:T(8,128)(2,1)} %get-tuple-element.63), channel_id=1, source_target_pairs={{0,28},{4,24},{8,20},{12,16},{16,12},{20,8},{24,4},{28,0},{1,29},{... | collective-permute-start | bytes 393224 | tf_op jit(solution)/shard_map/ppermute | solution.py:402
  27.4 4.1 %copy-start = (bf16[3,256,256]{2,1,0:T(8,128)(2,1)S(1)}, bf16[3,256,256]{2,1,0:T(8,128)(2,1)}, u32[]{:S(2)}) copy-start(bf16[3,256,256]{2,1,0:T(8,128)(2,1)} %get-tuple-element.51.refs_0_) | copy-start | bytes 1179652
  40.6 9.7 %collective-permute-start.7 = (bf16[272,256]{1,0:T(8,128)(2,1)S(1)}, bf16[272,256]{1,0:T(8,128)(2,1)S(1)}, u32[]{:S(2)}, u32[]{:S(2)}) collective-permute-start(bf16[272,256]{1,0:T(8,128)(2,1)S(1)} %get-tuple-element.70), channel_id=1, source_target_pairs={{0,4},{4,0},{8,12},{12,8},{16,20},{20,16},{24,28},{28,24},{1,5},{5... | collective-permute-start | bytes 417800 | tf_op jit(solution)/shard_map/ppermute | solution.py:434
  42.2 9.4 %collective-permute-start.8 = (bf16[272,128]{1,0:T(8,128)(2,1)S(1)}, bf16[272,128]{1,0:T(8,128)(2,1)S(1)}, u32[]{:S(2)}, u32[]{:S(2)}) collective-permute-start(bf16[272,128]{1,0:T(8,128)(2,1)S(1)} %get-tuple-element.73), channel_id=1, source_target_pairs={{0,16},{4,20},{8,24},{12,28},{1,17},{5,21},{9,25},{13,29},{2,18},{... | collective-permute-start | bytes 208904 | tf_op jit(solution)/shard_map/ppermute | solution.py:438
  46.0 7.9 %collective-permute-start.12 = (bf16[272,256]{1,0:T(8,128)(2,1)S(1)}, bf16[272,256]{1,0:T(8,128)(2,1)S(1)}, u32[]{:S(2)}, u32[]{:S(2)}) collective-permute-start(bf16[272,256]{1,0:T(8,128)(2,1)S(1)} %get-tuple-element.77), channel_id=1, source_target_pairs={{0,8},{4,12},{8,0},{12,4},{16,24},{20,28},{24,16},{28,20},{1,9},{5... | collective-permute-start | bytes 417800 | tf_op jit(solution)/shard_map/ppermute | solution.py:434
  46.2 7.7 %collective-permute-start.13 = (bf16[272,256]{1,0:T(8,128)(2,1)S(1)}, bf16[272,256]{1,0:T(8,128)(2,1)S(1)}, u32[]{:S(2)}, u32[]{:S(2)}) collective-permute-start(bf16[272,256]{1,0:T(8,128)(2,1)S(1)} %get-tuple-element.78), channel_id=1, source_target_pairs={{0,12},{4,8},{8,4},{12,0},{16,28},{20,24},{24,20},{28,16},{1,13},{... | collective-permute-start | bytes 417800 | tf_op jit(solution)/shard_map/ppermute | solution.py:434
  48.2 5.7 %collective-permute-start.9 = (bf16[272,128]{1,0:T(8,128)(2,1)S(1)}, bf16[272,128]{1,0:T(8,128)(2,1)S(1)}, u32[]{:S(2)}, u32[]{:S(2)}) collective-permute-start(bf16[272,128]{1,0:T(8,128)(2,1)S(1)} %get-tuple-element.74), channel_id=1, source_target_pairs={{0,20},{4,16},{8,28},{12,24},{1,21},{5,17},{9,29},{13,25},{2,22},{... | collective-permute-start | bytes 208904 | tf_op jit(solution)/shard_map/ppermute | solution.py:438
  50.3 4.3 %collective-permute-start.11 = (bf16[272,128]{1,0:T(8,128)(2,1)S(1)}, bf16[272,128]{1,0:T(8,128)(2,1)S(1)}, u32[]{:S(2)}, u32[]{:S(2)}) collective-permute-start(bf16[272,128]{1,0:T(8,128)(2,1)S(1)} %get-tuple-element.76), channel_id=1, source_target_pairs={{0,28},{4,24},{8,20},{12,16},{1,29},{5,25},{9,21},{13,17},{2,30},{... | collective-permute-start | bytes 208904 | tf_op jit(solution)/shard_map/ppermute | solution.py:438
  51.6 3.8 %collective-permute-start.10 = (bf16[272,128]{1,0:T(8,128)(2,1)S(1)}, bf16[272,128]{1,0:T(8,128)(2,1)S(1)}, u32[]{:S(2)}, u32[]{:S(2)}) collective-permute-start(bf16[272,128]{1,0:T(8,128)(2,1)S(1)} %get-tuple-element.75), channel_id=1, source_target_pairs={{0,24},{4,28},{8,16},{12,20},{1,25},{5,29},{9,17},{13,21},{2,26},{... | collective-permute-start | bytes 208904 | tf_op jit(solution)/shard_map/ppermute | solution.py:438
  56.8 2.7 %collective-permute-start.14 = (bf16[256,2048]{1,0:T(8,128)(2,1)S(1)}, bf16[256,2048]{1,0:T(8,128)(2,1)S(1)}, u32[]{:S(2)}, u32[]{:S(2)}) collective-permute-start(bf16[256,2048]{1,0:T(8,128)(2,1)S(1)} %get-tuple-element.89), channel_id=1, source_target_pairs={{0,1},{1,0},{2,3},{3,2},{4,5},{5,4},{6,7},{7,6},{8,9},{9,8},{10,11... | collective-permute-start | bytes 3145736 | tf_op jit(solution)/shard_map/ppermute | solution.py:461
  59.9 25.3 %collective-permute-start.17 = (bf16[256,2048]{1,0:T(8,128)(2,1)S(1)}, bf16[256,2048]{1,0:T(8,128)(2,1)S(1)}, u32[]{:S(2)}, u32[]{:S(2)}) collective-permute-start(bf16[256,2048]{1,0:T(8,128)(2,1)S(1)} %add_convert_fusion), channel_id=1, source_target_pairs={{0,2},{1,3},{2,0},{3,1},{4,6},{5,7},{6,4},{7,5},{8,10},{9,11},{10,... | collective-permute-start | bytes 3145736 | tf_op jit(solution)/shard_map/ppermute | solution.py:462
  68.1 2.0 %collective-permute-start.16 = (bf16[256,1024]{1,0:T(8,128)(2,1)S(1)}, bf16[256,1024]{1,0:T(8,128)(2,1)S(1)}, u32[]{:S(2)}, u32[]{:S(2)}) collective-permute-start(bf16[256,1024]{1,0:T(8,128)(2,1)S(1)} %get-tuple-element.97), channel_id=1, source_target_pairs={{0,1},{1,0},{2,3},{3,2},{4,5},{5,4},{6,7},{7,6},{8,9},{9,8},{10,11... | collective-permute-start | bytes 1572872 | tf_op jit(solution)/shard_map/ppermute | solution.py:468
  68.2 2.6 %collective-permute-start.15 = (bf16[256,1024]{1,0:T(8,128)(2,1)S(1)}, bf16[256,1024]{1,0:T(8,128)(2,1)S(1)}, u32[]{:S(2)}, u32[]{:S(2)}) collective-permute-start(bf16[256,1024]{1,0:T(8,128)(2,1)S(1)} %get-tuple-element.98), channel_id=1, source_target_pairs={{0,1},{1,0},{2,3},{3,2},{4,5},{5,4},{6,7},{7,6},{8,9},{9,8},{10,11... | collective-permute-start | bytes 1572872 | tf_op jit(solution)/shard_map/ppermute | solution.py:468

commit v8 on v6

--- a/solution.py
+++ b/solution.py
@@ -270,10 +270,12 @@
         heads[:, odd] = back[shift][0:rows, HD:]
 
 
-def multiply(heads, weight, out, tile):
+def multiply(heads, weight, out, tile, start=0):
     for at in range(0, out.shape[1], tile):
         out[:, at : at + tile] = jnp.dot(
-            heads[...], weight[:, at : at + tile], preferred_element_type=jnp.float32
+            heads[...],
+            weight[:, start + at : start + at + tile],
+            preferred_element_type=jnp.float32,
         ).astype(jnp.bfloat16)
 
 
@@ -283,10 +285,10 @@
     multiply(heads, weight, out, tile)
 
 
-def later_kernel(tile, heads, *refs):
+def later_kernel(tile, start, heads, *refs):
     count = len(refs) // 2
     for weight, out in zip(refs[:count], refs[count:]):
-        multiply(heads, weight, out, tile)
+        multiply(heads, weight, out, tile, start)
 
 
 def last_kernel(keep, *refs):
@@ -307,10 +309,10 @@
         one.wait()
 
 
-def project(heads, weights):
-    out = jax.ShapeDtypeStruct((heads.shape[0], weights[0].shape[1]), jnp.bfloat16)
+def project(heads, weights, start, cols):
+    out = jax.ShapeDtypeStruct((heads.shape[0], cols), jnp.bfloat16)
     return pl.pallas_call(
-        functools.partial(later_kernel, 512),
+        functools.partial(later_kernel, 512, start),
         in_specs=[VMEM] * (1 + len(weights)),
         out_specs=[VMEM] * len(weights),
         out_shape=[out] * len(weights),
@@ -446,19 +448,21 @@
                 out_specs=[VMEM] * 2,
                 out_shape=[
                     jax.ShapeDtypeStruct((rows, n * HD), bf16),
-                    jax.ShapeDtypeStruct((rows, cols), bf16),
+                    jax.ShapeDtypeStruct((rows, cols // 2), bf16),
                 ],
                 compiler_params=params(16),
                 cost_estimate=COST,
             )(place, *back, *over, w_give)
         else:
-            (give,) = project(heads, [w_give])
-        (keep,) = project(heads, [w_keep])
-        both = (keep.astype(f32) + lax.ppermute(give, "tp", swap).astype(f32)).astype(bf16)
+            (give,) = project(heads, [w_give], 0, cols // 2)
+        (rest,) = project(heads, [w_give], cols // 2, cols // 2)
+        (keep,) = project(heads, [w_keep], 0, cols)
+        came = [lax.ppermute(one, "tp", swap).astype(f32) for one in (give, rest)]
+        both = (keep.astype(f32) + jnp.concatenate(came, axis=1)).astype(bf16)
         crossing.append(lax.ppermute(both, "tp", perm))
         both, heads = lax.optimization_barrier((both, heads))
     out_weight, heads = lax.optimization_barrier((out_weight, heads))
-    give, keep = project(heads, fetch(wanted(y), out_weight, cols))
+    give, keep = project(heads, fetch(wanted(y), out_weight, cols), 0, cols)
     piece = cols // OWN_PARTS
     swapped = [
         lax.ppermute(give[:, at : at + piece], "tp", swap) for at in range(0, cols, piece)

time: 87.2 us -> 87 us (level)
  waiting for transfers between devices: 32.6 us -> 31.7 us
    ppermute x1 -> x2, waiting for transfers between devices: 1.36 us -> 0.25 us  [heads_form(): came = [lax.ppermute(one, 'tp', swap).astype(f32) for one in (give, rest)]]
    pallas_call x2 -> x3, Pallas kernels: 3.66 us -> 4.37 us  [project(): pl.pallas_call(functools.partial(later_kernel, 512, start), in_specs=[VME...]
  transfers between devices with their start and end apart: 18 -> 19, of which waited for: 11 -> 11; matrix products, arithmetic and copies ran while one was open for 0% -> 0% of each run, Pallas kernels for 17% -> 18%
where the time goes in v8:
time: 87 us; the launch traced here: 86.6 us
  waiting for transfers between devices  31.7 us (36%)
  starting transfers between devices  31.2 us (36%)
  Pallas kernels  22.9 us (26%)
    ppermute x1, waiting for transfers between devices, heads_form(): crossing.append(lax.ppermute(both, 'tp', perm))  14.6 us
    ppermute x4, starting transfers between devices, heads_form(): lax.ppermute(piece, 'ctx', between(shift, 1, 1))  11.5 us
    ppermute x4, starting transfers between devices, heads_form(): over[shift] = lax.ppermute(over[shift], 'ctx', between(shift, 1, 0))  8.55 us
    ppermute x3, waiting for transfers between devices, heads_form(): inner[shift] = lax.ppermute(inner[shift], 'ctx', within(shift))  8.24 us
    pallas_call x2, Pallas kernels, fetch(): pl.pallas_call(fetch_kernel, in_specs=[pl.BlockSpec(memory_space=pltpu.SM...  8.07 us
    ppermute x3, starting transfers between devices, heads_form(): inner[shift] = lax.ppermute(inner[shift], 'ctx', within(shift))  4.58 us
    pallas_call x3, Pallas kernels, project(): pl.pallas_call(functools.partial(later_kernel, 512, start), in_specs=[VME...  4.37 us
    ppermute x4, waiting for transfers between devices, heads_form(): lax.ppermute(piece, 'ctx', between(shift, 1, 1))  3.96 us
  transfers between devices with their start and end apart: 19, of which 11 were waited for; matrix products, arithmetic and copies ran while one was open for 0% of the time, Pallas kernels for 18%

profile of v8, /device:TPU:0, one launch (start us, length us, event | category | flops | bytes accessed | tf_op | source)
XLA Modules:
  0.0 86.6 jit_solution(6524059098520676304)
XLA Ops:
  0.0 3.0 %shard_map.46 = (bf16[3,256,256]{2,1,0:T(8,128)(2,1)}, bf16[3,256,256]{2,1,0:T(8,128)(2,1)}, bf16[3,256,256]{2,1,0:T(8,128)(2,1)}, bf16[3,256,256]{2,1,0:T(8,128...) custom-call(s32[1]{0:T(128)} %bitcast.me_ref, ...), custom_call_target="tpu_custom_call" | custom-call | flops 1 | bytes 1 | tf_op jit(solution)/shard_map/pallas_call | solution.py:371
  3.0 3.0 %collective-permute-start = (bf16[3,256,256]{2,1,0:T(8,128)(2,1)}, bf16[3,256,256]{2,1,0:T(8,128)(2,1)S(1)}, u32[]{:S(2)}, u32[]{:S(2)}) collective-permute-start(bf16[3,256,256]{2,1,0:T(8,128)(2,1)} %get-tuple-element.52), channel_id=1, source_target_pairs={{0,4},{4,0},{8,12},{12,8},{16,20},{20,16},{24,28},{28,24},{1,5},{5... | collective-permute-start | bytes 1179656 | tf_op jit(solution)/shard_map/ppermute | solution.py:398
  6.0 1.6 %collective-permute-start.1 = (bf16[3,256,256]{2,1,0:T(8,128)(2,1)}, bf16[3,256,256]{2,1,0:T(8,128)(2,1)S(1)}, u32[]{:S(2)}, u32[]{:S(2)}) collective-permute-start(bf16[3,256,256]{2,1,0:T(8,128)(2,1)} %get-tuple-element.53), channel_id=1, source_target_pairs={{0,8},{4,12},{8,0},{12,4},{16,24},{20,28},{24,16},{28,20},{1,9},{5... | collective-permute-start | bytes 1179656 | tf_op jit(solution)/shard_map/ppermute | solution.py:398
  7.5 2.9 %collective-permute-start.3 = (bf16[2,256,128]{2,1,0:T(8,128)(2,1)}, bf16[2,256,128]{2,1,0:T(8,128)(2,1)S(1)}, u32[]{:S(2)}, u32[]{:S(2)}) collective-permute-start(bf16[2,256,128]{2,1,0:T(8,128)(2,1)} %get-tuple-element.60), channel_id=1, source_target_pairs={{0,16},{4,20},{8,24},{12,28},{16,0},{20,4},{24,8},{28,12},{1,17},{... | collective-permute-start | bytes 393224 | tf_op jit(solution)/shard_map/ppermute | solution.py:400
  10.5 1.3 %collective-permute-start.4 = (bf16[2,256,128]{2,1,0:T(8,128)(2,1)}, bf16[2,256,128]{2,1,0:T(8,128)(2,1)S(1)}, u32[]{:S(2)}, u32[]{:S(2)}) collective-permute-start(bf16[2,256,128]{2,1,0:T(8,128)(2,1)} %get-tuple-element.61), channel_id=1, source_target_pairs={{0,20},{4,16},{8,28},{12,24},{16,4},{20,0},{24,12},{28,8},{1,21},{... | collective-permute-start | bytes 393224 | tf_op jit(solution)/shard_map/ppermute | solution.py:400
  11.8 6.3 %collective-permute-done.refs_1_ = bf16[3,256,256]{2,1,0:T(8,128)(2,1)S(1)} collective-permute-done((bf16[3,256,256]{2,1,0:T(8,128)(2,1)}, bf16[3,256,256]{2,1,0:T(8,128)(2,1)S(1)}, u32[]{:S(2)}, u32[]{:S(2)}) %collective-permute-start) | collective-permute-done | bytes 393248 | tf_op jit(solution)/shard_map/ppermute | solution.py:398
  18.1 3.8 %collective-permute-start.5 = (bf16[2,256,128]{2,1,0:T(8,128)(2,1)}, bf16[2,256,128]{2,1,0:T(8,128)(2,1)S(1)}, u32[]{:S(2)}, u32[]{:S(2)}) collective-permute-start(bf16[2,256,128]{2,1,0:T(8,128)(2,1)} %get-tuple-element.62), channel_id=1, source_target_pairs={{0,24},{4,28},{8,16},{12,20},{16,8},{20,12},{24,0},{28,4},{1,25},{... | collective-permute-start | bytes 393224 | tf_op jit(solution)/shard_map/ppermute | solution.py:400
  21.9 2.0 %collective-permute-done.1.refs_2_ = bf16[3,256,256]{2,1,0:T(8,128)(2,1)S(1)} collective-permute-done((bf16[3,256,256]{2,1,0:T(8,128)(2,1)}, bf16[3,256,256]{2,1,0:T(8,128)(2,1)S(1)}, u32[]{:S(2)}, u32[]{:S(2)}) %collective-permute-start.1) | collective-permute-done | bytes 393248 | tf_op jit(solution)/shard_map/ppermute | solution.py:398
  23.8 3.5 %collective-permute-start.6 = (bf16[2,256,128]{2,1,0:T(8,128)(2,1)}, bf16[2,256,128]{2,1,0:T(8,128)(2,1)S(1)}, u32[]{:S(2)}, u32[]{:S(2)}) collective-permute-start(bf16[2,256,128]{2,1,0:T(8,128)(2,1)} %get-tuple-element.63), channel_id=1, source_target_pairs={{0,28},{4,24},{8,20},{12,16},{16,12},{20,8},{24,4},{28,0},{1,29},{... | collective-permute-start | bytes 393224 | tf_op jit(solution)/shard_map/ppermute | solution.py:400
  27.4 4.0 %shard_map.47 = (bf16[1024,2048]{1,0:T(8,128)(2,1)S(1)}, bf16[1024,2048]{1,0:T(8,128)(2,1)S(1)}) custom-call(s32[3]{0:T(128)S(1)} %pad_add_fusion.place_ref, bf16[1024,8192]{1,0:T(8,128)(2,1)} %w_ref.2), custom_call_target="tpu_custom_call" | custom-call | flops 1 | bytes 16777216 | tf_op jit(solution)/shard_map/pallas_call | solution.py:339
  31.5 3.0 %shard_map.48 = (bf16[1024,128]{1,0:T(8,128)(2,1)S(1)}, f32[1024,128]{1,0:T(8,128)S(1)}, f32[256,128]{1,0:T(8,128)S(1)}) custom-call(s32[1]{0:T(128)} %bitcast.me_ref, bf16[3,256,256]{2,1,0:T(8,128)(2,1)S(1)} %copy-done, bf16[3,256,256]{2,1,0:T(8,128)(2,1)S(1)} %collective-permute-done.refs_1_, bf16[3,256,256]{2,1,0:T(8,128)(2,1)S(1)} %collective-permute-done.1.refs_2_, ...), custom_call_target="tpu_custom_call" | custom-call | flops 1 | bytes 1 | tf_op jit(solution)/shard_map/pallas_call | solution.py:408
  34.5 2.6 %collective-permute-done.5.refs_6_ = bf16[2,256,128]{2,1,0:T(8,128)(2,1)S(1)} collective-permute-done((bf16[2,256,128]{2,1,0:T(8,128)(2,1)}, bf16[2,256,128]{2,1,0:T(8,128)(2,1)S(1)}, u32[]{:S(2)}, u32[]{:S(2)}) %collective-permute-start.5) | collective-permute-done | bytes 131104 | tf_op jit(solution)/shard_map/ppermute | solution.py:400
  37.1 1.4 %collective-permute-done.6.refs_7_ = bf16[2,256,128]{2,1,0:T(8,128)(2,1)S(1)} collective-permute-done((bf16[2,256,128]{2,1,0:T(8,128)(2,1)}, bf16[2,256,128]{2,1,0:T(8,128)(2,1)S(1)}, u32[]{:S(2)}, u32[]{:S(2)}) %collective-permute-start.6) | collective-permute-done | bytes 131104 | tf_op jit(solution)/shard_map/ppermute | solution.py:400
  38.4 2.2 %shard_map.49 = (bf16[272,256]{1,0:T(8,128)(2,1)S(1)}, bf16[272,256]{1,0:T(8,128)(2,1)S(1)}, bf16[272,256]{1,0:T(8,128)(2,1)S(1)}, bf16[272,256]{1,0:T(8,128)(2,...) custom-call(s32[1]{0:T(128)} %bitcast.me_ref, ...), custom_call_target="tpu_custom_call" | custom-call | flops 1 | bytes 1 | tf_op jit(solution)/shard_map/pallas_call | solution.py:421
  40.7 1.6 %collective-permute-start.7 = (bf16[272,256]{1,0:T(8,128)(2,1)S(1)}, bf16[272,256]{1,0:T(8,128)(2,1)S(1)}, u32[]{:S(2)}, u32[]{:S(2)}) collective-permute-start(bf16[272,256]{1,0:T(8,128)(2,1)S(1)} %get-tuple-element.70), channel_id=1, source_target_pairs={{0,4},{4,0},{8,12},{12,8},{16,20},{20,16},{24,28},{28,24},{1,5},{5... | collective-permute-start | bytes 417800 | tf_op jit(solution)/shard_map/ppermute | solution.py:432
  42.2 3.8 %collective-permute-start.8 = (bf16[272,128]{1,0:T(8,128)(2,1)S(1)}, bf16[272,128]{1,0:T(8,128)(2,1)S(1)}, u32[]{:S(2)}, u32[]{:S(2)}) collective-permute-start(bf16[272,128]{1,0:T(8,128)(2,1)S(1)} %get-tuple-element.73), channel_id=1, source_target_pairs={{0,16},{4,20},{8,24},{12,28},{1,17},{5,21},{9,25},{13,29},{2,18},{... | collective-permute-start | bytes 208904 | tf_op jit(solution)/shard_map/ppermute | solution.py:436
  46.3 1.9 %collective-permute-start.13 = (bf16[272,256]{1,0:T(8,128)(2,1)S(1)}, bf16[272,256]{1,0:T(8,128)(2,1)S(1)}, u32[]{:S(2)}, u32[]{:S(2)}) collective-permute-start(bf16[272,256]{1,0:T(8,128)(2,1)S(1)} %get-tuple-element.78), channel_id=1, source_target_pairs={{0,12},{4,8},{8,4},{12,0},{16,28},{20,24},{24,20},{28,16},{1,13},{... | collective-permute-start | bytes 417800 | tf_op jit(solution)/shard_map/ppermute | solution.py:432
  48.2 2.1 %collective-permute-start.9 = (bf16[272,128]{1,0:T(8,128)(2,1)S(1)}, bf16[272,128]{1,0:T(8,128)(2,1)S(1)}, u32[]{:S(2)}, u32[]{:S(2)}) collective-permute-start(bf16[272,128]{1,0:T(8,128)(2,1)S(1)} %get-tuple-element.74), channel_id=1, source_target_pairs={{0,20},{4,16},{8,28},{12,24},{1,21},{5,17},{9,29},{13,25},{2,22},{... | collective-permute-start | bytes 208904 | tf_op jit(solution)/shard_map/ppermute | solution.py:436
  50.3 1.3 %collective-permute-start.11 = (bf16[272,128]{1,0:T(8,128)(2,1)S(1)}, bf16[272,128]{1,0:T(8,128)(2,1)S(1)}, u32[]{:S(2)}, u32[]{:S(2)}) collective-permute-start(bf16[272,128]{1,0:T(8,128)(2,1)S(1)} %get-tuple-element.76), channel_id=1, source_target_pairs={{0,28},{4,24},{8,20},{12,16},{1,29},{5,25},{9,21},{13,17},{2,30},{... | collective-permute-start | bytes 208904 | tf_op jit(solution)/shard_map/ppermute | solution.py:436
  60.0 1.6 %collective-permute-start.18 = (bf16[256,2048]{1,0:T(8,128)(2,1)S(1)}, bf16[256,2048]{1,0:T(8,128)(2,1)S(1)}, u32[]{:S(2)}, u32[]{:S(2)}) collective-permute-start(bf16[256,2048]{1,0:T(8,128)(2,1)S(1)} %add_convert_fusion), channel_id=1, source_target_pairs={{0,2},{1,3},{2,0},{3,1},{4,6},{5,7},{6,4},{7,5},{8,10},{9,11},{10,... | collective-permute-start | bytes 3145736 | tf_op jit(solution)/shard_map/ppermute | solution.py:462
  61.7 4.0 %shard_map.53 = (bf16[1024,2048]{1,0:T(8,128)(2,1)S(1)}, bf16[1024,2048]{1,0:T(8,128)(2,1)S(1)}) custom-call(s32[3]{0:T(128)S(1)} %pad_add_fusion.1.place_ref, bf16[1024,8192]{1,0:T(8,128)(2,1)} %w_ref.2), custom_call_target="tpu_custom_call" | custom-call | flops 1 | bytes 16777216 | tf_op jit(solution)/shard_map/pallas_call | solution.py:339
  65.7 2.4 %shard_map.54 = (bf16[256,2048]{1,0:T(8,128)(2,1)S(1)}, bf16[256,2048]{1,0:T(8,128)(2,1)S(1)}) custom-call(bf16[256,1024]{1,0:T(8,128)(2,1)S(1)} %get-tuple-element.91.heads, bf16[1024,2048]{1,0:T(8,128)(2,1)S(1)} %get-tuple-element.93.refs_0_, bf16[1024,2048]{1,0:T(8,128)(2,1)S(1)} %get-tuple-element.94.refs_1_), custom_call_target="tpu_custom_call" | custom-call | flops 1 | bytes 1 | tf_op jit(solution)/shard_map/pallas_call | solution.py:314
  68.8 1.4 %collective-permute-done.17.refs_1_ = bf16[256,1024]{1,0:T(8,128)(2,1)S(1)} collective-permute-done((bf16[256,1024]{1,0:T(8,128)(2,1)S(1)}, bf16[256,1024]{1,0:T(8,128)(2,1)S(1)}, u32[]{:S(2)}, u32[]{:S(2)}) %collective-permute-start.17) | collective-permute-done | bytes 524320 | tf_op jit(solution)/shard_map/ppermute | solution.py:468
  70.9 14.6 %collective-permute-done.18.refs_2_ = bf16[256,2048]{1,0:T(8,128)(2,1)S(1)} collective-permute-done((bf16[256,2048]{1,0:T(8,128)(2,1)S(1)}, bf16[256,2048]{1,0:T(8,128)(2,1)S(1)}, u32[]{:S(2)}, u32[]{:S(2)}) %collective-permute-start.18) | collective-permute-done | bytes 1048608 | tf_op jit(solution)/shard_map/ppermute | solution.py:462
  (30 shorter events, 11.2 us)
Async XLA Ops:
  3.0 15.1 %collective-permute-start = (bf16[3,256,256]{2,1,0:T(8,128)(2,1)}, bf16[3,256,256]{2,1,0:T(8,128)(2,1)S(1)}, u32[]{:S(2)}, u32[]{:S(2)}) collective-permute-start(bf16[3,256,256]{2,1,0:T(8,128)(2,1)} %get-tuple-element.52), channel_id=1, source_target_pairs={{0,4},{4,0},{8,12},{12,8},{16,20},{20,16},{24,28},{28,24},{1,5},{5... | collective-permute-start | bytes 1179656 | tf_op jit(solution)/shard_map/ppermute | solution.py:398
  6.0 17.9 %collective-permute-start.1 = (bf16[3,256,256]{2,1,0:T(8,128)(2,1)}, bf16[3,256,256]{2,1,0:T(8,128)(2,1)S(1)}, u32[]{:S(2)}, u32[]{:S(2)}) collective-permute-start(bf16[3,256,256]{2,1,0:T(8,128)(2,1)} %get-tuple-element.53), channel_id=1, source_target_pairs={{0,8},{4,12},{8,0},{12,4},{16,24},{20,28},{24,16},{28,20},{1,9},{5... | collective-permute-start | bytes 1179656 | tf_op jit(solution)/shard_map/ppermute | solution.py:398
  7.5 23.9 %collective-permute-start.2 = (bf16[3,256,256]{2,1,0:T(8,128)(2,1)}, bf16[3,256,256]{2,1,0:T(8,128)(2,1)S(1)}, u32[]{:S(2)}, u32[]{:S(2)}) collective-permute-start(bf16[3,256,256]{2,1,0:T(8,128)(2,1)} %get-tuple-element.54), channel_id=1, source_target_pairs={{0,12},{4,8},{8,4},{12,0},{16,28},{20,24},{24,20},{28,16},{1,13},{... | collective-permute-start | bytes 1179656 | tf_op jit(solution)/shard_map/ppermute | solution.py:398
  7.5 26.9 %collective-permute-start.3 = (bf16[2,256,128]{2,1,0:T(8,128)(2,1)}, bf16[2,256,128]{2,1,0:T(8,128)(2,1)S(1)}, u32[]{:S(2)}, u32[]{:S(2)}) collective-permute-start(bf16[2,256,128]{2,1,0:T(8,128)(2,1)} %get-tuple-element.60), channel_id=1, source_target_pairs={{0,16},{4,20},{8,24},{12,28},{16,0},{20,4},{24,8},{28,12},{1,17},{... | collective-permute-start | bytes 393224 | tf_op jit(solution)/shard_map/ppermute | solution.py:400
  10.5 24.0 %collective-permute-start.4 = (bf16[2,256,128]{2,1,0:T(8,128)(2,1)}, bf16[2,256,128]{2,1,0:T(8,128)(2,1)S(1)}, u32[]{:S(2)}, u32[]{:S(2)}) collective-permute-start(bf16[2,256,128]{2,1,0:T(8,128)(2,1)} %get-tuple-element.61), channel_id=1, source_target_pairs={{0,20},{4,16},{8,28},{12,24},{16,4},{20,0},{24,12},{28,8},{1,21},{... | collective-permute-start | bytes 393224 | tf_op jit(solution)/shard_map/ppermute | solution.py:400
  18.1 19.0 %collective-permute-start.5 = (bf16[2,256,128]{2,1,0:T(8,128)(2,1)}, bf16[2,256,128]{2,1,0:T(8,128)(2,1)S(1)}, u32[]{:S(2)}, u32[]{:S(2)}) collective-permute-start(bf16[2,256,128]{2,1,0:T(8,128)(2,1)} %get-tuple-element.62), channel_id=1, source_target_pairs={{0,24},{4,28},{8,16},{12,20},{16,8},{20,12},{24,0},{28,4},{1,25},{... | collective-permute-start | bytes 393224 | tf_op jit(solution)/shard_map/ppermute | solution.py:400
  23.8 14.6 %collective-permute-start.6 = (bf16[2,256,128]{2,1,0:T(8,128)(2,1)}, bf16[2,256,128]{2,1,0:T(8,128)(2,1)S(1)}, u32[]{:S(2)}, u32[]{:S(2)}) collective-permute-start(bf16[2,256,128]{2,1,0:T(8,128)(2,1)} %get-tuple-element.63), channel_id=1, source_target_pairs={{0,28},{4,24},{8,20},{12,16},{16,12},{20,8},{24,4},{28,0},{1,29},{... | collective-permute-start | bytes 393224 | tf_op jit(solution)/shard_map/ppermute | solution.py:400
  27.4 4.1 %copy-start = (bf16[3,256,256]{2,1,0:T(8,128)(2,1)S(1)}, bf16[3,256,256]{2,1,0:T(8,128)(2,1)}, u32[]{:S(2)}) copy-start(bf16[3,256,256]{2,1,0:T(8,128)(2,1)} %get-tuple-element.51.refs_0_) | copy-start | bytes 1179652
  40.7 9.7 %collective-permute-start.7 = (bf16[272,256]{1,0:T(8,128)(2,1)S(1)}, bf16[272,256]{1,0:T(8,128)(2,1)S(1)}, u32[]{:S(2)}, u32[]{:S(2)}) collective-permute-start(bf16[272,256]{1,0:T(8,128)(2,1)S(1)} %get-tuple-element.70), channel_id=1, source_target_pairs={{0,4},{4,0},{8,12},{12,8},{16,20},{20,16},{24,28},{28,24},{1,5},{5... | collective-permute-start | bytes 417800 | tf_op jit(solution)/shard_map/ppermute | solution.py:432
  42.2 9.4 %collective-permute-start.8 = (bf16[272,128]{1,0:T(8,128)(2,1)S(1)}, bf16[272,128]{1,0:T(8,128)(2,1)S(1)}, u32[]{:S(2)}, u32[]{:S(2)}) collective-permute-start(bf16[272,128]{1,0:T(8,128)(2,1)S(1)} %get-tuple-element.73), channel_id=1, source_target_pairs={{0,16},{4,20},{8,24},{12,28},{1,17},{5,21},{9,25},{13,29},{2,18},{... | collective-permute-start | bytes 208904 | tf_op jit(solution)/shard_map/ppermute | solution.py:436
  46.0 7.9 %collective-permute-start.12 = (bf16[272,256]{1,0:T(8,128)(2,1)S(1)}, bf16[272,256]{1,0:T(8,128)(2,1)S(1)}, u32[]{:S(2)}, u32[]{:S(2)}) collective-permute-start(bf16[272,256]{1,0:T(8,128)(2,1)S(1)} %get-tuple-element.77), channel_id=1, source_target_pairs={{0,8},{4,12},{8,0},{12,4},{16,24},{20,28},{24,16},{28,20},{1,9},{5... | collective-permute-start | bytes 417800 | tf_op jit(solution)/shard_map/ppermute | solution.py:432
  46.3 7.7 %collective-permute-start.13 = (bf16[272,256]{1,0:T(8,128)(2,1)S(1)}, bf16[272,256]{1,0:T(8,128)(2,1)S(1)}, u32[]{:S(2)}, u32[]{:S(2)}) collective-permute-start(bf16[272,256]{1,0:T(8,128)(2,1)S(1)} %get-tuple-element.78), channel_id=1, source_target_pairs={{0,12},{4,8},{8,4},{12,0},{16,28},{20,24},{24,20},{28,16},{1,13},{... | collective-permute-start | bytes 417800 | tf_op jit(solution)/shard_map/ppermute | solution.py:432
  48.2 5.7 %collective-permute-start.9 = (bf16[272,128]{1,0:T(8,128)(2,1)S(1)}, bf16[272,128]{1,0:T(8,128)(2,1)S(1)}, u32[]{:S(2)}, u32[]{:S(2)}) collective-permute-start(bf16[272,128]{1,0:T(8,128)(2,1)S(1)} %get-tuple-element.74), channel_id=1, source_target_pairs={{0,20},{4,16},{8,28},{12,24},{1,21},{5,17},{9,29},{13,25},{2,22},{... | collective-permute-start | bytes 208904 | tf_op jit(solution)/shard_map/ppermute | solution.py:436
  50.3 4.3 %collective-permute-start.11 = (bf16[272,128]{1,0:T(8,128)(2,1)S(1)}, bf16[272,128]{1,0:T(8,128)(2,1)S(1)}, u32[]{:S(2)}, u32[]{:S(2)}) collective-permute-start(bf16[272,128]{1,0:T(8,128)(2,1)S(1)} %get-tuple-element.76), channel_id=1, source_target_pairs={{0,28},{4,24},{8,20},{12,16},{1,29},{5,25},{9,21},{13,17},{2,30},{... | collective-permute-start | bytes 208904 | tf_op jit(solution)/shard_map/ppermute | solution.py:436
  51.7 3.8 %collective-permute-start.10 = (bf16[272,128]{1,0:T(8,128)(2,1)S(1)}, bf16[272,128]{1,0:T(8,128)(2,1)S(1)}, u32[]{:S(2)}, u32[]{:S(2)}) collective-permute-start(bf16[272,128]{1,0:T(8,128)(2,1)S(1)} %get-tuple-element.75), channel_id=1, source_target_pairs={{0,24},{4,28},{8,16},{12,20},{1,25},{5,29},{9,17},{13,21},{2,26},{... | collective-permute-start | bytes 208904 | tf_op jit(solution)/shard_map/ppermute | solution.py:436
  56.7 2.6 %collective-permute-start.14 = (bf16[256,1024]{1,0:T(8,128)(2,1)S(1)}, bf16[256,1024]{1,0:T(8,128)(2,1)S(1)}, u32[]{:S(2)}, u32[]{:S(2)}) collective-permute-start(bf16[256,1024]{1,0:T(8,128)(2,1)S(1)} %get-tuple-element.89), channel_id=1, source_target_pairs={{0,1},{1,0},{2,3},{3,2},{4,5},{5,4},{6,7},{7,6},{8,9},{9,8},{10,11... | collective-permute-start | bytes 1572872 | tf_op jit(solution)/shard_map/ppermute | solution.py:460
  57.5 2.1 %collective-permute-start.15 = (bf16[256,1024]{1,0:T(8,128)(2,1)S(1)}, bf16[256,1024]{1,0:T(8,128)(2,1)S(1)}, u32[]{:S(2)}, u32[]{:S(2)}) collective-permute-start(bf16[256,1024]{1,0:T(8,128)(2,1)S(1)} %shard_map.52), channel_id=1, source_target_pairs={{0,1},{1,0},{2,3},{3,2},{4,5},{5,4},{6,7},{7,6},{8,9},{9,8},{10,11... | collective-permute-start | bytes 1572872 | tf_op jit(solution)/shard_map/ppermute | solution.py:460
  60.0 25.5 %collective-permute-start.18 = (bf16[256,2048]{1,0:T(8,128)(2,1)S(1)}, bf16[256,2048]{1,0:T(8,128)(2,1)S(1)}, u32[]{:S(2)}, u32[]{:S(2)}) collective-permute-start(bf16[256,2048]{1,0:T(8,128)(2,1)S(1)} %add_convert_fusion), channel_id=1, source_target_pairs={{0,2},{1,3},{2,0},{3,1},{4,6},{5,7},{6,4},{7,5},{8,10},{9,11},{10,... | collective-permute-start | bytes 3145736 | tf_op jit(solution)/shard_map/ppermute | solution.py:462
  68.2 2.0 %collective-permute-start.17 = (bf16[256,1024]{1,0:T(8,128)(2,1)S(1)}, bf16[256,1024]{1,0:T(8,128)(2,1)S(1)}, u32[]{:S(2)}, u32[]{:S(2)}) collective-permute-start(bf16[256,1024]{1,0:T(8,128)(2,1)S(1)} %get-tuple-element.97), channel_id=1, source_target_pairs={{0,1},{1,0},{2,3},{3,2},{4,5},{5,4},{6,7},{7,6},{8,9},{9,8},{10,11... | collective-permute-start | bytes 1572872 | tf_op jit(solution)/shard_map/ppermute | solution.py:468
  68.3 2.6 %collective-permute-start.16 = (bf16[256,1024]{1,0:T(8,128)(2,1)S(1)}, bf16[256,1024]{1,0:T(8,128)(2,1)S(1)}, u32[]{:S(2)}, u32[]{:S(2)}) collective-permute-start(bf16[256,1024]{1,0:T(8,128)(2,1)S(1)} %get-tuple-element.98), channel_id=1, source_target_pairs={{0,1},{1,0},{2,3},{3,2},{4,5},{5,4},{6,7},{7,6},{8,9},{9,8},{10,11... | collective-permute-start | bytes 1572872 | tf_op jit(solution)/shard_map/ppermute | solution.py:468

commit v9 on v6

--- a/solution.py
+++ b/solution.py
@@ -278,7 +278,7 @@
 
 
 def first_kernel(half, tile, me_ref, *refs):
-    back, over, (weight, heads, out) = refs[:half], refs[half : 2 * half], refs[2 * half :]
+    over, back, (weight, heads, out) = refs[:half], refs[half : 2 * half], refs[2 * half :]
     assemble(half, me_ref, back, over, heads)
     multiply(heads, weight, out, tile)
 
@@ -433,9 +433,6 @@
             over[shift], back[1] = lax.optimization_barrier((over[shift], back[1]))
         over[shift] = lax.ppermute(over[shift], "ctx", between(shift, 1, 0))
 
-    tied = (back[1], *over, *back[2:])
-    back[1], *tied = lax.optimization_barrier(tied)
-    over, back[2:] = tied[:half], tied[half:]
     heads, crossing = None, []
     for shift, (w_give, w_keep) in enumerate(near, 1):
         perm = [(i, (i + 2 * shift) % tp) for i in range(tp)]
@@ -450,7 +447,7 @@
                 ],
                 compiler_params=params(16),
                 cost_estimate=COST,
-            )(place, *back, *over, w_give)
+            )(place, *over, *back, w_give)
         else:
             (give,) = project(heads, [w_give])
         (keep,) = project(heads, [w_keep])

time: 87.2 us -> 87.2 us (level)
  no operation moved by 1% of the time
where the time goes in v9:
time: 87.2 us; the launch traced here: 86.8 us
  waiting for transfers between devices  32.6 us (37%)
  starting transfers between devices  30.6 us (35%)
  Pallas kernels  22.8 us (26%)
    ppermute x1, waiting for transfers between devices, heads_form(): crossing.append(lax.ppermute(both, 'tp', perm))  14.4 us
    ppermute x4, starting transfers between devices, heads_form(): lax.ppermute(piece, 'ctx', between(shift, 1, 1))  11.5 us
    ppermute x4, starting transfers between devices, heads_form(): over[shift] = lax.ppermute(over[shift], 'ctx', between(shift, 1, 0))  8.55 us
    ppermute x3, waiting for transfers between devices, heads_form(): inner[shift] = lax.ppermute(inner[shift], 'ctx', within(shift))  8.24 us
    pallas_call x2, Pallas kernels, fetch(): pl.pallas_call(fetch_kernel, in_specs=[pl.BlockSpec(memory_space=pltpu.SM...  8.07 us
    ppermute x3, starting transfers between devices, heads_form(): inner[shift] = lax.ppermute(inner[shift], 'ctx', within(shift))  4.58 us
    ppermute x4, waiting for transfers between devices, heads_form(): lax.ppermute(piece, 'ctx', between(shift, 1, 1))  3.96 us
    ppermute x3, starting transfers between devices, heads_form(): back[shift] = lax.ppermute(back[shift], 'ctx', within(shift))  3.69 us
  transfers between devices with their start and end apart: 18, of which 11 were waited for; matrix products, arithmetic and copies ran while one was open for 0% of the time, Pallas kernels for 17%

profile of v9, /device:TPU:0, one launch (start us, length us, event | category | flops | bytes accessed | tf_op | source)
XLA Modules:
  0.0 86.8 jit_solution(3523390681041824485)
XLA Ops:
  0.0 2.9 %shard_map.46 = (bf16[3,256,256]{2,1,0:T(8,128)(2,1)}, bf16[3,256,256]{2,1,0:T(8,128)(2,1)}, bf16[3,256,256]{2,1,0:T(8,128)(2,1)}, bf16[3,256,256]{2,1,0:T(8,128...) custom-call(s32[1]{0:T(128)} %bitcast.me_ref, ...), custom_call_target="tpu_custom_call" | custom-call | flops 1 | bytes 1 | tf_op jit(solution)/shard_map/pallas_call | solution.py:369
  3.0 3.0 %collective-permute-start = (bf16[3,256,256]{2,1,0:T(8,128)(2,1)}, bf16[3,256,256]{2,1,0:T(8,128)(2,1)S(1)}, u32[]{:S(2)}, u32[]{:S(2)}) collective-permute-start(bf16[3,256,256]{2,1,0:T(8,128)(2,1)} %get-tuple-element.45), channel_id=1, source_target_pairs={{0,4},{4,0},{8,12},{12,8},{16,20},{20,16},{24,28},{28,24},{1,5},{5... | collective-permute-start | bytes 1179656 | tf_op jit(solution)/shard_map/ppermute | solution.py:396
  6.0 1.6 %collective-permute-start.1 = (bf16[3,256,256]{2,1,0:T(8,128)(2,1)}, bf16[3,256,256]{2,1,0:T(8,128)(2,1)S(1)}, u32[]{:S(2)}, u32[]{:S(2)}) collective-permute-start(bf16[3,256,256]{2,1,0:T(8,128)(2,1)} %get-tuple-element.46), channel_id=1, source_target_pairs={{0,8},{4,12},{8,0},{12,4},{16,24},{20,28},{24,16},{28,20},{1,9},{5... | collective-permute-start | bytes 1179656 | tf_op jit(solution)/shard_map/ppermute | solution.py:396
  7.5 2.9 %collective-permute-start.3 = (bf16[2,256,128]{2,1,0:T(8,128)(2,1)}, bf16[2,256,128]{2,1,0:T(8,128)(2,1)S(1)}, u32[]{:S(2)}, u32[]{:S(2)}) collective-permute-start(bf16[2,256,128]{2,1,0:T(8,128)(2,1)} %get-tuple-element.53), channel_id=1, source_target_pairs={{0,16},{4,20},{8,24},{12,28},{16,0},{20,4},{24,8},{28,12},{1,17},{... | collective-permute-start | bytes 393224 | tf_op jit(solution)/shard_map/ppermute | solution.py:398
  11.8 6.3 %collective-permute-done.refs_1_ = bf16[3,256,256]{2,1,0:T(8,128)(2,1)S(1)} collective-permute-done((bf16[3,256,256]{2,1,0:T(8,128)(2,1)}, bf16[3,256,256]{2,1,0:T(8,128)(2,1)S(1)}, u32[]{:S(2)}, u32[]{:S(2)}) %collective-permute-start) | collective-permute-done | bytes 393248 | tf_op jit(solution)/shard_map/ppermute | solution.py:396
  18.1 3.8 %collective-permute-start.5 = (bf16[2,256,128]{2,1,0:T(8,128)(2,1)}, bf16[2,256,128]{2,1,0:T(8,128)(2,1)S(1)}, u32[]{:S(2)}, u32[]{:S(2)}) collective-permute-start(bf16[2,256,128]{2,1,0:T(8,128)(2,1)} %get-tuple-element.55), channel_id=1, source_target_pairs={{0,24},{4,28},{8,16},{12,20},{16,8},{20,12},{24,0},{28,4},{1,25},{... | collective-permute-start | bytes 393224 | tf_op jit(solution)/shard_map/ppermute | solution.py:398
  21.9 2.0 %collective-permute-done.1.refs_2_ = bf16[3,256,256]{2,1,0:T(8,128)(2,1)S(1)} collective-permute-done((bf16[3,256,256]{2,1,0:T(8,128)(2,1)}, bf16[3,256,256]{2,1,0:T(8,128)(2,1)S(1)}, u32[]{:S(2)}, u32[]{:S(2)}) %collective-permute-start.1) | collective-permute-done | bytes 393248 | tf_op jit(solution)/shard_map/ppermute | solution.py:396
  23.8 3.5 %collective-permute-start.6 = (bf16[2,256,128]{2,1,0:T(8,128)(2,1)}, bf16[2,256,128]{2,1,0:T(8,128)(2,1)S(1)}, u32[]{:S(2)}, u32[]{:S(2)}) collective-permute-start(bf16[2,256,128]{2,1,0:T(8,128)(2,1)} %get-tuple-element.56), channel_id=1, source_target_pairs={{0,28},{4,24},{8,20},{12,16},{16,12},{20,8},{24,4},{28,0},{1,29},{... | collective-permute-start | bytes 393224 | tf_op jit(solution)/shard_map/ppermute | solution.py:398
  27.4 4.0 %shard_map.47 = (bf16[1024,2048]{1,0:T(8,128)(2,1)S(1)}, bf16[1024,2048]{1,0:T(8,128)(2,1)S(1)}) custom-call(s32[3]{0:T(128)S(1)} %pad_add_fusion.place_ref, bf16[1024,8192]{1,0:T(8,128)(2,1)} %w_ref.2), custom_call_target="tpu_custom_call" | custom-call | flops 1 | bytes 16777216 | tf_op jit(solution)/shard_map/pallas_call | solution.py:337
  31.5 3.0 %shard_map.48 = (bf16[1024,128]{1,0:T(8,128)(2,1)S(1)}, f32[1024,128]{1,0:T(8,128)S(1)}, f32[256,128]{1,0:T(8,128)S(1)}) custom-call(s32[1]{0:T(128)} %bitcast.me_ref, bf16[3,256,256]{2,1,0:T(8,128)(2,1)S(1)} %copy-done, bf16[3,256,256]{2,1,0:T(8,128)(2,1)S(1)} %collective-permute-done.refs_1_, bf16[3,256,256]{2,1,0:T(8,128)(2,1)S(1)} %collective-permute-done.1.refs_2_, ...), custom_call_target="tpu_custom_call" | custom-call | flops 1 | bytes 1 | tf_op jit(solution)/shard_map/pallas_call | solution.py:406
  34.5 2.6 %collective-permute-done.5.refs_6_ = bf16[2,256,128]{2,1,0:T(8,128)(2,1)S(1)} collective-permute-done((bf16[2,256,128]{2,1,0:T(8,128)(2,1)}, bf16[2,256,128]{2,1,0:T(8,128)(2,1)S(1)}, u32[]{:S(2)}, u32[]{:S(2)}) %collective-permute-start.5) | collective-permute-done | bytes 131104 | tf_op jit(solution)/shard_map/ppermute | solution.py:398
  37.0 1.4 %collective-permute-done.6.refs_7_ = bf16[2,256,128]{2,1,0:T(8,128)(2,1)S(1)} collective-permute-done((bf16[2,256,128]{2,1,0:T(8,128)(2,1)}, bf16[2,256,128]{2,1,0:T(8,128)(2,1)S(1)}, u32[]{:S(2)}, u32[]{:S(2)}) %collective-permute-start.6) | collective-permute-done | bytes 131104 | tf_op jit(solution)/shard_map/ppermute | solution.py:398
  38.4 2.2 %shard_map.49 = (bf16[272,256]{1,0:T(8,128)(2,1)S(1)}, bf16[272,256]{1,0:T(8,128)(2,1)S(1)}, bf16[272,256]{1,0:T(8,128)(2,1)S(1)}, bf16[272,256]{1,0:T(8,128)(2,...) custom-call(s32[1]{0:T(128)} %bitcast.me_ref, ...), custom_call_target="tpu_custom_call" | custom-call | flops 1 | bytes 1 | tf_op jit(solution)/shard_map/pallas_call | solution.py:419
  40.6 1.6 %collective-permute-start.9 = (bf16[272,256]{1,0:T(8,128)(2,1)S(1)}, bf16[272,256]{1,0:T(8,128)(2,1)S(1)}, u32[]{:S(2)}, u32[]{:S(2)}) collective-permute-start(bf16[272,256]{1,0:T(8,128)(2,1)S(1)} %get-tuple-element.63), channel_id=1, source_target_pairs={{0,4},{4,0},{8,12},{12,8},{16,20},{20,16},{24,28},{28,24},{1,5},{5... | collective-permute-start | bytes 417800 | tf_op jit(solution)/shard_map/ppermute | solution.py:430
  42.2 3.8 %collective-permute-start.7 = (bf16[272,128]{1,0:T(8,128)(2,1)S(1)}, bf16[272,128]{1,0:T(8,128)(2,1)S(1)}, u32[]{:S(2)}, u32[]{:S(2)}) collective-permute-start(bf16[272,128]{1,0:T(8,128)(2,1)S(1)} %get-tuple-element.60), channel_id=1, source_target_pairs={{0,16},{4,20},{8,24},{12,28},{1,17},{5,21},{9,25},{13,29},{2,18},{... | collective-permute-start | bytes 208904 | tf_op jit(solution)/shard_map/ppermute | solution.py:434
  46.2 1.9 %collective-permute-start.13 = (bf16[272,256]{1,0:T(8,128)(2,1)S(1)}, bf16[272,256]{1,0:T(8,128)(2,1)S(1)}, u32[]{:S(2)}, u32[]{:S(2)}) collective-permute-start(bf16[272,256]{1,0:T(8,128)(2,1)S(1)} %get-tuple-element.71), channel_id=1, source_target_pairs={{0,12},{4,8},{8,4},{12,0},{16,28},{20,24},{24,20},{28,16},{1,13},{... | collective-permute-start | bytes 417800 | tf_op jit(solution)/shard_map/ppermute | solution.py:430
  48.2 2.1 %collective-permute-start.8 = (bf16[272,128]{1,0:T(8,128)(2,1)S(1)}, bf16[272,128]{1,0:T(8,128)(2,1)S(1)}, u32[]{:S(2)}, u32[]{:S(2)}) collective-permute-start(bf16[272,128]{1,0:T(8,128)(2,1)S(1)} %get-tuple-element.61), channel_id=1, source_target_pairs={{0,20},{4,16},{8,28},{12,24},{1,21},{5,17},{9,29},{13,25},{2,22},{... | collective-permute-start | bytes 208904 | tf_op jit(solution)/shard_map/ppermute | solution.py:434
  55.4 1.8 %shard_map.50 = (bf16[256,1024]{1,0:T(8,128)(2,1)S(1)}, bf16[256,2048]{1,0:T(8,128)(2,1)S(1)}) custom-call(s32[1]{0:T(128)} %bitcast.me_ref, bf16[272,128]{1,0:T(8,128)(2,1)S(1)} %collective-permute-done.7.refs_0_, bf16[272,128]{1,0:T(8,128)(2,1)S(1)} %collective-permute-done.8.refs_1_, bf16[272,128]{1,0:T(8,128)(2,1)S(1)} %collective-permute-done.10.refs_2_, ...), custom_call_target="tpu_custom_call" | custom-call | flops 1 | bytes 1 | tf_op jit(solution)/shard_map/pallas_call | solution.py:440
  58.6 1.4 %collective-permute-done.14 = bf16[256,2048]{1,0:T(8,128)(2,1)S(1)} collective-permute-done((bf16[256,2048]{1,0:T(8,128)(2,1)S(1)}, bf16[256,2048]{1,0:T(8,128)(2,1)S(1)}, u32[]{:S(2)}, u32[]{:S(2)}) %collective-permute-start.14) | collective-permute-done | bytes 1048608 | tf_op jit(solution)/shard_map/ppermute | solution.py:454
  60.4 1.6 %collective-permute-start.17 = (bf16[256,2048]{1,0:T(8,128)(2,1)S(1)}, bf16[256,2048]{1,0:T(8,128)(2,1)S(1)}, u32[]{:S(2)}, u32[]{:S(2)}) collective-permute-start(bf16[256,2048]{1,0:T(8,128)(2,1)S(1)} %add_convert_fusion), channel_id=1, source_target_pairs={{0,2},{1,3},{2,0},{3,1},{4,6},{5,7},{6,4},{7,5},{8,10},{9,11},{10,... | collective-permute-start | bytes 3145736 | tf_op jit(solution)/shard_map/ppermute | solution.py:455
  62.0 4.0 %shard_map.52 = (bf16[1024,2048]{1,0:T(8,128)(2,1)S(1)}, bf16[1024,2048]{1,0:T(8,128)(2,1)S(1)}) custom-call(s32[3]{0:T(128)S(1)} %pad_add_fusion.1.place_ref, bf16[1024,8192]{1,0:T(8,128)(2,1)} %w_ref.2), custom_call_target="tpu_custom_call" | custom-call | flops 1 | bytes 16777216 | tf_op jit(solution)/shard_map/pallas_call | solution.py:337
  66.1 2.4 %shard_map.53 = (bf16[256,2048]{1,0:T(8,128)(2,1)S(1)}, bf16[256,2048]{1,0:T(8,128)(2,1)S(1)}) custom-call(bf16[256,1024]{1,0:T(8,128)(2,1)S(1)} %get-tuple-element.77.heads, bf16[1024,2048]{1,0:T(8,128)(2,1)S(1)} %get-tuple-element.79.refs_0_, bf16[1024,2048]{1,0:T(8,128)(2,1)S(1)} %get-tuple-element.80.refs_1_), custom_call_target="tpu_custom_call" | custom-call | flops 1 | bytes 1 | tf_op jit(solution)/shard_map/pallas_call | solution.py:312
  69.1 1.4 %collective-permute-done.16.refs_1_ = bf16[256,1024]{1,0:T(8,128)(2,1)S(1)} collective-permute-done((bf16[256,1024]{1,0:T(8,128)(2,1)S(1)}, bf16[256,1024]{1,0:T(8,128)(2,1)S(1)}, u32[]{:S(2)}, u32[]{:S(2)}) %collective-permute-start.16) | collective-permute-done | bytes 524320 | tf_op jit(solution)/shard_map/ppermute | solution.py:461
  71.3 14.4 %collective-permute-done.17.refs_2_ = bf16[256,2048]{1,0:T(8,128)(2,1)S(1)} collective-permute-done((bf16[256,2048]{1,0:T(8,128)(2,1)S(1)}, bf16[256,2048]{1,0:T(8,128)(2,1)S(1)}, u32[]{:S(2)}, u32[]{:S(2)}) %collective-permute-start.17) | collective-permute-done | bytes 1048608 | tf_op jit(solution)/shard_map/ppermute | solution.py:455
  (27 shorter events, 11.0 us)
Async XLA Ops:
  3.0 15.1 %collective-permute-start = (bf16[3,256,256]{2,1,0:T(8,128)(2,1)}, bf16[3,256,256]{2,1,0:T(8,128)(2,1)S(1)}, u32[]{:S(2)}, u32[]{:S(2)}) collective-permute-start(bf16[3,256,256]{2,1,0:T(8,128)(2,1)} %get-tuple-element.45), channel_id=1, source_target_pairs={{0,4},{4,0},{8,12},{12,8},{16,20},{20,16},{24,28},{28,24},{1,5},{5... | collective-permute-start | bytes 1179656 | tf_op jit(solution)/shard_map/ppermute | solution.py:396
  6.0 17.9 %collective-permute-start.1 = (bf16[3,256,256]{2,1,0:T(8,128)(2,1)}, bf16[3,256,256]{2,1,0:T(8,128)(2,1)S(1)}, u32[]{:S(2)}, u32[]{:S(2)}) collective-permute-start(bf16[3,256,256]{2,1,0:T(8,128)(2,1)} %get-tuple-element.46), channel_id=1, source_target_pairs={{0,8},{4,12},{8,0},{12,4},{16,24},{20,28},{24,16},{28,20},{1,9},{5... | collective-permute-start | bytes 1179656 | tf_op jit(solution)/shard_map/ppermute | solution.py:396
  7.5 23.9 %collective-permute-start.2 = (bf16[3,256,256]{2,1,0:T(8,128)(2,1)}, bf16[3,256,256]{2,1,0:T(8,128)(2,1)S(1)}, u32[]{:S(2)}, u32[]{:S(2)}) collective-permute-start(bf16[3,256,256]{2,1,0:T(8,128)(2,1)} %get-tuple-element.47), channel_id=1, source_target_pairs={{0,12},{4,8},{8,4},{12,0},{16,28},{20,24},{24,20},{28,16},{1,13},{... | collective-permute-start | bytes 1179656 | tf_op jit(solution)/shard_map/ppermute | solution.py:396
  7.5 26.9 %collective-permute-start.3 = (bf16[2,256,128]{2,1,0:T(8,128)(2,1)}, bf16[2,256,128]{2,1,0:T(8,128)(2,1)S(1)}, u32[]{:S(2)}, u32[]{:S(2)}) collective-permute-start(bf16[2,256,128]{2,1,0:T(8,128)(2,1)} %get-tuple-element.53), channel_id=1, source_target_pairs={{0,16},{4,20},{8,24},{12,28},{16,0},{20,4},{24,8},{28,12},{1,17},{... | collective-permute-start | bytes 393224 | tf_op jit(solution)/shard_map/ppermute | solution.py:398
  10.5 24.0 %collective-permute-start.4 = (bf16[2,256,128]{2,1,0:T(8,128)(2,1)}, bf16[2,256,128]{2,1,0:T(8,128)(2,1)S(1)}, u32[]{:S(2)}, u32[]{:S(2)}) collective-permute-start(bf16[2,256,128]{2,1,0:T(8,128)(2,1)} %get-tuple-element.54), channel_id=1, source_target_pairs={{0,20},{4,16},{8,28},{12,24},{16,4},{20,0},{24,12},{28,8},{1,21},{... | collective-permute-start | bytes 393224 | tf_op jit(solution)/shard_map/ppermute | solution.py:398
  18.1 19.0 %collective-permute-start.5 = (bf16[2,256,128]{2,1,0:T(8,128)(2,1)}, bf16[2,256,128]{2,1,0:T(8,128)(2,1)S(1)}, u32[]{:S(2)}, u32[]{:S(2)}) collective-permute-start(bf16[2,256,128]{2,1,0:T(8,128)(2,1)} %get-tuple-element.55), channel_id=1, source_target_pairs={{0,24},{4,28},{8,16},{12,20},{16,8},{20,12},{24,0},{28,4},{1,25},{... | collective-permute-start | bytes 393224 | tf_op jit(solution)/shard_map/ppermute | solution.py:398
  23.8 14.6 %collective-permute-start.6 = (bf16[2,256,128]{2,1,0:T(8,128)(2,1)}, bf16[2,256,128]{2,1,0:T(8,128)(2,1)S(1)}, u32[]{:S(2)}, u32[]{:S(2)}) collective-permute-start(bf16[2,256,128]{2,1,0:T(8,128)(2,1)} %get-tuple-element.56), channel_id=1, source_target_pairs={{0,28},{4,24},{8,20},{12,16},{16,12},{20,8},{24,4},{28,0},{1,29},{... | collective-permute-start | bytes 393224 | tf_op jit(solution)/shard_map/ppermute | solution.py:398
  27.4 4.1 %copy-start = (bf16[3,256,256]{2,1,0:T(8,128)(2,1)S(1)}, bf16[3,256,256]{2,1,0:T(8,128)(2,1)}, u32[]{:S(2)}) copy-start(bf16[3,256,256]{2,1,0:T(8,128)(2,1)} %get-tuple-element.44.refs_0_) | copy-start | bytes 1179652
  40.6 9.7 %collective-permute-start.9 = (bf16[272,256]{1,0:T(8,128)(2,1)S(1)}, bf16[272,256]{1,0:T(8,128)(2,1)S(1)}, u32[]{:S(2)}, u32[]{:S(2)}) collective-permute-start(bf16[272,256]{1,0:T(8,128)(2,1)S(1)} %get-tuple-element.63), channel_id=1, source_target_pairs={{0,4},{4,0},{8,12},{12,8},{16,20},{20,16},{24,28},{28,24},{1,5},{5... | collective-permute-start | bytes 417800 | tf_op jit(solution)/shard_map/ppermute | solution.py:430
  42.2 9.4 %collective-permute-start.7 = (bf16[272,128]{1,0:T(8,128)(2,1)S(1)}, bf16[272,128]{1,0:T(8,128)(2,1)S(1)}, u32[]{:S(2)}, u32[]{:S(2)}) collective-permute-start(bf16[272,128]{1,0:T(8,128)(2,1)S(1)} %get-tuple-element.60), channel_id=1, source_target_pairs={{0,16},{4,20},{8,24},{12,28},{1,17},{5,21},{9,25},{13,29},{2,18},{... | collective-permute-start | bytes 208904 | tf_op jit(solution)/shard_map/ppermute | solution.py:434
  46.0 7.9 %collective-permute-start.12 = (bf16[272,256]{1,0:T(8,128)(2,1)S(1)}, bf16[272,256]{1,0:T(8,128)(2,1)S(1)}, u32[]{:S(2)}, u32[]{:S(2)}) collective-permute-start(bf16[272,256]{1,0:T(8,128)(2,1)S(1)} %get-tuple-element.70), channel_id=1, source_target_pairs={{0,8},{4,12},{8,0},{12,4},{16,24},{20,28},{24,16},{28,20},{1,9},{5... | collective-permute-start | bytes 417800 | tf_op jit(solution)/shard_map/ppermute | solution.py:430
  46.2 7.7 %collective-permute-start.13 = (bf16[272,256]{1,0:T(8,128)(2,1)S(1)}, bf16[272,256]{1,0:T(8,128)(2,1)S(1)}, u32[]{:S(2)}, u32[]{:S(2)}) collective-permute-start(bf16[272,256]{1,0:T(8,128)(2,1)S(1)} %get-tuple-element.71), channel_id=1, source_target_pairs={{0,12},{4,8},{8,4},{12,0},{16,28},{20,24},{24,20},{28,16},{1,13},{... | collective-permute-start | bytes 417800 | tf_op jit(solution)/shard_map/ppermute | solution.py:430
  48.2 5.7 %collective-permute-start.8 = (bf16[272,128]{1,0:T(8,128)(2,1)S(1)}, bf16[272,128]{1,0:T(8,128)(2,1)S(1)}, u32[]{:S(2)}, u32[]{:S(2)}) collective-permute-start(bf16[272,128]{1,0:T(8,128)(2,1)S(1)} %get-tuple-element.61), channel_id=1, source_target_pairs={{0,20},{4,16},{8,28},{12,24},{1,21},{5,17},{9,29},{13,25},{2,22},{... | collective-permute-start | bytes 208904 | tf_op jit(solution)/shard_map/ppermute | solution.py:434
  50.3 4.3 %collective-permute-start.11 = (bf16[272,128]{1,0:T(8,128)(2,1)S(1)}, bf16[272,128]{1,0:T(8,128)(2,1)S(1)}, u32[]{:S(2)}, u32[]{:S(2)}) collective-permute-start(bf16[272,128]{1,0:T(8,128)(2,1)S(1)} %get-tuple-element.67), channel_id=1, source_target_pairs={{0,28},{4,24},{8,20},{12,16},{1,29},{5,25},{9,21},{13,17},{2,30},{... | collective-permute-start | bytes 208904 | tf_op jit(solution)/shard_map/ppermute | solution.py:434
  51.6 3.8 %collective-permute-start.10 = (bf16[272,128]{1,0:T(8,128)(2,1)S(1)}, bf16[272,128]{1,0:T(8,128)(2,1)S(1)}, u32[]{:S(2)}, u32[]{:S(2)}) collective-permute-start(bf16[272,128]{1,0:T(8,128)(2,1)S(1)} %get-tuple-element.64), channel_id=1, source_target_pairs={{0,24},{4,28},{8,16},{12,20},{1,25},{5,29},{9,17},{13,21},{2,26},{... | collective-permute-start | bytes 208904 | tf_op jit(solution)/shard_map/ppermute | solution.py:434
  57.2 2.7 %collective-permute-start.14 = (bf16[256,2048]{1,0:T(8,128)(2,1)S(1)}, bf16[256,2048]{1,0:T(8,128)(2,1)S(1)}, u32[]{:S(2)}, u32[]{:S(2)}) collective-permute-start(bf16[256,2048]{1,0:T(8,128)(2,1)S(1)} %get-tuple-element.75), channel_id=1, source_target_pairs={{0,1},{1,0},{2,3},{3,2},{4,5},{5,4},{6,7},{7,6},{8,9},{9,8},{10,11... | collective-permute-start | bytes 3145736 | tf_op jit(solution)/shard_map/ppermute | solution.py:454
  60.4 25.3 %collective-permute-start.17 = (bf16[256,2048]{1,0:T(8,128)(2,1)S(1)}, bf16[256,2048]{1,0:T(8,128)(2,1)S(1)}, u32[]{:S(2)}, u32[]{:S(2)}) collective-permute-start(bf16[256,2048]{1,0:T(8,128)(2,1)S(1)} %add_convert_fusion), channel_id=1, source_target_pairs={{0,2},{1,3},{2,0},{3,1},{4,6},{5,7},{6,4},{7,5},{8,10},{9,11},{10,... | collective-permute-start | bytes 3145736 | tf_op jit(solution)/shard_map/ppermute | solution.py:455
  68.6 2.0 %collective-permute-start.16 = (bf16[256,1024]{1,0:T(8,128)(2,1)S(1)}, bf16[256,1024]{1,0:T(8,128)(2,1)S(1)}, u32[]{:S(2)}, u32[]{:S(2)}) collective-permute-start(bf16[256,1024]{1,0:T(8,128)(2,1)S(1)} %get-tuple-element.83), channel_id=1, source_target_pairs={{0,1},{1,0},{2,3},{3,2},{4,5},{5,4},{6,7},{7,6},{8,9},{9,8},{10,11... | collective-permute-start | bytes 1572872 | tf_op jit(solution)/shard_map/ppermute | solution.py:461
  68.6 2.6 %collective-permute-start.15 = (bf16[256,1024]{1,0:T(8,128)(2,1)S(1)}, bf16[256,1024]{1,0:T(8,128)(2,1)S(1)}, u32[]{:S(2)}, u32[]{:S(2)}) collective-permute-start(bf16[256,1024]{1,0:T(8,128)(2,1)S(1)} %get-tuple-element.84), channel_id=1, source_target_pairs={{0,1},{1,0},{2,3},{3,2},{4,5},{5,4},{6,7},{7,6},{8,9},{9,8},{10,11... | collective-permute-start | bytes 1572872 | tf_op jit(solution)/shard_map/ppermute | solution.py:461
